TPU v7x, 512 devices: a whole 4x4x16 slice. The times are simulated.
512 devices in a mesh: tm: 32 (over y_lo, z), tensor: 16 (over x, y_hi, core).
Axes of the slice: x: 4, y: 4 (y_hi: 2, y_lo: 2; y = y_hi * 2 + y_lo), z: 16, core: 2. Of those that a mesh axis runs over, the one named last changes fastest.
Arguments:
- patches: bfloat16 [8192, 6144], P('tm', 'tensor'), may hold values from -400 to 400
- ln_gain: float32 [6144], replicated, may hold values from 0.25 to 1.75
- w_query: bfloat16 [6144, 4096], P('tm', 'tensor'), may hold values from -0.05103104 to 0.05103104
- w_key: bfloat16 [6144, 4096], P('tm', 'tensor'), may hold values from -0.053582588 to 0.053582588
- w_value: bfloat16 [6144, 4096], P('tm', 'tensor'), may hold values from -0.078125 to 0.078125
- query_gain: float32 [4096], P('tensor'), may hold values from 0.5 to 21
- key_gain: float32 [4096], P('tensor'), may hold values from 0.5 to 1.5
- w_out: bfloat16 [4096, 6144], P('tensor', 'tm'), may hold values from -0.375 to 0.375
Outputs:
- block_out: bfloat16 [8192, 6144], P('tm', 'tensor')
All inputs are finite; a program needn't handle non-finite values.
Results may differ from a plain program's by a relative error of at most 0.019.
Values may be sent and summed in bfloat16 or wider, within the bound.
No kernel may reach another device: no remote copies, remote signals or barrier semaphores. Data moves between devices by JAX's collectives and lax.ppermute only.
A program may use at most 64 MiB of HBM per device.

v0:
```python
import jax
import jax.numpy as jnp
from jax import lax
from jax.sharding import PartitionSpec as P

HD = 128


epsilon = 1e-06


def shifted(shard, axis, by):
    size = lax.axis_size(axis)
    pairs = [(i, i + by) for i in range(size) if 0 <= i + by < size]
    return lax.ppermute(shard, axis, pairs)


def layer_norm(values, gain):
    average = jnp.mean(values, axis=-1, keepdims=True)
    centred = values - average
    spread = jnp.mean(centred * centred, axis=-1, keepdims=True)
    return centred * lax.rsqrt(spread + epsilon) * gain


def head_norm(values, gain):
    shaped = values.reshape(values.shape[0], -1, HD)
    normed = layer_norm(shaped, gain.reshape(-1, HD))
    return normed.reshape(values.shape[0], -1)


def per_device(patches, ln_gain, w_query, w_key, w_value, query_gain, key_gain, w_out):
    gathered = lax.all_gather(patches, "tensor", axis=1, tiled=True)
    normed = layer_norm(gathered.astype(jnp.float32), ln_gain).astype(jnp.bfloat16)
    row_count = normed.shape[0]
    col_count = w_query.shape[1]
    head_count = col_count // HD

    def add_rows(weight_piece):
        return jnp.dot(normed, weight_piece, preferred_element_type=jnp.float32)

    q_raw = add_rows(lax.all_gather(w_query, "tm", axis=0, tiled=True))
    k_raw = add_rows(lax.all_gather(w_key, "tm", axis=0, tiled=True))
    v_raw = add_rows(lax.all_gather(w_value, "tm", axis=0, tiled=True))
    key = head_norm(k_raw, key_gain).astype(jnp.bfloat16)
    value = v_raw.astype(jnp.bfloat16)
    found = {0: (key, value)}
    for offset in (2, 1, -1, -2):
        found[-offset] = shifted((key, value), "tm", offset)
    ordered = [found[place] for place in (-2, -1, 0, 1, 2)]
    keys_all = jnp.concatenate([pair[0] for pair in ordered], axis=0)
    values_all = jnp.concatenate([pair[1] for pair in ordered], axis=0)
    keys_all, values_all = (keys_all, values_all)
    query = (head_norm(q_raw, query_gain) * HD ** (-0.5)).astype(jnp.bfloat16)
    frame_index = lax.axis_index("tm")
    seen = frame_index + jnp.arange(5 * row_count, dtype=jnp.int32) // row_count - 2
    in_clip = (seen >= 0) & (seen < lax.axis_size("tm"))
    key_heads = keys_all.reshape(5 * row_count, head_count, HD)
    value_heads = values_all.reshape(5 * row_count, head_count, HD)
    block_rows = min(row_count, 512)
    query_blocks = query.reshape(row_count // block_rows, block_rows, head_count, HD)

    def attend(query_heads):
        scores = jnp.einsum(
            "phd,khd->hpk", query_heads, key_heads, preferred_element_type=jnp.float32
        )
        scores = jnp.where(in_clip[None, None, :], scores, -jnp.inf)
        top = jnp.max(scores, axis=-1, keepdims=True)
        expd = jnp.exp(scores - top)
        row_totals = jnp.sum(expd, axis=-1)
        probs = expd.astype(jnp.bfloat16)
        mixed = jnp.einsum("hpk,khd->phd", probs, value_heads, preferred_element_type=jnp.float32)
        return (mixed / jnp.transpose(row_totals)[:, :, None]).astype(jnp.bfloat16)

    attended = lax.map(attend, query_blocks).reshape(row_count, col_count)
    partials = jnp.dot(
        attended,
        lax.all_gather(w_out, "tm", axis=1, tiled=True),
        preferred_element_type=jnp.float32,
    ).astype(jnp.bfloat16)
    partials = lax.optimization_barrier(partials)
    summed = lax.psum_scatter(
        partials.astype(jnp.float32).astype(jnp.bfloat16), "tensor", scatter_dimension=1, tiled=True
    )
    return summed


def solution(mesh):
    return jax.shard_map(
        per_device,
        mesh=mesh,
        in_specs=(
            P("tm", "tensor"),
            P(),
            P("tm", "tensor"),
            P("tm", "tensor"),
            P("tm", "tensor"),
            P("tensor"),
            P("tensor"),
            P("tensor", "tm"),
        ),
        out_specs=P("tm", "tensor"),
        check_vma=False,
    )
```

profile of v0, /device:TPU:1, one launch (start us, length us, event | category | flops | bytes accessed | tf_op | source)
XLA Modules:
  0.0 721.0 jit_solution(13392567914748548369)
XLA Ops:
  10.0 75.8 %all-gather.6.cloned.1.call-done = bf16[256,6144]{1,0:T(8,128)(2,1)} async-done(((bf16[256,384]{1,0:T(8,128)(2,1)}), bf16[256,6144]{1,0:T(8,128)(2,1)}) %all-gather.6.cloned.1.call-update) | async-done | bytes 3145744 | tf_op jit(solution)/shard_map/all_gather | solution.py:32
  85.8 2.5 convert_reduce_fusion
  88.6 1.0 fusion.2
  89.6 1.4 fusion.4
  91.0 110.5 %all-gather.8.cloned.1.call-done = bf16[6144,256]{1,0:T(8,128)(2,1)} async-done(((bf16[192,256]{1,0:T(8,128)(2,1)}), bf16[6144,256]{1,0:T(8,128)(2,1)}) %all-gather.8.cloned.1.call-update) | async-done | bytes 3145744 | tf_op jit(solution)/shard_map/all_gather | solution.py:43
  201.5 2.9 convolution_convert_fusion.1
  204.4 3.4 collective-permute-start
  207.8 2.6 collective-permute-start.1
  210.4 1.3 collective-permute-start.2
  211.7 1.3 collective-permute-start.3
  213.0 122.0 %all-gather.10.cloned.1.call-done = bf16[6144,256]{1,0:T(8,128)(2,1)} async-done(((bf16[192,256]{1,0:T(8,128)(2,1)}), bf16[6144,256]{1,0:T(8,128)(2,1)}) %all-gather.10.cloned.1.call-update) | async-done | bytes 3145744 | tf_op jit(solution)/shard_map/all_gather | solution.py:41
  335.0 3.2 bitcast_reduce_fusion.1
  338.3 126.3 %all-gather.12.cloned.1.call-done = bf16[6144,256]{1,0:T(8,128)(2,1)} async-done(((bf16[192,256]{1,0:T(8,128)(2,1)}), bf16[6144,256]{1,0:T(8,128)(2,1)}) %all-gather.12.cloned.1.call-update) | async-done | bytes 3145744 | tf_op jit(solution)/shard_map/all_gather | solution.py:42
  464.6 3.2 bitcast_reduce_fusion
  468.0 2.7 collective-permute-start.4
  470.9 2.0 collective-permute-start.5
  473.8 1.3 collective-permute-start.6
  476.1 1.3 collective-permute-start.7
  480.3 4.4 collective-permute-done.7
  486.6 109.2 %all-gather.14.cloned.1.call-done = bf16[256,6144]{0,1:T(8,128)(2,1)} async-done(((bf16[256,192]{0,1:T(8,128)(2,1)}), bf16[256,6144]{0,1:T(8,128)(2,1)}) %all-gather.14.cloned.1.call-update) | async-done | bytes 3145744 | tf_op jit(solution)/shard_map/all_gather | solution.py:77
  595.8 2.9 convolution_convert_fusion
  598.8 2.8 copy.18
  601.6 110.8 %reduce-scatter.4.cloned.1.call-done = bf16[384,256]{1,0:T(8,128)(2,1)} async-done(((bf16[6144,256]{1,0:T(8,128)(2,1)}), bf16[384,256]{1,0:T(8,128)(2,1)}) %reduce-scatter.4.cloned.1.call-update) | async-done | bytes 196624
  712.4 1.7 copy.19
  (52 shorter events, 10.6 us)
Async XLA Ops:
  6.5 79.3 %all-gather.6.cloned.1.call-start = ((), (), s32[]{:S(2)}) async-start(), calls=%async_computation.1 | async-start | bytes 3342336 | tf_op jit(solution)/shard_map/all_gather | solution.py:32
  7.3 194.3 %all-gather.8.cloned.1.call-start = ((), (), s32[]{:S(2)}) async-start(), calls=%async_computation.2 | async-start | bytes 3244032 | tf_op jit(solution)/shard_map/all_gather | solution.py:43
  8.0 327.0 %all-gather.10.cloned.1.call-start = ((), (), s32[]{:S(2)}) async-start(), calls=%async_computation.3 | async-start | bytes 3244032 | tf_op jit(solution)/shard_map/all_gather | solution.py:41
  8.7 455.8 %all-gather.12.cloned.1.call-start = ((), (), s32[]{:S(2)}) async-start(), calls=%async_computation.4 | async-start | bytes 3244032 | tf_op jit(solution)/shard_map/all_gather | solution.py:42
  9.3 586.5 %all-gather.14.cloned.1.call-start = ((), (), s32[]{:S(2)}) async-start(), calls=%async_computation.5 | async-start | bytes 3244032 | tf_op jit(solution)/shard_map/all_gather | solution.py:77
  9.9 702.5 %reduce-scatter.4.cloned.1.call-start = ((), (), s32[]{:S(2)}) async-start(), calls=%async_computation.6 | async-start | bytes 3342336
  85.8 2.8 copy-start
  85.8 3.8 copy-start.1
  204.4 266.5 %collective-permute-start = (bf16[256,256]{1,0:T(8,128)(2,1)S(1)}, bf16[256,256]{1,0:T(8,128)(2,1)}, u32[]{:S(2)}, u32[]{:S(2)}) collective-permute-start(bf16[256,256]{1,0:T(8,128)(2,1)S(1)} %convolution_convert_fusion.1), channel_id=1, source_target_pairs={{0,32},{16,48},{32,64},{48,80},{64,96},{80,112},{96,128},{112,144}... | collective-permute-start | bytes 393224 | tf_op jit(solution)/shard_map/ppermute | solution.py:15
  207.8 266.0 %collective-permute-start.1 = (bf16[256,256]{1,0:T(8,128)(2,1)S(1)}, bf16[256,256]{1,0:T(8,128)(2,1)}, u32[]{:S(2)}, u32[]{:S(2)}) collective-permute-start(bf16[256,256]{1,0:T(8,128)(2,1)S(1)} %convolution_convert_fusion.1), channel_id=1, source_target_pairs={{0,16},{16,32},{32,48},{48,64},{64,80},{80,96},{96,112},{112,128},... | collective-permute-start | bytes 393224 | tf_op jit(solution)/shard_map/ppermute | solution.py:15
  210.4 267.0 %collective-permute-start.2 = (bf16[256,256]{1,0:T(8,128)(2,1)S(1)}, bf16[256,256]{1,0:T(8,128)(2,1)}, u32[]{:S(2)}, u32[]{:S(2)}) collective-permute-start(bf16[256,256]{1,0:T(8,128)(2,1)S(1)} %convolution_convert_fusion.1), channel_id=1, source_target_pairs={{16,0},{32,16},{48,32},{64,48},{80,64},{96,80},{112,96},{128,112},... | collective-permute-start | bytes 393224 | tf_op jit(solution)/shard_map/ppermute | solution.py:15
  211.7 266.7 %collective-permute-start.3 = (bf16[256,256]{1,0:T(8,128)(2,1)S(1)}, bf16[256,256]{1,0:T(8,128)(2,1)}, u32[]{:S(2)}, u32[]{:S(2)}) collective-permute-start(bf16[256,256]{1,0:T(8,128)(2,1)S(1)} %convolution_convert_fusion.1), channel_id=1, source_target_pairs={{32,0},{48,16},{64,32},{80,48},{96,64},{112,80},{128,96},{144,112}... | collective-permute-start | bytes 393224 | tf_op jit(solution)/shard_map/ppermute | solution.py:15
  338.3 129.6 %copy-start.2 = (f32[256]{0:T(256)S(1)}, f32[256]{0:T(256)}, u32[]{:S(2)}) copy-start(f32[256]{0:T(256)} %param.14) | copy-start | bytes 3076
  464.6 6.2 copy-start.3
  468.0 8.0 %collective-permute-start.4 = (bf16[256,256]{0,1:T(8,128)(2,1)S(1)}, bf16[256,256]{0,1:T(8,128)(2,1)S(1)}, u32[]{:S(2)}, u32[]{:S(2)}) collective-permute-start(bf16[256,256]{0,1:T(8,128)(2,1)S(1)} %fusion.20), channel_id=1, source_target_pairs={{0,32},{16,48},{32,64},{48,80},{64,96},{80,112},{96,128},{112,144}... | collective-permute-start | bytes 393224 | tf_op jit(solution)/shard_map/ppermute | solution.py:15
  470.9 6.5 collective-permute-start.5
  473.8 6.5 collective-permute-start.6
  476.1 8.6 %collective-permute-start.7 = (bf16[256,256]{0,1:T(8,128)(2,1)S(1)}, bf16[256,256]{0,1:T(8,128)(2,1)S(1)}, u32[]{:S(2)}, u32[]{:S(2)}) collective-permute-start(bf16[256,256]{0,1:T(8,128)(2,1)S(1)} %fusion.20), channel_id=1, source_target_pairs={{32,0},{48,16},{64,32},{80,48},{96,64},{112,80},{128,96},{144,112}... | collective-permute-start | bytes 393224 | tf_op jit(solution)/shard_map/ppermute | solution.py:15
Sparse Core Ops, SparseCore 0:
  10.5 75.2 all-gather.5
  87.9 113.6 all-gather.7
  203.6 131.3 all-gather.9
  336.9 127.5 all-gather.11
  466.5 129.2 all-gather.13
  601.7 110.6 reduce-scatter.3
where the time goes:
time: 722 us; the launch traced here: 721 us
  waiting for transfers between devices  663 us (92%)
  starting transfers between devices  16 us (2%)
  between operations  13.8 us (2%)
  matrix products  13.6 us (2%)
  local copies, waits for them, and re-layouts  8.79 us (1%)
    all_gather x1, waiting for transfers between devices, per_device(): k_raw = add_rows(lax.all_gather(w_key, 'tm', axis=0, tiled=True))  126 us
    all_gather x1, waiting for transfers between devices, per_device(): q_raw = add_rows(lax.all_gather(w_query, 'tm', axis=0, tiled=True))  122 us
    unnamed x7, waiting for transfers between devices  114 us
    all_gather x1, waiting for transfers between devices, per_device(): v_raw = add_rows(lax.all_gather(w_value, 'tm', axis=0, tiled=True))  110 us
    all_gather x1, waiting for transfers between devices, per_device(): lax.all_gather(w_out, 'tm', axis=1, tiled=True)  109 us
    all_gather x1, waiting for transfers between devices, per_device(): gathered = lax.all_gather(patches, 'tensor', axis=1, tiled=True)  75.8 us
    ppermute x8, starting transfers between devices, shifted(): return lax.ppermute(shard, axis, pairs)  15.8 us
  transfers between devices with their start and end apart: 14, of which 8 were waited for; matrix products, arithmetic and copies ran while one was open for 3% of the time, Pallas kernels for 0%

commit v1 on v0

v1 whole, which is shorter than its diff:
```python
import functools

import jax
import jax.numpy as jnp
from jax import lax
from jax.experimental import pallas as pl
from jax.experimental.pallas import tpu as pltpu
from jax.sharding import Mesh
from jax.sharding import PartitionSpec as P

HD = 128
EPS = 1e-06
AXES = ("ylo", "z", "x", "yh", "core")
SIZES = (2, 16, 4, 2, 2)
ROWS = 192
WIDTH = 6144
WINDOW = 9 * 384
BF = jnp.bfloat16
F32 = jnp.float32


def _places():
    for ylo in range(2):
        for z in range(16):
            for x in range(4):
                for yh in range(2):
                    for core in range(2):
                        yield ylo, z, x, yh, core


def _number(ylo, z, x, yh, core):
    return (((ylo * 16 + z) * 4 + x) * 2 + yh) * 2 + core


def send(value, target):
    pairs = [(_number(*p), _number(*target(*p))) for p in _places() if target(*p) is not None]
    return lax.ppermute(value, AXES, pairs)


def along_z(by):
    return lambda ylo, z, x, yh, core: (ylo, (z + by) % 16, x, yh, core)


def other_core(ylo, z, x, yh, core):
    return ylo, z, x, yh, 1 - core


def cross(ylo, z, x, yh, core):
    return (ylo, z, x, yh, 1 - core) if core == ylo else (core, z, x, yh, core)


def from_home(ylo, z, x, yh, core):
    return (ylo, z, x, yh, 1 - core) if core == ylo else None


def onward(ylo, z, x, yh, core):
    return ylo, (z + 1 - 2 * core) % 16, x, yh, core


def out_weight(ylo, z, x, yh, core):
    return core, x * 4 + ((z // 4) % 2) * 2 + z % 2, ylo * 2 + z // 8, yh, (z // 2) % 2


def norm_kernel(place_ref, acts_ref, gain_ref, out_ref):
    ylo, z, core = place_ref[0], place_ref[1], place_ref[4]
    total = jnp.zeros((acts_ref.shape[2], 1), F32)
    for t in range(16):
        total += jnp.sum(acts_ref[0, t].astype(F32), axis=-1, keepdims=True)
    mean = total / WIDTH
    spread = jnp.zeros_like(total)
    for t in range(16):
        centred = acts_ref[0, t].astype(F32) - mean
        spread += jnp.sum(centred * centred, axis=-1, keepdims=True)
    scale = lax.rsqrt(spread / WIDTH + EPS)
    large = lax.rem(z + 8 * (1 - core), 16) // 2
    small = lax.rem(z + 1 + 8 * (1 - core), 16) // 2
    for i in range(9):
        if i < 5:
            t = (ylo ^ core) * 8 + lax.rem(large + i, 8)
        else:
            t = (ylo ^ (1 - core)) * 8 + lax.rem(small + i - 5, 8)
        centred = acts_ref[0, t].astype(F32) - mean
        gain = gain_ref[pl.ds(t, 1), :]
        out_ref[:, i * 384 : (i + 1) * 384] = (centred * scale * gain).astype(BF)


def normalise(place, acts, gain):
    rows = 64
    return pl.pallas_call(
        norm_kernel,
        grid=(2, 256 // rows),
        out_shape=jax.ShapeDtypeStruct((512, WINDOW), BF),
        in_specs=[
            pl.BlockSpec(memory_space=pltpu.SMEM),
            pl.BlockSpec((1, 16, rows, 384), lambda s, r: (s, 0, r, 0)),
            pl.BlockSpec((16, 384), lambda s, r: (0, 0)),
        ],
        out_specs=pl.BlockSpec((rows, WINDOW), lambda s, r: (s * (256 // rows) + r, 0)),
        compiler_params=pltpu.CompilerParams(vmem_limit_bytes=32 << 20),
        cost_estimate=pl.CostEstimate(flops=30_000_000, bytes_accessed=10_000_000, transcendentals=0),
    )(place, acts.reshape(2, 16, 256, 384), gain.reshape(16, 384))


def head_norm(raw, gain):
    mean = jnp.mean(raw, axis=-1, keepdims=True)
    centred = raw - mean
    spread = jnp.mean(centred * centred, axis=-1, keepdims=True)
    return centred * lax.rsqrt(spread + EPS) * gain


def product_kernel(place_ref, normed_ref, *refs):
    first, second, own, last = refs[:7], refs[7:14], refs[14], refs[15]
    mine_ref, theirs_ref, weights, sem = refs[16:]
    core = place_ref[4]

    @pl.when(pl.program_id(0) == 0)
    def _():
        odd = lax.rem(place_ref[1], 2)
        up = core == 0
        blocks = [(own, odd + jnp.where(up, 8, 0)), (last, odd + jnp.where(up, 0, 8))]
        for i in range(7):
            n = i + 1
            blocks.append((first[i], jnp.where(up, odd + 8 - n, 11 - odd + n - 1)))
            blocks.append((second[i], jnp.where(up, 11 - odd + 7 - n, odd + n)))
        copies = []
        for ref, block in blocks:
            rows = pl.ds(pl.multiple_of(block * ROWS, ROWS), ROWS)
            for m in range(3):
                copies.append(pltpu.make_async_copy(ref.at[m], weights.at[rows, pl.ds(m * 256, 256)], sem.at[len(copies)]))
        for copy in copies:
            copy.start()
        for block in (9 * (1 - odd), 10 + 7 * odd):
            weights[pl.ds(pl.multiple_of(block * ROWS, ROWS), ROWS), :] = jnp.zeros((ROWS, 768), BF)
        for copy in copies:
            copy.wait()

    raw = jnp.dot(normed_ref[...], weights[...], preferred_element_type=F32)
    for m in range(3):
        one, two = raw[:, m * 256 : m * 256 + HD], raw[:, m * 256 + HD : (m + 1) * 256]
        mine_ref[:, m * HD : (m + 1) * HD] = jnp.where(core == 0, one, two)
        theirs_ref[:, m * HD : (m + 1) * HD] = jnp.where(core == 0, two, one)


def multiply(place, normed, shards):
    rows = 128
    return pl.pallas_call(
        product_kernel,
        grid=(512 // rows,),
        out_shape=[jax.ShapeDtypeStruct((512, 3 * HD), F32)] * 2,
        in_specs=[pl.BlockSpec(memory_space=pltpu.SMEM), pl.BlockSpec((rows, WINDOW), lambda r: (r, 0))]
        + [pl.BlockSpec(memory_space=pl.ANY)] * 16,
        out_specs=[pl.BlockSpec((rows, 3 * HD), lambda r: (r, 0))] * 2,
        scratch_shapes=[pltpu.VMEM((WINDOW, 768), BF), pltpu.SemaphoreType.DMA((48,))],
        compiler_params=pltpu.CompilerParams(vmem_limit_bytes=32 << 20),
        cost_estimate=pl.CostEstimate(flops=2 * 512 * WINDOW * 768, bytes_accessed=10_000_000, transcendentals=0),
    )(place, normed, *shards)


def heads_kernel(mine_ref, theirs_ref, gains_ref, q_ref, kv_ref):
    raw = mine_ref[...] + theirs_ref[...]
    query = head_norm(raw[:, :HD], gains_ref[0:1, :]) * HD ** (-0.5)
    q_ref[...] = query.astype(BF)
    kv_ref[0] = head_norm(raw[:, HD : 2 * HD], gains_ref[1:2, :]).astype(BF)
    kv_ref[1] = raw[:, 2 * HD :].astype(BF)


def split_heads(mine, theirs, gains):
    return pl.pallas_call(
        heads_kernel,
        out_shape=(jax.ShapeDtypeStruct((512, HD), BF), jax.ShapeDtypeStruct((2, 512, HD), BF)),
        in_specs=[pl.BlockSpec(memory_space=pltpu.VMEM)] * 3,
        out_specs=(pl.BlockSpec(memory_space=pltpu.VMEM), pl.BlockSpec(memory_space=pltpu.VMEM)),
        compiler_params=pltpu.CompilerParams(vmem_limit_bytes=32 << 20),
        cost_estimate=pl.CostEstimate(flops=4_000_000, bytes_accessed=2_000_000, transcendentals=0),
    )(mine, theirs, gains)


def attend_kernel(place_ref, q_ref, *refs):
    kvs, out_ref = refs[:5], refs[5]
    z = place_ref[1]
    for slot in range(2):
        query = q_ref[slot * 256 : (slot + 1) * 256, :]
        scores = []
        starts = []
        for offset, ref in zip((-2, -1, 0, 1, 2), kvs, strict=True):
            wrap = jnp.where(z + offset < 0, -1, jnp.where(z + offset >= 16, 1, 0))
            held = slot + wrap
            valid = (held >= 0) & (held < 2)
            start = pl.multiple_of(jnp.clip(held, 0, 1) * 256, 256)
            starts.append(start)
            key = ref[0, pl.ds(start, 256), :]
            part = lax.dot_general(query, key, (((1,), (1,)), ((), ())), preferred_element_type=F32)
            scores.append(part + jnp.where(valid, 0.0, -jnp.inf))
        top = scores[0]
        for part in scores[1:]:
            top = jnp.maximum(top, part)
        top = jnp.max(top, axis=-1, keepdims=True)
        total = jnp.zeros((256, 1), F32)
        mixed = jnp.zeros((256, HD), F32)
        for part, start, ref in zip(scores, starts, kvs, strict=True):
            expd = jnp.exp(part - top)
            total += jnp.sum(expd, axis=-1, keepdims=True)
            value = ref[1, pl.ds(start, 256), :]
            mixed += jnp.dot(expd.astype(BF), value, preferred_element_type=F32)
        result = (mixed / total).astype(BF)
        for copy in range(8):
            out_ref[copy, slot * 256 : (slot + 1) * 256, :] = result


def attend(place, query, kvs):
    return pl.pallas_call(
        attend_kernel,
        out_shape=jax.ShapeDtypeStruct((8, 512, HD), BF),
        in_specs=[pl.BlockSpec(memory_space=pltpu.SMEM)] + [pl.BlockSpec(memory_space=pltpu.VMEM)] * 6,
        out_specs=pl.BlockSpec(memory_space=pltpu.VMEM),
        compiler_params=pltpu.CompilerParams(vmem_limit_bytes=32 << 20),
        cost_estimate=pl.CostEstimate(flops=4 * 512 * 1280 * HD, bytes_accessed=1_600_000, transcendentals=512 * 1280),
    )(place, query, *kvs)


def out_kernel(heads_ref, weights_ref, out_ref):
    for slot in range(2):
        part = jnp.zeros((256, 768), F32)
        for x in range(4):
            rows = slice(slot * 256, (slot + 1) * 256)
            pair = jnp.concatenate([heads_ref[2 * x, rows, :], heads_ref[2 * x + 1, rows, :]], axis=1)
            part += lax.dot_general(pair, weights_ref[x], (((1,), (1,)), ((), ())), preferred_element_type=F32)
        out_ref[slot] = part[:, :384].astype(BF)
        out_ref[2 + slot] = part[:, 384:].astype(BF)


def project_out(heads, weights):
    return pl.pallas_call(
        out_kernel,
        out_shape=jax.ShapeDtypeStruct((4, 256, 384), BF),
        in_specs=[pl.BlockSpec(memory_space=pltpu.VMEM)] * 2,
        out_specs=pl.BlockSpec(memory_space=pltpu.VMEM),
        compiler_params=pltpu.CompilerParams(vmem_limit_bytes=32 << 20),
        cost_estimate=pl.CostEstimate(flops=2 * 512 * 768 * 1024, bytes_accessed=3_500_000, transcendentals=0),
    )(heads, weights)


def per_device(patches, ln_gain, w_query, w_key, w_value, query_gain, key_gain, w_out):
    place = jnp.stack([lax.axis_index(a) for a in AXES]).astype(jnp.int32)
    ylo, core = place[0], place[4]
    home = core == ylo
    acts = lax.all_gather(patches, ("ylo", "x", "yh", "core"), axis=0, tiled=False)

    held = jnp.stack([w_query, w_key, w_value])
    got = send(held, cross)
    one = jnp.where(home, held, got)
    two = jnp.where(home, got, send(got, from_home))
    shards = [[], []]
    ends = [one, two]
    for step in range(7):
        for chain in range(2):
            ends[chain] = send(ends[chain], onward)
            shards[chain].append(ends[chain])
    last = send(jnp.where(core == 0, ends[0], ends[1]), onward)
    own = jnp.where(core == 0, one, two)

    turned = send(w_out.T, out_weight)
    out_weights = lax.all_gather(turned, "z", axis=0, tiled=False).reshape(4, 768, 256)

    normed = normalise(place, acts, ln_gain)
    mine, theirs = multiply(place, normed, shards[0] + shards[1] + [own, last])
    gains = jnp.stack([query_gain, key_gain])
    gains = jnp.where(home, gains, send(gains, other_core)).reshape(2, 2, HD)
    gains = jnp.where(core == 0, gains[:, 0], gains[:, 1])
    query, kv = split_heads(mine, send(theirs, other_core), gains)
    near = {offset: send(kv, along_z(-offset)) for offset in (-2, 2, -1, 1)}
    near[0] = kv
    attended = attend(place, query, [near[o] for o in (-2, -1, 0, 1, 2)])
    heads = lax.all_to_all(attended, ("x", "core"), 0, 0, tiled=True)
    parts = project_out(heads, out_weights)
    parts = lax.all_to_all(parts, ("yh", "ylo"), 0, 0, tiled=True)
    return jnp.sum(parts.astype(F32), axis=0).astype(BF)


def solution(mesh):
    fine = Mesh(mesh.devices.reshape(SIZES), AXES)
    tm, tensor = ("ylo", "z"), ("x", "yh", "core")
    return jax.shard_map(
        per_device,
        mesh=fine,
        in_specs=(
            P(tm, tensor),
            P(),
            P(tm, tensor),
            P(tm, tensor),
            P(tm, tensor),
            P(tensor),
            P(tensor),
            P(tensor, tm),
        ),
        out_specs=P(tm, tensor),
        check_vma=False,
    )
```

time: 722 us -> 225 us (0.31)
  waiting for transfers between devices: 663 us -> 52.4 us
  starting transfers between devices: 16 us -> 115 us
  Pallas kernels: 0 us -> 17 us
  blocking collectives: 0 us -> 15.2 us
  matrix products: 13.6 us -> 0 us
    all_gather x5 -> x2, waiting for transfers between devices: 544 us -> 0.01 us  [the longest x1 0.01 us: per_device(): lax.all_gather(turned, 'z', axis=0, tiled=False).reshape(4, 768, 256)]
    unnamed x7 -> x2, waiting for transfers between devices: 114 us -> 0.73 us
    ppermute x8 -> x24, starting transfers between devices: 15.8 us -> 103 us  [send(): return lax.ppermute(value, AXES, pairs)]
    ppermute x8 -> x24, waiting for transfers between devices: 5.18 us -> 36.6 us  [send(): return lax.ppermute(value, AXES, pairs)]
    pallas_call x0 -> x5, Pallas kernels: none -> 17 us  [the longest x1 6.4 us: normalise(): pl.pallas_call(norm_kernel, grid=(2, 256 // rows), out_shape=jax.ShapeDty...]
    all_to_all x0 -> x1, blocking collectives: none -> 15.2 us  [per_device(): parts = lax.all_to_all(parts, ('yh', 'ylo'), 0, 0, tiled=True)]
    all_to_all x0 -> x1, waiting for transfers between devices: none -> 15.1 us  [per_device(): heads = lax.all_to_all(attended, ('x', 'core'), 0, 0, tiled=True)]
    dot_general x6 -> x0, matrix products: 13.6 us -> none  [the longest x3 9.34 us: add_rows(): return jnp.dot(normed, weight_piece, preferred_element_type=jnp.float32)]
  transfers between devices with their start and end apart: 14 -> 27, of which waited for: 8 -> 13; matrix products, arithmetic and copies ran while one was open for 3% -> 1% of each run, Pallas kernels for 0% -> 7%
where the time goes in v1:
time: 225 us; the launch traced here: 224 us
  starting transfers between devices  115 us (51%)
  waiting for transfers between devices  52.4 us (23%)
  Pallas kernels  17 us (8%)
  blocking collectives  15.2 us (7%)
  between operations  13.8 us (6%)
  local copies, waits for them, and re-layouts  6.38 us (3%)
  other arithmetic  3.68 us (2%)
    ppermute x24, starting transfers between devices, send(): return lax.ppermute(value, AXES, pairs)  103 us
    ppermute x24, waiting for transfers between devices, send(): return lax.ppermute(value, AXES, pairs)  36.6 us
    all_to_all x1, blocking collectives, per_device(): parts = lax.all_to_all(parts, ('yh', 'ylo'), 0, 0, tiled=True)  15.2 us
    all_to_all x1, waiting for transfers between devices, per_device(): heads = lax.all_to_all(attended, ('x', 'core'), 0, 0, tiled=True)  15.1 us
    all_to_all x1, starting transfers between devices, per_device(): heads = lax.all_to_all(attended, ('x', 'core'), 0, 0, tiled=True)  12.6 us
    pallas_call x1, Pallas kernels, normalise(): pl.pallas_call(norm_kernel, grid=(2, 256 // rows), out_shape=jax.ShapeDty...  6.4 us
    pallas_call x1, Pallas kernels, multiply(): pl.pallas_call(product_kernel, grid=(512 // rows,), out_shape=[jax.ShapeD...  6.34 us
    unnamed x20, local copies, waits for them, and re-layouts  6.29 us
  transfers between devices with their start and end apart: 27, of which 13 were waited for; matrix products, arithmetic and copies ran while one was open for 1% of the time, Pallas kernels for 7%

profile of v1, /device:TPU:1, one launch (start us, length us, event | category | flops | bytes accessed | tf_op | source)
XLA Modules:
  0.0 223.8 jit_solution(4266345386484508476)
XLA Ops:
  8.3 4.0 %collective-permute-start = (bf16[3,192,256]{2,1,0:T(8,128)(2,1)S(1)}, bf16[3,192,256]{2,1,0:T(8,128)(2,1)S(1)}, u32[]{:S(2)}, u32[]{:S(2)}) collective-permute-start(bf16[3,192,256]{2,1,0:T(8,128)(2,1)S(1)} %pad_maximum_fusion), channel_id=1, source_target_pairs={{0,1},{1,257},{2,3},{3,259},{4,5},{5,261},{6,7},{7,263},{8,9},{9,2... | collective-permute-start | bytes 884744 | tf_op jit(solution)/shard_map/ppermute | solution.py:37
  12.4 5.8 %collective-permute-done = bf16[3,192,256]{2,1,0:T(8,128)(2,1)S(1)} collective-permute-done((bf16[3,192,256]{2,1,0:T(8,128)(2,1)S(1)}, bf16[3,192,256]{2,1,0:T(8,128)(2,1)S(1)}, u32[]{:S(2)}, u32[]{:S(2)}) %collective-permute-start) | collective-permute-done | bytes 294944 | tf_op jit(solution)/shard_map/ppermute | solution.py:37
  19.5 6.7 %collective-permute-done.8 = bf16[3,192,256]{2,1,0:T(8,128)(2,1)S(1)} collective-permute-done((bf16[3,192,256]{2,1,0:T(8,128)(2,1)S(1)}, bf16[3,192,256]{2,1,0:T(8,128)(2,1)S(1)}, u32[]{:S(2)}, u32[]{:S(2)}) %collective-permute-start.8) | collective-permute-done | bytes 294944 | tf_op jit(solution)/shard_map/ppermute | solution.py:37
  27.2 5.7 %collective-permute-start.1 = (bf16[3,192,256]{2,1,0:T(8,128)(2,1)S(1)}, bf16[3,192,256]{2,1,0:T(8,128)(2,1)S(1)}, u32[]{:S(2)}, u32[]{:S(2)}) collective-permute-start(bf16[3,192,256]{2,1,0:T(8,128)(2,1)S(1)} %get-tuple-element.15), channel_id=1, source_target_pairs={{0,16},{1,241},{2,18},{3,243},{4,20},{5,245},{6,22},{7,247},{8,24}... | collective-permute-start | bytes 884744 | tf_op jit(solution)/shard_map/ppermute | solution.py:37
  36.6 5.0 %collective-permute-start.2 = (bf16[3,192,256]{2,1,0:T(8,128)(2,1)S(1)}, bf16[3,192,256]{2,1,0:T(8,128)(2,1)S(1)}, u32[]{:S(2)}, u32[]{:S(2)}) collective-permute-start(bf16[3,192,256]{2,1,0:T(8,128)(2,1)S(1)} %collective-permute-done.1.refs_0_), channel_id=1, source_target_pairs={{0,16},{1,241},{2,18},{3,243},{4,20},{5,245},{6,22},{7,247},{8,24}... | collective-permute-start | bytes 884744 | tf_op jit(solution)/shard_map/ppermute | solution.py:37
  41.7 3.1 %collective-permute-start.10 = (bf16[3,192,256]{2,1,0:T(8,128)(2,1)S(1)}, bf16[3,192,256]{2,1,0:T(8,128)(2,1)S(1)}, u32[]{:S(2)}, u32[]{:S(2)}) collective-permute-start(bf16[3,192,256]{2,1,0:T(8,128)(2,1)S(1)} %collective-permute-done.9.refs_7_), channel_id=1, source_target_pairs={{0,16},{1,241},{2,18},{3,243},{4,20},{5,245},{6,22},{7,247},{8,24}... | collective-permute-start | bytes 884744 | tf_op jit(solution)/shard_map/ppermute | solution.py:37
  45.3 5.0 %collective-permute-start.3 = (bf16[3,192,256]{2,1,0:T(8,128)(2,1)S(1)}, bf16[3,192,256]{2,1,0:T(8,128)(2,1)S(1)}, u32[]{:S(2)}, u32[]{:S(2)}) collective-permute-start(bf16[3,192,256]{2,1,0:T(8,128)(2,1)S(1)} %collective-permute-done.2.refs_1_), channel_id=1, source_target_pairs={{0,16},{1,241},{2,18},{3,243},{4,20},{5,245},{6,22},{7,247},{8,24}... | collective-permute-start | bytes 884744 | tf_op jit(solution)/shard_map/ppermute | solution.py:37
  54.0 5.0 %collective-permute-start.4 = (bf16[3,192,256]{2,1,0:T(8,128)(2,1)S(1)}, bf16[3,192,256]{2,1,0:T(8,128)(2,1)S(1)}, u32[]{:S(2)}, u32[]{:S(2)}) collective-permute-start(bf16[3,192,256]{2,1,0:T(8,128)(2,1)S(1)} %collective-permute-done.3.refs_2_), channel_id=1, source_target_pairs={{0,16},{1,241},{2,18},{3,243},{4,20},{5,245},{6,22},{7,247},{8,24}... | collective-permute-start | bytes 884744 | tf_op jit(solution)/shard_map/ppermute | solution.py:37
  59.0 3.1 %collective-permute-start.12 = (bf16[3,192,256]{2,1,0:T(8,128)(2,1)S(1)}, bf16[3,192,256]{2,1,0:T(8,128)(2,1)S(1)}, u32[]{:S(2)}, u32[]{:S(2)}) collective-permute-start(bf16[3,192,256]{2,1,0:T(8,128)(2,1)S(1)} %collective-permute-done.11.refs_9_), channel_id=1, source_target_pairs={{0,16},{1,241},{2,18},{3,243},{4,20},{5,245},{6,22},{7,247},{8,24}... | collective-permute-start | bytes 884744 | tf_op jit(solution)/shard_map/ppermute | solution.py:37
  62.6 5.0 %collective-permute-start.5 = (bf16[3,192,256]{2,1,0:T(8,128)(2,1)S(1)}, bf16[3,192,256]{2,1,0:T(8,128)(2,1)S(1)}, u32[]{:S(2)}, u32[]{:S(2)}) collective-permute-start(bf16[3,192,256]{2,1,0:T(8,128)(2,1)S(1)} %collective-permute-done.4.refs_3_), channel_id=1, source_target_pairs={{0,16},{1,241},{2,18},{3,243},{4,20},{5,245},{6,22},{7,247},{8,24}... | collective-permute-start | bytes 884744 | tf_op jit(solution)/shard_map/ppermute | solution.py:37
  71.3 5.0 %collective-permute-start.6 = (bf16[3,192,256]{2,1,0:T(8,128)(2,1)S(1)}, bf16[3,192,256]{2,1,0:T(8,128)(2,1)}, u32[]{:S(2)}, u32[]{:S(2)}) collective-permute-start(bf16[3,192,256]{2,1,0:T(8,128)(2,1)S(1)} %collective-permute-done.5.refs_4_), channel_id=1, source_target_pairs={{0,16},{1,241},{2,18},{3,243},{4,20},{5,245},{6,22},{7,247},{8,24}... | collective-permute-start | bytes 884744 | tf_op jit(solution)/shard_map/ppermute | solution.py:37
  80.2 4.9 %collective-permute-start.7 = (bf16[3,192,256]{2,1,0:T(8,128)(2,1)}, bf16[3,192,256]{2,1,0:T(8,128)(2,1)S(1)}, u32[]{:S(2)}, u32[]{:S(2)}) collective-permute-start(bf16[3,192,256]{2,1,0:T(8,128)(2,1)} %collective-permute-done.6.refs_5_), channel_id=1, source_target_pairs={{0,16},{1,241},{2,18},{3,243},{4,20},{5,245},{6,22},{7,247},{8,24}... | collective-permute-start | bytes 884744 | tf_op jit(solution)/shard_map/ppermute | solution.py:37
  88.2 6.1 %collective-permute-start.23 = (bf16[192,256]{1,0:T(8,128)(2,1)}, bf16[192,256]{1,0:T(8,128)(2,1)S(1)}, u32[]{:S(2)}, u32[]{:S(2)}) collective-permute-start(bf16[192,256]{1,0:T(8,128)(2,1)} %bitcast.29), channel_id=1, source_target_pairs={{0,0},{1,256},{2,2},{3,258},{4,64},{5,320},{6,66},{7,322},{8,128},... | collective-permute-start | bytes 294920 | tf_op jit(solution)/shard_map/ppermute | solution.py:37
  98.9 13.8 %collective-permute-start.16 = (bf16[3,192,256]{2,1,0:T(8,128)(2,1)}, bf16[3,192,256]{2,1,0:T(8,128)(2,1)}, u32[]{:S(2)}, u32[]{:S(2)}) collective-permute-start(bf16[3,192,256]{2,1,0:T(8,128)(2,1)} %broadcast_select_fusion), channel_id=1, source_target_pairs={{0,16},{1,241},{2,18},{3,243},{4,20},{5,245},{6,22},{7,247},{8,24}... | collective-permute-start | bytes 884744 | tf_op jit(solution)/shard_map/ppermute | solution.py:37
  115.6 6.4 %shard_map.82.normed_ref = bf16[512,3456]{1,0:T(8,128)(2,1)S(1)} custom-call(s32[5]{0:T(128)S(1)} %stack.44.place_ref, bf16[2,16,256,384]{3,2,1,0:T(8,128)(2,1)S(1)} %bitcast.17, f32[16,384]{1,0:T(8,128)S(1)} %reshape.15.gain_ref), custom_call_target="tpu_custom_call" | custom-call | flops 30000000 | bytes 10000000 | tf_op jit(solution)/shard_map/pallas_call | solution.py:89
  122.1 6.3 %shard_map.83 = (f32[512,384]{1,0:T(8,128)S(1)}, f32[512,384]{1,0:T(8,128)S(1)}) custom-call(s32[5]{0:T(128)S(1)} %stack.44.place_ref, bf16[512,3456]{1,0:T(8,128)(2,1)S(1)} %shard_map.82.normed_ref, bf16[3,192,256]{2,1,0:T(8,128)(2,1)S(1)} %collective-permute-done.1.refs_0_, bf16[3,192,256]{2,1,0:T(8,128)(2,1)S(1)} %collective-permute-done.2.refs_1_, ...), custom_call_target="tpu_custom_call" | custom-call | flops 2717908992 | bytes 10000000 | tf_op jit(solution)/shard_map/pallas_call | solution.py:146
  128.4 6.0 %collective-permute-start.17 = (f32[512,384]{1,0:T(8,128)S(1)}, f32[512,384]{1,0:T(8,128)S(1)}, u32[]{:S(2)}, u32[]{:S(2)}) collective-permute-start(f32[512,384]{1,0:T(8,128)S(1)} %get-tuple-element.10), channel_id=1, source_target_pairs={{0,1},{1,0},{2,3},{3,2},{4,5},{5,4},{6,7},{7,6},{8,9},{9,8},{10,11... | collective-permute-start | bytes 2359304 | tf_op jit(solution)/shard_map/ppermute | solution.py:37
  141.8 4.8 %collective-permute-start.21 = (bf16[2,512,128]{2,1,0:T(8,128)(2,1)S(1)}, bf16[2,512,128]{2,1,0:T(8,128)(2,1)S(1)}, u32[]{:S(2)}, u32[]{:S(2)}) collective-permute-start(bf16[2,512,128]{2,1,0:T(8,128)(2,1)S(1)} %get-tuple-element.12.refs_2_), channel_id=1, source_target_pairs={{0,240},{1,241},{2,242},{3,243},{4,244},{5,245},{6,246},{7,247},{8... | collective-permute-start | bytes 786440 | tf_op jit(solution)/shard_map/ppermute | solution.py:37
  146.7 4.3 %collective-permute-start.22 = (bf16[2,512,128]{2,1,0:T(8,128)(2,1)S(1)}, bf16[2,512,128]{2,1,0:T(8,128)(2,1)S(1)}, u32[]{:S(2)}, u32[]{:S(2)}) collective-permute-start(bf16[2,512,128]{2,1,0:T(8,128)(2,1)S(1)} %get-tuple-element.12.refs_2_), channel_id=1, source_target_pairs={{0,224},{1,225},{2,226},{3,227},{4,228},{5,229},{6,230},{7,231},{8... | collective-permute-start | bytes 786440 | tf_op jit(solution)/shard_map/ppermute | solution.py:37
  151.0 9.1 %collective-permute-done.19.refs_0_ = bf16[2,512,128]{2,1,0:T(8,128)(2,1)S(1)} collective-permute-done((bf16[2,512,128]{2,1,0:T(8,128)(2,1)S(1)}, bf16[2,512,128]{2,1,0:T(8,128)(2,1)S(1)}, u32[]{:S(2)}, u32[]{:S(2)}) %collective-permute-start.19) | collective-permute-done | bytes 262176 | tf_op jit(solution)/shard_map/ppermute | solution.py:37
  160.1 5.5 %collective-permute-done.20.refs_1_ = bf16[2,512,128]{2,1,0:T(8,128)(2,1)S(1)} collective-permute-done((bf16[2,512,128]{2,1,0:T(8,128)(2,1)S(1)}, bf16[2,512,128]{2,1,0:T(8,128)(2,1)S(1)}, u32[]{:S(2)}, u32[]{:S(2)}) %collective-permute-start.20) | collective-permute-done | bytes 262176 | tf_op jit(solution)/shard_map/ppermute | solution.py:37
  170.8 12.6 %all-to-all-start = ((bf16[8,512,128]{2,1,0:T(8,128)(2,1)}), bf16[8,512,128]{2,1,0:T(8,128)(2,1)S(1)}, u32[]{:S(2)}, u32[]{:S(2)}) async-start(bf16[8,512,128]{2,1,0:T(8,128)(2,1)} %shard_map.85), calls=%async_computation | async-start | bytes 2097152 | tf_op jit(solution)/shard_map/all_to_all | solution.py:274
  183.4 15.1 %all-to-all-done.heads_ref = bf16[8,512,128]{2,1,0:T(8,128)(2,1)S(1)} async-done(((bf16[8,512,128]{2,1,0:T(8,128)(2,1)}), bf16[8,512,128]{2,1,0:T(8,128)(2,1)S(1)}, u32[]{:S(2)}, u32[]{:S(2)}) %all-to-all-start) | async-done | bytes 1048608 | tf_op jit(solution)/shard_map/all_to_all | solution.py:274
  200.9 15.2 %all_to_all.10 = bf16[4,256,384]{2,1,0:T(8,128)(2,1)S(1)} all-to-all(bf16[4,256,384]{2,1,0:T(8,128)(2,1)S(1)} %shard_map.86), channel_id=1, replica_groups=mesh['ylo'=2,'z'=16,'x'=4,'yh'=2,'core'=2] {'yh','ylo'}, dimensions={0} | all-to-all | bytes 1572864 | tf_op jit(solution)/shard_map/all_to_all | solution.py:276
  (67 shorter events, 46.2 us)
Async XLA Ops:
  6.5 106.3 %all-gather.5.cloned.1.call-start = ((), (), s32[]{:S(2)}) async-start(), calls=%async_computation.2 | async-start | bytes 6488064 | tf_op jit(solution)/shard_map/all_gather | solution.py:247
  7.3 176.2 %all-gather.7.cloned.1.call-start = ((), (), s32[]{:S(2)}) async-start(), calls=%async_computation.3 | async-start | bytes 1671168 | tf_op jit(solution)/shard_map/all_gather | solution.py:263
  8.3 9.9 %collective-permute-start = (bf16[3,192,256]{2,1,0:T(8,128)(2,1)S(1)}, bf16[3,192,256]{2,1,0:T(8,128)(2,1)S(1)}, u32[]{:S(2)}, u32[]{:S(2)}) collective-permute-start(bf16[3,192,256]{2,1,0:T(8,128)(2,1)S(1)} %pad_maximum_fusion), channel_id=1, source_target_pairs={{0,1},{1,257},{2,3},{3,259},{4,5},{5,261},{6,7},{7,263},{8,9},{9,2... | collective-permute-start | bytes 884744 | tf_op jit(solution)/shard_map/ppermute | solution.py:37
  27.2 9.4 %collective-permute-start.1 = (bf16[3,192,256]{2,1,0:T(8,128)(2,1)S(1)}, bf16[3,192,256]{2,1,0:T(8,128)(2,1)S(1)}, u32[]{:S(2)}, u32[]{:S(2)}) collective-permute-start(bf16[3,192,256]{2,1,0:T(8,128)(2,1)S(1)} %get-tuple-element.15), channel_id=1, source_target_pairs={{0,16},{1,241},{2,18},{3,243},{4,20},{5,245},{6,22},{7,247},{8,24}... | collective-permute-start | bytes 884744 | tf_op jit(solution)/shard_map/ppermute | solution.py:37
  33.0 8.7 %collective-permute-start.9 = (bf16[3,192,256]{2,1,0:T(8,128)(2,1)S(1)}, bf16[3,192,256]{2,1,0:T(8,128)(2,1)S(1)}, u32[]{:S(2)}, u32[]{:S(2)}) collective-permute-start(bf16[3,192,256]{2,1,0:T(8,128)(2,1)S(1)} %get-tuple-element.14), channel_id=1, source_target_pairs={{0,16},{1,241},{2,18},{3,243},{4,20},{5,245},{6,22},{7,247},{8,24}... | collective-permute-start | bytes 884744 | tf_op jit(solution)/shard_map/ppermute | solution.py:37
  36.6 8.7 %collective-permute-start.2 = (bf16[3,192,256]{2,1,0:T(8,128)(2,1)S(1)}, bf16[3,192,256]{2,1,0:T(8,128)(2,1)S(1)}, u32[]{:S(2)}, u32[]{:S(2)}) collective-permute-start(bf16[3,192,256]{2,1,0:T(8,128)(2,1)S(1)} %collective-permute-done.1.refs_0_), channel_id=1, source_target_pairs={{0,16},{1,241},{2,18},{3,243},{4,20},{5,245},{6,22},{7,247},{8,24}... | collective-permute-start | bytes 884744 | tf_op jit(solution)/shard_map/ppermute | solution.py:37
  41.7 8.7 %collective-permute-start.10 = (bf16[3,192,256]{2,1,0:T(8,128)(2,1)S(1)}, bf16[3,192,256]{2,1,0:T(8,128)(2,1)S(1)}, u32[]{:S(2)}, u32[]{:S(2)}) collective-permute-start(bf16[3,192,256]{2,1,0:T(8,128)(2,1)S(1)} %collective-permute-done.9.refs_7_), channel_id=1, source_target_pairs={{0,16},{1,241},{2,18},{3,243},{4,20},{5,245},{6,22},{7,247},{8,24}... | collective-permute-start | bytes 884744 | tf_op jit(solution)/shard_map/ppermute | solution.py:37
  45.3 8.7 %collective-permute-start.3 = (bf16[3,192,256]{2,1,0:T(8,128)(2,1)S(1)}, bf16[3,192,256]{2,1,0:T(8,128)(2,1)S(1)}, u32[]{:S(2)}, u32[]{:S(2)}) collective-permute-start(bf16[3,192,256]{2,1,0:T(8,128)(2,1)S(1)} %collective-permute-done.2.refs_1_), channel_id=1, source_target_pairs={{0,16},{1,241},{2,18},{3,243},{4,20},{5,245},{6,22},{7,247},{8,24}... | collective-permute-start | bytes 884744 | tf_op jit(solution)/shard_map/ppermute | solution.py:37
  50.3 8.7 %collective-permute-start.11 = (bf16[3,192,256]{2,1,0:T(8,128)(2,1)S(1)}, bf16[3,192,256]{2,1,0:T(8,128)(2,1)S(1)}, u32[]{:S(2)}, u32[]{:S(2)}) collective-permute-start(bf16[3,192,256]{2,1,0:T(8,128)(2,1)S(1)} %collective-permute-done.10.refs_8_), channel_id=1, source_target_pairs={{0,16},{1,241},{2,18},{3,243},{4,20},{5,245},{6,22},{7,247},{8,24}... | collective-permute-start | bytes 884744 | tf_op jit(solution)/shard_map/ppermute | solution.py:37
  54.0 8.7 %collective-permute-start.4 = (bf16[3,192,256]{2,1,0:T(8,128)(2,1)S(1)}, bf16[3,192,256]{2,1,0:T(8,128)(2,1)S(1)}, u32[]{:S(2)}, u32[]{:S(2)}) collective-permute-start(bf16[3,192,256]{2,1,0:T(8,128)(2,1)S(1)} %collective-permute-done.3.refs_2_), channel_id=1, source_target_pairs={{0,16},{1,241},{2,18},{3,243},{4,20},{5,245},{6,22},{7,247},{8,24}... | collective-permute-start | bytes 884744 | tf_op jit(solution)/shard_map/ppermute | solution.py:37
  59.0 8.7 %collective-permute-start.12 = (bf16[3,192,256]{2,1,0:T(8,128)(2,1)S(1)}, bf16[3,192,256]{2,1,0:T(8,128)(2,1)S(1)}, u32[]{:S(2)}, u32[]{:S(2)}) collective-permute-start(bf16[3,192,256]{2,1,0:T(8,128)(2,1)S(1)} %collective-permute-done.11.refs_9_), channel_id=1, source_target_pairs={{0,16},{1,241},{2,18},{3,243},{4,20},{5,245},{6,22},{7,247},{8,24}... | collective-permute-start | bytes 884744 | tf_op jit(solution)/shard_map/ppermute | solution.py:37
  62.6 8.7 %collective-permute-start.5 = (bf16[3,192,256]{2,1,0:T(8,128)(2,1)S(1)}, bf16[3,192,256]{2,1,0:T(8,128)(2,1)S(1)}, u32[]{:S(2)}, u32[]{:S(2)}) collective-permute-start(bf16[3,192,256]{2,1,0:T(8,128)(2,1)S(1)} %collective-permute-done.4.refs_3_), channel_id=1, source_target_pairs={{0,16},{1,241},{2,18},{3,243},{4,20},{5,245},{6,22},{7,247},{8,24}... | collective-permute-start | bytes 884744 | tf_op jit(solution)/shard_map/ppermute | solution.py:37
  67.7 9.4 %collective-permute-start.13 = (bf16[3,192,256]{2,1,0:T(8,128)(2,1)S(1)}, bf16[3,192,256]{2,1,0:T(8,128)(2,1)S(1)}, u32[]{:S(2)}, u32[]{:S(2)}) collective-permute-start(bf16[3,192,256]{2,1,0:T(8,128)(2,1)S(1)} %collective-permute-done.12.refs_10_), channel_id=1, source_target_pairs={{0,16},{1,241},{2,18},{3,243},{4,20},{5,245},{6,22},{7,247},{8,24}... | collective-permute-start | bytes 884744 | tf_op jit(solution)/shard_map/ppermute | solution.py:37
  71.3 8.9 %collective-permute-start.6 = (bf16[3,192,256]{2,1,0:T(8,128)(2,1)S(1)}, bf16[3,192,256]{2,1,0:T(8,128)(2,1)}, u32[]{:S(2)}, u32[]{:S(2)}) collective-permute-start(bf16[3,192,256]{2,1,0:T(8,128)(2,1)S(1)} %collective-permute-done.5.refs_4_), channel_id=1, source_target_pairs={{0,16},{1,241},{2,18},{3,243},{4,20},{5,245},{6,22},{7,247},{8,24}... | collective-permute-start | bytes 884744 | tf_op jit(solution)/shard_map/ppermute | solution.py:37
  80.2 17.9 %collective-permute-start.7 = (bf16[3,192,256]{2,1,0:T(8,128)(2,1)}, bf16[3,192,256]{2,1,0:T(8,128)(2,1)S(1)}, u32[]{:S(2)}, u32[]{:S(2)}) collective-permute-start(bf16[3,192,256]{2,1,0:T(8,128)(2,1)} %collective-permute-done.6.refs_5_), channel_id=1, source_target_pairs={{0,16},{1,241},{2,18},{3,243},{4,20},{5,245},{6,22},{7,247},{8,24}... | collective-permute-start | bytes 884744 | tf_op jit(solution)/shard_map/ppermute | solution.py:37
  85.1 13.0 %collective-permute-start.15 = (bf16[3,192,256]{2,1,0:T(8,128)(2,1)}, bf16[3,192,256]{2,1,0:T(8,128)(2,1)S(1)}, u32[]{:S(2)}, u32[]{:S(2)}) collective-permute-start(bf16[3,192,256]{2,1,0:T(8,128)(2,1)} %collective-permute-done.14.refs_12_), channel_id=1, source_target_pairs={{0,16},{1,241},{2,18},{3,243},{4,20},{5,245},{6,22},{7,247},{8,24}... | collective-permute-start | bytes 884744 | tf_op jit(solution)/shard_map/ppermute | solution.py:37
  88.2 9.2 %collective-permute-start.23 = (bf16[192,256]{1,0:T(8,128)(2,1)}, bf16[192,256]{1,0:T(8,128)(2,1)S(1)}, u32[]{:S(2)}, u32[]{:S(2)}) collective-permute-start(bf16[192,256]{1,0:T(8,128)(2,1)} %bitcast.29), channel_id=1, source_target_pairs={{0,0},{1,256},{2,2},{3,258},{4,64},{5,320},{6,66},{7,322},{8,128},... | collective-permute-start | bytes 294920 | tf_op jit(solution)/shard_map/ppermute | solution.py:37
  98.9 23.1 %collective-permute-start.16 = (bf16[3,192,256]{2,1,0:T(8,128)(2,1)}, bf16[3,192,256]{2,1,0:T(8,128)(2,1)}, u32[]{:S(2)}, u32[]{:S(2)}) collective-permute-start(bf16[3,192,256]{2,1,0:T(8,128)(2,1)} %broadcast_select_fusion), channel_id=1, source_target_pairs={{0,16},{1,241},{2,18},{3,243},{4,20},{5,245},{6,22},{7,247},{8,24}... | collective-permute-start | bytes 884744 | tf_op jit(solution)/shard_map/ppermute | solution.py:37
  128.4 9.2 %collective-permute-start.17 = (f32[512,384]{1,0:T(8,128)S(1)}, f32[512,384]{1,0:T(8,128)S(1)}, u32[]{:S(2)}, u32[]{:S(2)}) collective-permute-start(f32[512,384]{1,0:T(8,128)S(1)} %get-tuple-element.10), channel_id=1, source_target_pairs={{0,1},{1,0},{2,3},{3,2},{4,5},{5,4},{6,7},{7,6},{8,9},{9,8},{10,11... | collective-permute-start | bytes 2359304 | tf_op jit(solution)/shard_map/ppermute | solution.py:37
  138.0 22.1 %collective-permute-start.19 = (bf16[2,512,128]{2,1,0:T(8,128)(2,1)S(1)}, bf16[2,512,128]{2,1,0:T(8,128)(2,1)S(1)}, u32[]{:S(2)}, u32[]{:S(2)}) collective-permute-start(bf16[2,512,128]{2,1,0:T(8,128)(2,1)S(1)} %get-tuple-element.12.refs_2_), channel_id=1, source_target_pairs={{0,32},{1,33},{2,34},{3,35},{4,36},{5,37},{6,38},{7,39},{8,40},{9,... | collective-permute-start | bytes 786440 | tf_op jit(solution)/shard_map/ppermute | solution.py:37
  139.9 25.7 %collective-permute-start.20 = (bf16[2,512,128]{2,1,0:T(8,128)(2,1)S(1)}, bf16[2,512,128]{2,1,0:T(8,128)(2,1)S(1)}, u32[]{:S(2)}, u32[]{:S(2)}) collective-permute-start(bf16[2,512,128]{2,1,0:T(8,128)(2,1)S(1)} %get-tuple-element.12.refs_2_), channel_id=1, source_target_pairs={{0,16},{1,17},{2,18},{3,19},{4,20},{5,21},{6,22},{7,23},{8,24},{9,... | collective-permute-start | bytes 786440 | tf_op jit(solution)/shard_map/ppermute | solution.py:37
  141.8 23.8 %collective-permute-start.21 = (bf16[2,512,128]{2,1,0:T(8,128)(2,1)S(1)}, bf16[2,512,128]{2,1,0:T(8,128)(2,1)S(1)}, u32[]{:S(2)}, u32[]{:S(2)}) collective-permute-start(bf16[2,512,128]{2,1,0:T(8,128)(2,1)S(1)} %get-tuple-element.12.refs_2_), channel_id=1, source_target_pairs={{0,240},{1,241},{2,242},{3,243},{4,244},{5,245},{6,246},{7,247},{8... | collective-permute-start | bytes 786440 | tf_op jit(solution)/shard_map/ppermute | solution.py:37
  146.7 21.2 %collective-permute-start.22 = (bf16[2,512,128]{2,1,0:T(8,128)(2,1)S(1)}, bf16[2,512,128]{2,1,0:T(8,128)(2,1)S(1)}, u32[]{:S(2)}, u32[]{:S(2)}) collective-permute-start(bf16[2,512,128]{2,1,0:T(8,128)(2,1)S(1)} %get-tuple-element.12.refs_2_), channel_id=1, source_target_pairs={{0,224},{1,225},{2,226},{3,227},{4,228},{5,229},{6,230},{7,231},{8... | collective-permute-start | bytes 786440 | tf_op jit(solution)/shard_map/ppermute | solution.py:37
  170.8 27.7 %all-to-all-start = ((bf16[8,512,128]{2,1,0:T(8,128)(2,1)}), bf16[8,512,128]{2,1,0:T(8,128)(2,1)S(1)}, u32[]{:S(2)}, u32[]{:S(2)}) async-start(bf16[8,512,128]{2,1,0:T(8,128)(2,1)} %shard_map.85), calls=%async_computation | async-start | bytes 2097152 | tf_op jit(solution)/shard_map/all_to_all | solution.py:274
  (13 other events, 169.2 us)
Sparse Core Ops, SparseCore 0:
  9.5 76.7 all-gather.4
  98.2 84.7 all-gather.6

commit v2 on v1

--- a/solution.py
+++ b/solution.py
@@ -58,7 +58,9 @@
 
 
 def out_weight(ylo, z, x, yh, core):
-    return core, x * 4 + ((z // 4) % 2) * 2 + z % 2, ylo * 2 + z // 8, yh, (z // 2) % 2
+    low = z % 8
+    nearby = z - low - 4 + 4 * (low % 2 + 2 * (low // 4)) + x
+    return core, nearby % 16, ylo * 2 + z // 8, yh, (z // 2) % 2
 
 
 def norm_kernel(place_ref, acts_ref, gain_ref, out_ref):
@@ -218,26 +220,28 @@
     )(place, query, *kvs)
 
 
-def out_kernel(heads_ref, weights_ref, out_ref):
+def out_kernel(place_ref, heads_ref, weights_ref, out_ref):
+    corner = 12 + 8 * lax.rem(place_ref[2], 2)
     for slot in range(2):
         part = jnp.zeros((256, 768), F32)
         for x in range(4):
             rows = slice(slot * 256, (slot + 1) * 256)
             pair = jnp.concatenate([heads_ref[2 * x, rows, :], heads_ref[2 * x + 1, rows, :]], axis=1)
-            part += lax.dot_general(pair, weights_ref[x], (((1,), (1,)), ((), ())), preferred_element_type=F32)
+            block = jnp.concatenate([weights_ref[lax.rem(corner + 4 * r + x, 16)] for r in range(4)], axis=0)
+            part += lax.dot_general(pair, block, (((1,), (1,)), ((), ())), preferred_element_type=F32)
         out_ref[slot] = part[:, :384].astype(BF)
         out_ref[2 + slot] = part[:, 384:].astype(BF)
 
 
-def project_out(heads, weights):
+def project_out(place, heads, weights):
     return pl.pallas_call(
         out_kernel,
         out_shape=jax.ShapeDtypeStruct((4, 256, 384), BF),
-        in_specs=[pl.BlockSpec(memory_space=pltpu.VMEM)] * 2,
+        in_specs=[pl.BlockSpec(memory_space=pltpu.SMEM)] + [pl.BlockSpec(memory_space=pltpu.VMEM)] * 2,
         out_specs=pl.BlockSpec(memory_space=pltpu.VMEM),
         compiler_params=pltpu.CompilerParams(vmem_limit_bytes=32 << 20),
         cost_estimate=pl.CostEstimate(flops=2 * 512 * 768 * 1024, bytes_accessed=3_500_000, transcendentals=0),
-    )(heads, weights)
+    )(place, heads, weights)
 
 
 def per_device(patches, ln_gain, w_query, w_key, w_value, query_gain, key_gain, w_out):
@@ -260,7 +264,7 @@
     own = jnp.where(core == 0, one, two)
 
     turned = send(w_out.T, out_weight)
-    out_weights = lax.all_gather(turned, "z", axis=0, tiled=False).reshape(4, 768, 256)
+    out_weights = lax.all_gather(turned, "z", axis=0, tiled=False)
 
     normed = normalise(place, acts, ln_gain)
     mine, theirs = multiply(place, normed, shards[0] + shards[1] + [own, last])
@@ -272,7 +276,7 @@
     near[0] = kv
     attended = attend(place, query, [near[o] for o in (-2, -1, 0, 1, 2)])
     heads = lax.all_to_all(attended, ("x", "core"), 0, 0, tiled=True)
-    parts = project_out(heads, out_weights)
+    parts = project_out(place, heads, out_weights)
     parts = lax.all_to_all(parts, ("yh", "ylo"), 0, 0, tiled=True)
     return jnp.sum(parts.astype(F32), axis=0).astype(BF)
 

time: 225 us -> 216 us (0.960)
  starting transfers between devices: 115 us -> 100 us
  waiting for transfers between devices: 52.4 us -> 58.2 us
    ppermute x24, starting transfers between devices: 103 us -> 93.5 us  [send(): return lax.ppermute(value, AXES, pairs)]
    all_to_all x1, starting transfers between devices: 12.6 us -> 6.54 us  [per_device(): heads = lax.all_to_all(attended, ('x', 'core'), 0, 0, tiled=True)]
    ppermute x24, waiting for transfers between devices: 36.6 us -> 42.4 us  [send(): return lax.ppermute(value, AXES, pairs)]
    all_gather x1, waiting for transfers between devices: 0.01 us -> 4.34 us  [per_device(): out_weights = lax.all_gather(turned, 'z', axis=0, tiled=False)]
    all_to_all x1, waiting for transfers between devices: 15.1 us -> 10.8 us  [per_device(): heads = lax.all_to_all(attended, ('x', 'core'), 0, 0, tiled=True)]
  transfers between devices with their start and end apart: 27 -> 27, of which waited for: 13 -> 14; matrix products, arithmetic and copies ran while one was open for 1% -> 1% of each run, Pallas kernels for 7% -> 7%
where the time goes in v2:
time: 216 us; the launch traced here: 215 us
  starting transfers between devices  100 us (46%)
  waiting for transfers between devices  58.2 us (27%)
  Pallas kernels  17.6 us (8%)
  blocking collectives  15.5 us (7%)
  between operations  13.8 us (6%)
  local copies, waits for them, and re-layouts  6.38 us (3%)
  other arithmetic  3.68 us (2%)
    ppermute x24, starting transfers between devices, send(): return lax.ppermute(value, AXES, pairs)  93.5 us
    ppermute x24, waiting for transfers between devices, send(): return lax.ppermute(value, AXES, pairs)  42.4 us
    all_to_all x1, blocking collectives, per_device(): parts = lax.all_to_all(parts, ('yh', 'ylo'), 0, 0, tiled=True)  15.5 us
    all_to_all x1, waiting for transfers between devices, per_device(): heads = lax.all_to_all(attended, ('x', 'core'), 0, 0, tiled=True)  10.8 us
    all_to_all x1, starting transfers between devices, per_device(): heads = lax.all_to_all(attended, ('x', 'core'), 0, 0, tiled=True)  6.54 us
    pallas_call x1, Pallas kernels, normalise(): pl.pallas_call(norm_kernel, grid=(2, 256 // rows), out_shape=jax.ShapeDty...  6.4 us
    pallas_call x1, Pallas kernels, multiply(): pl.pallas_call(product_kernel, grid=(512 // rows,), out_shape=[jax.ShapeD...  6.34 us
    unnamed x20, local copies, waits for them, and re-layouts  6.29 us
  transfers between devices with their start and end apart: 27, of which 14 were waited for; matrix products, arithmetic and copies ran while one was open for 1% of the time, Pallas kernels for 7%

profile of v2, /device:TPU:1, one launch (start us, length us, event | category | flops | bytes accessed | tf_op | source)
XLA Modules:
  0.0 215.3 jit_solution(13368260347661498483)
XLA Ops:
  8.3 4.0 %collective-permute-start = (bf16[3,192,256]{2,1,0:T(8,128)(2,1)S(1)}, bf16[3,192,256]{2,1,0:T(8,128)(2,1)S(1)}, u32[]{:S(2)}, u32[]{:S(2)}) collective-permute-start(bf16[3,192,256]{2,1,0:T(8,128)(2,1)S(1)} %pad_maximum_fusion), channel_id=1, source_target_pairs={{0,1},{1,257},{2,3},{3,259},{4,5},{5,261},{6,7},{7,263},{8,9},{9,2... | collective-permute-start | bytes 884744 | tf_op jit(solution)/shard_map/ppermute | solution.py:37
  12.4 5.8 %collective-permute-done = bf16[3,192,256]{2,1,0:T(8,128)(2,1)S(1)} collective-permute-done((bf16[3,192,256]{2,1,0:T(8,128)(2,1)S(1)}, bf16[3,192,256]{2,1,0:T(8,128)(2,1)S(1)}, u32[]{:S(2)}, u32[]{:S(2)}) %collective-permute-start) | collective-permute-done | bytes 294944 | tf_op jit(solution)/shard_map/ppermute | solution.py:37
  19.5 6.7 %collective-permute-done.8 = bf16[3,192,256]{2,1,0:T(8,128)(2,1)S(1)} collective-permute-done((bf16[3,192,256]{2,1,0:T(8,128)(2,1)S(1)}, bf16[3,192,256]{2,1,0:T(8,128)(2,1)S(1)}, u32[]{:S(2)}, u32[]{:S(2)}) %collective-permute-start.8) | collective-permute-done | bytes 294944 | tf_op jit(solution)/shard_map/ppermute | solution.py:37
  27.2 5.7 %collective-permute-start.1 = (bf16[3,192,256]{2,1,0:T(8,128)(2,1)S(1)}, bf16[3,192,256]{2,1,0:T(8,128)(2,1)S(1)}, u32[]{:S(2)}, u32[]{:S(2)}) collective-permute-start(bf16[3,192,256]{2,1,0:T(8,128)(2,1)S(1)} %get-tuple-element.15), channel_id=1, source_target_pairs={{0,16},{1,241},{2,18},{3,243},{4,20},{5,245},{6,22},{7,247},{8,24}... | collective-permute-start | bytes 884744 | tf_op jit(solution)/shard_map/ppermute | solution.py:37
  36.6 5.0 %collective-permute-start.2 = (bf16[3,192,256]{2,1,0:T(8,128)(2,1)S(1)}, bf16[3,192,256]{2,1,0:T(8,128)(2,1)S(1)}, u32[]{:S(2)}, u32[]{:S(2)}) collective-permute-start(bf16[3,192,256]{2,1,0:T(8,128)(2,1)S(1)} %collective-permute-done.1.refs_0_), channel_id=1, source_target_pairs={{0,16},{1,241},{2,18},{3,243},{4,20},{5,245},{6,22},{7,247},{8,24}... | collective-permute-start | bytes 884744 | tf_op jit(solution)/shard_map/ppermute | solution.py:37
  41.7 3.1 %collective-permute-start.10 = (bf16[3,192,256]{2,1,0:T(8,128)(2,1)S(1)}, bf16[3,192,256]{2,1,0:T(8,128)(2,1)S(1)}, u32[]{:S(2)}, u32[]{:S(2)}) collective-permute-start(bf16[3,192,256]{2,1,0:T(8,128)(2,1)S(1)} %collective-permute-done.9.refs_7_), channel_id=1, source_target_pairs={{0,16},{1,241},{2,18},{3,243},{4,20},{5,245},{6,22},{7,247},{8,24}... | collective-permute-start | bytes 884744 | tf_op jit(solution)/shard_map/ppermute | solution.py:37
  45.3 5.0 %collective-permute-start.3 = (bf16[3,192,256]{2,1,0:T(8,128)(2,1)S(1)}, bf16[3,192,256]{2,1,0:T(8,128)(2,1)S(1)}, u32[]{:S(2)}, u32[]{:S(2)}) collective-permute-start(bf16[3,192,256]{2,1,0:T(8,128)(2,1)S(1)} %collective-permute-done.2.refs_1_), channel_id=1, source_target_pairs={{0,16},{1,241},{2,18},{3,243},{4,20},{5,245},{6,22},{7,247},{8,24}... | collective-permute-start | bytes 884744 | tf_op jit(solution)/shard_map/ppermute | solution.py:37
  54.0 5.0 %collective-permute-start.4 = (bf16[3,192,256]{2,1,0:T(8,128)(2,1)S(1)}, bf16[3,192,256]{2,1,0:T(8,128)(2,1)S(1)}, u32[]{:S(2)}, u32[]{:S(2)}) collective-permute-start(bf16[3,192,256]{2,1,0:T(8,128)(2,1)S(1)} %collective-permute-done.3.refs_2_), channel_id=1, source_target_pairs={{0,16},{1,241},{2,18},{3,243},{4,20},{5,245},{6,22},{7,247},{8,24}... | collective-permute-start | bytes 884744 | tf_op jit(solution)/shard_map/ppermute | solution.py:37
  59.0 3.1 %collective-permute-start.12 = (bf16[3,192,256]{2,1,0:T(8,128)(2,1)S(1)}, bf16[3,192,256]{2,1,0:T(8,128)(2,1)S(1)}, u32[]{:S(2)}, u32[]{:S(2)}) collective-permute-start(bf16[3,192,256]{2,1,0:T(8,128)(2,1)S(1)} %collective-permute-done.11.refs_9_), channel_id=1, source_target_pairs={{0,16},{1,241},{2,18},{3,243},{4,20},{5,245},{6,22},{7,247},{8,24}... | collective-permute-start | bytes 884744 | tf_op jit(solution)/shard_map/ppermute | solution.py:37
  62.6 5.0 %collective-permute-start.5 = (bf16[3,192,256]{2,1,0:T(8,128)(2,1)S(1)}, bf16[3,192,256]{2,1,0:T(8,128)(2,1)S(1)}, u32[]{:S(2)}, u32[]{:S(2)}) collective-permute-start(bf16[3,192,256]{2,1,0:T(8,128)(2,1)S(1)} %collective-permute-done.4.refs_3_), channel_id=1, source_target_pairs={{0,16},{1,241},{2,18},{3,243},{4,20},{5,245},{6,22},{7,247},{8,24}... | collective-permute-start | bytes 884744 | tf_op jit(solution)/shard_map/ppermute | solution.py:37
  71.3 5.0 %collective-permute-start.6 = (bf16[3,192,256]{2,1,0:T(8,128)(2,1)S(1)}, bf16[3,192,256]{2,1,0:T(8,128)(2,1)}, u32[]{:S(2)}, u32[]{:S(2)}) collective-permute-start(bf16[3,192,256]{2,1,0:T(8,128)(2,1)S(1)} %collective-permute-done.5.refs_4_), channel_id=1, source_target_pairs={{0,16},{1,241},{2,18},{3,243},{4,20},{5,245},{6,22},{7,247},{8,24}... | collective-permute-start | bytes 884744 | tf_op jit(solution)/shard_map/ppermute | solution.py:37
  80.2 4.9 %collective-permute-start.7 = (bf16[3,192,256]{2,1,0:T(8,128)(2,1)}, bf16[3,192,256]{2,1,0:T(8,128)(2,1)S(1)}, u32[]{:S(2)}, u32[]{:S(2)}) collective-permute-start(bf16[3,192,256]{2,1,0:T(8,128)(2,1)} %collective-permute-done.6.refs_5_), channel_id=1, source_target_pairs={{0,16},{1,241},{2,18},{3,243},{4,20},{5,245},{6,22},{7,247},{8,24}... | collective-permute-start | bytes 884744 | tf_op jit(solution)/shard_map/ppermute | solution.py:37
  88.2 10.1 %collective-permute-start.23 = (bf16[192,256]{1,0:T(8,128)(2,1)}, bf16[192,256]{1,0:T(8,128)(2,1)S(1)}, u32[]{:S(2)}, u32[]{:S(2)}) collective-permute-start(bf16[192,256]{1,0:T(8,128)(2,1)} %bitcast.29), channel_id=1, source_target_pairs={{0,192},{1,448},{2,194},{3,450},{4,208},{5,464},{6,210},{7,466},{8... | collective-permute-start | bytes 294920 | tf_op jit(solution)/shard_map/ppermute | solution.py:37
  108.0 6.4 %shard_map.82.normed_ref = bf16[512,3456]{1,0:T(8,128)(2,1)S(1)} custom-call(s32[5]{0:T(128)S(1)} %stack.44.place_ref, bf16[2,16,256,384]{3,2,1,0:T(8,128)(2,1)S(1)} %bitcast.17, f32[16,384]{1,0:T(8,128)S(1)} %reshape.12.gain_ref), custom_call_target="tpu_custom_call" | custom-call | flops 30000000 | bytes 10000000 | tf_op jit(solution)/shard_map/pallas_call | solution.py:91
  114.5 6.3 %shard_map.83 = (f32[512,384]{1,0:T(8,128)S(1)}, f32[512,384]{1,0:T(8,128)S(1)}) custom-call(s32[5]{0:T(128)S(1)} %stack.44.place_ref, bf16[512,3456]{1,0:T(8,128)(2,1)S(1)} %shard_map.82.normed_ref, bf16[3,192,256]{2,1,0:T(8,128)(2,1)S(1)} %collective-permute-done.1.refs_0_, bf16[3,192,256]{2,1,0:T(8,128)(2,1)S(1)} %collective-permute-done.2.refs_1_, ...), custom_call_target="tpu_custom_call" | custom-call | flops 2717908992 | bytes 10000000 | tf_op jit(solution)/shard_map/pallas_call | solution.py:148
  127.4 4.0 %collective-permute-start.19 = (bf16[2,512,128]{2,1,0:T(8,128)(2,1)S(1)}, bf16[2,512,128]{2,1,0:T(8,128)(2,1)S(1)}, u32[]{:S(2)}, u32[]{:S(2)}) collective-permute-start(bf16[2,512,128]{2,1,0:T(8,128)(2,1)S(1)} %get-tuple-element.12.refs_2_), channel_id=1, source_target_pairs={{0,32},{1,33},{2,34},{3,35},{4,36},{5,37},{6,38},{7,39},{8,40},{9,... | collective-permute-start | bytes 786440 | tf_op jit(solution)/shard_map/ppermute | solution.py:37
  133.4 4.6 %collective-permute-start.21 = (bf16[2,512,128]{2,1,0:T(8,128)(2,1)S(1)}, bf16[2,512,128]{2,1,0:T(8,128)(2,1)S(1)}, u32[]{:S(2)}, u32[]{:S(2)}) collective-permute-start(bf16[2,512,128]{2,1,0:T(8,128)(2,1)S(1)} %get-tuple-element.12.refs_2_), channel_id=1, source_target_pairs={{0,240},{1,241},{2,242},{3,243},{4,244},{5,245},{6,246},{7,247},{8... | collective-permute-start | bytes 786440 | tf_op jit(solution)/shard_map/ppermute | solution.py:37
  141.2 6.0 %collective-permute-done.19.refs_0_ = bf16[2,512,128]{2,1,0:T(8,128)(2,1)S(1)} collective-permute-done((bf16[2,512,128]{2,1,0:T(8,128)(2,1)S(1)}, bf16[2,512,128]{2,1,0:T(8,128)(2,1)S(1)}, u32[]{:S(2)}, u32[]{:S(2)}) %collective-permute-start.19) | collective-permute-done | bytes 262176 | tf_op jit(solution)/shard_map/ppermute | solution.py:37
  147.1 8.7 %collective-permute-done.20.refs_1_ = bf16[2,512,128]{2,1,0:T(8,128)(2,1)S(1)} collective-permute-done((bf16[2,512,128]{2,1,0:T(8,128)(2,1)S(1)}, bf16[2,512,128]{2,1,0:T(8,128)(2,1)S(1)}, u32[]{:S(2)}, u32[]{:S(2)}) %collective-permute-start.20) | collective-permute-done | bytes 262176 | tf_op jit(solution)/shard_map/ppermute | solution.py:37
  155.8 8.8 %collective-permute-done.22.refs_4_ = bf16[2,512,128]{2,1,0:T(8,128)(2,1)S(1)} collective-permute-done((bf16[2,512,128]{2,1,0:T(8,128)(2,1)S(1)}, bf16[2,512,128]{2,1,0:T(8,128)(2,1)S(1)}, u32[]{:S(2)}, u32[]{:S(2)}) %collective-permute-start.22) | collective-permute-done | bytes 262176 | tf_op jit(solution)/shard_map/ppermute | solution.py:37
  167.5 6.5 %all-to-all-start = ((bf16[8,512,128]{2,1,0:T(8,128)(2,1)}), bf16[8,512,128]{2,1,0:T(8,128)(2,1)S(1)}, u32[]{:S(2)}, u32[]{:S(2)}) async-start(bf16[8,512,128]{2,1,0:T(8,128)(2,1)} %shard_map.85), calls=%async_computation | async-start | bytes 2097152 | tf_op jit(solution)/shard_map/all_to_all | solution.py:278
  174.1 4.3 %all-gather.7.cloned.1.call-done = bf16[3072,256]{1,0:T(8,128)(2,1)} async-done(((bf16[192,256]{1,0:T(8,128)(2,1)}), bf16[3072,256]{1,0:T(8,128)(2,1)}) %all-gather.7.cloned.1.call-update) | async-done | bytes 1572880 | tf_op jit(solution)/shard_map/all_gather | solution.py:267
  178.4 10.8 %all-to-all-done.heads_ref = bf16[8,512,128]{2,1,0:T(8,128)(2,1)S(1)} async-done(((bf16[8,512,128]{2,1,0:T(8,128)(2,1)}), bf16[8,512,128]{2,1,0:T(8,128)(2,1)S(1)}, u32[]{:S(2)}, u32[]{:S(2)}) %all-to-all-start) | async-done | bytes 1048608 | tf_op jit(solution)/shard_map/all_to_all | solution.py:278
  192.1 15.5 %all_to_all.10 = bf16[4,256,384]{2,1,0:T(8,128)(2,1)S(1)} all-to-all(bf16[4,256,384]{2,1,0:T(8,128)(2,1)S(1)} %shard_map.86), channel_id=1, replica_groups=mesh['ylo'=2,'z'=16,'x'=4,'yh'=2,'core'=2] {'yh','ylo'}, dimensions={0} | all-to-all | bytes 1572864 | tf_op jit(solution)/shard_map/all_to_all | solution.py:280
  (67 shorter events, 50.9 us)
Async XLA Ops:
  6.5 98.7 %all-gather.5.cloned.1.call-start = ((), (), s32[]{:S(2)}) async-start(), calls=%async_computation.2 | async-start | bytes 6488064 | tf_op jit(solution)/shard_map/all_gather | solution.py:251
  7.3 171.2 %all-gather.7.cloned.1.call-start = ((), (), s32[]{:S(2)}) async-start(), calls=%async_computation.3 | async-start | bytes 1671168 | tf_op jit(solution)/shard_map/all_gather | solution.py:267
  8.3 9.9 %collective-permute-start = (bf16[3,192,256]{2,1,0:T(8,128)(2,1)S(1)}, bf16[3,192,256]{2,1,0:T(8,128)(2,1)S(1)}, u32[]{:S(2)}, u32[]{:S(2)}) collective-permute-start(bf16[3,192,256]{2,1,0:T(8,128)(2,1)S(1)} %pad_maximum_fusion), channel_id=1, source_target_pairs={{0,1},{1,257},{2,3},{3,259},{4,5},{5,261},{6,7},{7,263},{8,9},{9,2... | collective-permute-start | bytes 884744 | tf_op jit(solution)/shard_map/ppermute | solution.py:37
  27.2 9.4 %collective-permute-start.1 = (bf16[3,192,256]{2,1,0:T(8,128)(2,1)S(1)}, bf16[3,192,256]{2,1,0:T(8,128)(2,1)S(1)}, u32[]{:S(2)}, u32[]{:S(2)}) collective-permute-start(bf16[3,192,256]{2,1,0:T(8,128)(2,1)S(1)} %get-tuple-element.15), channel_id=1, source_target_pairs={{0,16},{1,241},{2,18},{3,243},{4,20},{5,245},{6,22},{7,247},{8,24}... | collective-permute-start | bytes 884744 | tf_op jit(solution)/shard_map/ppermute | solution.py:37
  33.0 8.7 %collective-permute-start.9 = (bf16[3,192,256]{2,1,0:T(8,128)(2,1)S(1)}, bf16[3,192,256]{2,1,0:T(8,128)(2,1)S(1)}, u32[]{:S(2)}, u32[]{:S(2)}) collective-permute-start(bf16[3,192,256]{2,1,0:T(8,128)(2,1)S(1)} %get-tuple-element.14), channel_id=1, source_target_pairs={{0,16},{1,241},{2,18},{3,243},{4,20},{5,245},{6,22},{7,247},{8,24}... | collective-permute-start | bytes 884744 | tf_op jit(solution)/shard_map/ppermute | solution.py:37
  36.6 8.7 %collective-permute-start.2 = (bf16[3,192,256]{2,1,0:T(8,128)(2,1)S(1)}, bf16[3,192,256]{2,1,0:T(8,128)(2,1)S(1)}, u32[]{:S(2)}, u32[]{:S(2)}) collective-permute-start(bf16[3,192,256]{2,1,0:T(8,128)(2,1)S(1)} %collective-permute-done.1.refs_0_), channel_id=1, source_target_pairs={{0,16},{1,241},{2,18},{3,243},{4,20},{5,245},{6,22},{7,247},{8,24}... | collective-permute-start | bytes 884744 | tf_op jit(solution)/shard_map/ppermute | solution.py:37
  41.7 8.7 %collective-permute-start.10 = (bf16[3,192,256]{2,1,0:T(8,128)(2,1)S(1)}, bf16[3,192,256]{2,1,0:T(8,128)(2,1)S(1)}, u32[]{:S(2)}, u32[]{:S(2)}) collective-permute-start(bf16[3,192,256]{2,1,0:T(8,128)(2,1)S(1)} %collective-permute-done.9.refs_7_), channel_id=1, source_target_pairs={{0,16},{1,241},{2,18},{3,243},{4,20},{5,245},{6,22},{7,247},{8,24}... | collective-permute-start | bytes 884744 | tf_op jit(solution)/shard_map/ppermute | solution.py:37
  45.3 8.7 %collective-permute-start.3 = (bf16[3,192,256]{2,1,0:T(8,128)(2,1)S(1)}, bf16[3,192,256]{2,1,0:T(8,128)(2,1)S(1)}, u32[]{:S(2)}, u32[]{:S(2)}) collective-permute-start(bf16[3,192,256]{2,1,0:T(8,128)(2,1)S(1)} %collective-permute-done.2.refs_1_), channel_id=1, source_target_pairs={{0,16},{1,241},{2,18},{3,243},{4,20},{5,245},{6,22},{7,247},{8,24}... | collective-permute-start | bytes 884744 | tf_op jit(solution)/shard_map/ppermute | solution.py:37
  50.3 8.7 %collective-permute-start.11 = (bf16[3,192,256]{2,1,0:T(8,128)(2,1)S(1)}, bf16[3,192,256]{2,1,0:T(8,128)(2,1)S(1)}, u32[]{:S(2)}, u32[]{:S(2)}) collective-permute-start(bf16[3,192,256]{2,1,0:T(8,128)(2,1)S(1)} %collective-permute-done.10.refs_8_), channel_id=1, source_target_pairs={{0,16},{1,241},{2,18},{3,243},{4,20},{5,245},{6,22},{7,247},{8,24}... | collective-permute-start | bytes 884744 | tf_op jit(solution)/shard_map/ppermute | solution.py:37
  54.0 8.7 %collective-permute-start.4 = (bf16[3,192,256]{2,1,0:T(8,128)(2,1)S(1)}, bf16[3,192,256]{2,1,0:T(8,128)(2,1)S(1)}, u32[]{:S(2)}, u32[]{:S(2)}) collective-permute-start(bf16[3,192,256]{2,1,0:T(8,128)(2,1)S(1)} %collective-permute-done.3.refs_2_), channel_id=1, source_target_pairs={{0,16},{1,241},{2,18},{3,243},{4,20},{5,245},{6,22},{7,247},{8,24}... | collective-permute-start | bytes 884744 | tf_op jit(solution)/shard_map/ppermute | solution.py:37
  59.0 8.7 %collective-permute-start.12 = (bf16[3,192,256]{2,1,0:T(8,128)(2,1)S(1)}, bf16[3,192,256]{2,1,0:T(8,128)(2,1)S(1)}, u32[]{:S(2)}, u32[]{:S(2)}) collective-permute-start(bf16[3,192,256]{2,1,0:T(8,128)(2,1)S(1)} %collective-permute-done.11.refs_9_), channel_id=1, source_target_pairs={{0,16},{1,241},{2,18},{3,243},{4,20},{5,245},{6,22},{7,247},{8,24}... | collective-permute-start | bytes 884744 | tf_op jit(solution)/shard_map/ppermute | solution.py:37
  62.6 8.7 %collective-permute-start.5 = (bf16[3,192,256]{2,1,0:T(8,128)(2,1)S(1)}, bf16[3,192,256]{2,1,0:T(8,128)(2,1)S(1)}, u32[]{:S(2)}, u32[]{:S(2)}) collective-permute-start(bf16[3,192,256]{2,1,0:T(8,128)(2,1)S(1)} %collective-permute-done.4.refs_3_), channel_id=1, source_target_pairs={{0,16},{1,241},{2,18},{3,243},{4,20},{5,245},{6,22},{7,247},{8,24}... | collective-permute-start | bytes 884744 | tf_op jit(solution)/shard_map/ppermute | solution.py:37
  67.7 9.4 %collective-permute-start.13 = (bf16[3,192,256]{2,1,0:T(8,128)(2,1)S(1)}, bf16[3,192,256]{2,1,0:T(8,128)(2,1)S(1)}, u32[]{:S(2)}, u32[]{:S(2)}) collective-permute-start(bf16[3,192,256]{2,1,0:T(8,128)(2,1)S(1)} %collective-permute-done.12.refs_10_), channel_id=1, source_target_pairs={{0,16},{1,241},{2,18},{3,243},{4,20},{5,245},{6,22},{7,247},{8,24}... | collective-permute-start | bytes 884744 | tf_op jit(solution)/shard_map/ppermute | solution.py:37
  71.3 8.9 %collective-permute-start.6 = (bf16[3,192,256]{2,1,0:T(8,128)(2,1)S(1)}, bf16[3,192,256]{2,1,0:T(8,128)(2,1)}, u32[]{:S(2)}, u32[]{:S(2)}) collective-permute-start(bf16[3,192,256]{2,1,0:T(8,128)(2,1)S(1)} %collective-permute-done.5.refs_4_), channel_id=1, source_target_pairs={{0,16},{1,241},{2,18},{3,243},{4,20},{5,245},{6,22},{7,247},{8,24}... | collective-permute-start | bytes 884744 | tf_op jit(solution)/shard_map/ppermute | solution.py:37
  77.1 8.0 %collective-permute-start.14 = (bf16[3,192,256]{2,1,0:T(8,128)(2,1)S(1)}, bf16[3,192,256]{2,1,0:T(8,128)(2,1)}, u32[]{:S(2)}, u32[]{:S(2)}) collective-permute-start(bf16[3,192,256]{2,1,0:T(8,128)(2,1)S(1)} %collective-permute-done.13.refs_11_), channel_id=1, source_target_pairs={{0,16},{1,241},{2,18},{3,243},{4,20},{5,245},{6,22},{7,247},{8,24}... | collective-permute-start | bytes 884744 | tf_op jit(solution)/shard_map/ppermute | solution.py:37
  80.2 21.2 %collective-permute-start.7 = (bf16[3,192,256]{2,1,0:T(8,128)(2,1)}, bf16[3,192,256]{2,1,0:T(8,128)(2,1)S(1)}, u32[]{:S(2)}, u32[]{:S(2)}) collective-permute-start(bf16[3,192,256]{2,1,0:T(8,128)(2,1)} %collective-permute-done.6.refs_5_), channel_id=1, source_target_pairs={{0,16},{1,241},{2,18},{3,243},{4,20},{5,245},{6,22},{7,247},{8,24}... | collective-permute-start | bytes 884744 | tf_op jit(solution)/shard_map/ppermute | solution.py:37
  85.1 16.3 %collective-permute-start.15 = (bf16[3,192,256]{2,1,0:T(8,128)(2,1)}, bf16[3,192,256]{2,1,0:T(8,128)(2,1)S(1)}, u32[]{:S(2)}, u32[]{:S(2)}) collective-permute-start(bf16[3,192,256]{2,1,0:T(8,128)(2,1)} %collective-permute-done.14.refs_12_), channel_id=1, source_target_pairs={{0,16},{1,241},{2,18},{3,243},{4,20},{5,245},{6,22},{7,247},{8,24}... | collective-permute-start | bytes 884744 | tf_op jit(solution)/shard_map/ppermute | solution.py:37
  88.2 12.5 %collective-permute-start.23 = (bf16[192,256]{1,0:T(8,128)(2,1)}, bf16[192,256]{1,0:T(8,128)(2,1)S(1)}, u32[]{:S(2)}, u32[]{:S(2)}) collective-permute-start(bf16[192,256]{1,0:T(8,128)(2,1)} %bitcast.29), channel_id=1, source_target_pairs={{0,192},{1,448},{2,194},{3,450},{4,208},{5,464},{6,210},{7,466},{8... | collective-permute-start | bytes 294920 | tf_op jit(solution)/shard_map/ppermute | solution.py:37
  102.2 12.2 %collective-permute-start.16 = (bf16[3,192,256]{2,1,0:T(8,128)(2,1)}, bf16[3,192,256]{2,1,0:T(8,128)(2,1)}, u32[]{:S(2)}, u32[]{:S(2)}) collective-permute-start(bf16[3,192,256]{2,1,0:T(8,128)(2,1)} %broadcast_select_fusion), channel_id=1, source_target_pairs={{0,16},{1,241},{2,18},{3,243},{4,20},{5,245},{6,22},{7,247},{8,24}... | collective-permute-start | bytes 884744 | tf_op jit(solution)/shard_map/ppermute | solution.py:37
  127.4 19.7 %collective-permute-start.19 = (bf16[2,512,128]{2,1,0:T(8,128)(2,1)S(1)}, bf16[2,512,128]{2,1,0:T(8,128)(2,1)S(1)}, u32[]{:S(2)}, u32[]{:S(2)}) collective-permute-start(bf16[2,512,128]{2,1,0:T(8,128)(2,1)S(1)} %get-tuple-element.12.refs_2_), channel_id=1, source_target_pairs={{0,32},{1,33},{2,34},{3,35},{4,36},{5,37},{6,38},{7,39},{8,40},{9,... | collective-permute-start | bytes 786440 | tf_op jit(solution)/shard_map/ppermute | solution.py:37
  131.5 24.3 %collective-permute-start.20 = (bf16[2,512,128]{2,1,0:T(8,128)(2,1)S(1)}, bf16[2,512,128]{2,1,0:T(8,128)(2,1)S(1)}, u32[]{:S(2)}, u32[]{:S(2)}) collective-permute-start(bf16[2,512,128]{2,1,0:T(8,128)(2,1)S(1)} %get-tuple-element.12.refs_2_), channel_id=1, source_target_pairs={{0,16},{1,17},{2,18},{3,19},{4,20},{5,21},{6,22},{7,23},{8,24},{9,... | collective-permute-start | bytes 786440 | tf_op jit(solution)/shard_map/ppermute | solution.py:37
  133.4 22.4 %collective-permute-start.21 = (bf16[2,512,128]{2,1,0:T(8,128)(2,1)S(1)}, bf16[2,512,128]{2,1,0:T(8,128)(2,1)S(1)}, u32[]{:S(2)}, u32[]{:S(2)}) collective-permute-start(bf16[2,512,128]{2,1,0:T(8,128)(2,1)S(1)} %get-tuple-element.12.refs_2_), channel_id=1, source_target_pairs={{0,240},{1,241},{2,242},{3,243},{4,244},{5,245},{6,246},{7,247},{8... | collective-permute-start | bytes 786440 | tf_op jit(solution)/shard_map/ppermute | solution.py:37
  138.0 26.6 %collective-permute-start.22 = (bf16[2,512,128]{2,1,0:T(8,128)(2,1)S(1)}, bf16[2,512,128]{2,1,0:T(8,128)(2,1)S(1)}, u32[]{:S(2)}, u32[]{:S(2)}) collective-permute-start(bf16[2,512,128]{2,1,0:T(8,128)(2,1)S(1)} %get-tuple-element.12.refs_2_), channel_id=1, source_target_pairs={{0,224},{1,225},{2,226},{3,227},{4,228},{5,229},{6,230},{7,231},{8... | collective-permute-start | bytes 786440 | tf_op jit(solution)/shard_map/ppermute | solution.py:37
  167.5 21.6 %all-to-all-start = ((bf16[8,512,128]{2,1,0:T(8,128)(2,1)}), bf16[8,512,128]{2,1,0:T(8,128)(2,1)S(1)}, u32[]{:S(2)}, u32[]{:S(2)}) async-start(bf16[8,512,128]{2,1,0:T(8,128)(2,1)} %shard_map.85), calls=%async_computation | async-start | bytes 2097152 | tf_op jit(solution)/shard_map/all_to_all | solution.py:278
  (13 other events, 153.9 us)
Sparse Core Ops, SparseCore 0:
  9.5 76.7 all-gather.4
  101.5 76.8 all-gather.6

commit v3 on v2

--- a/solution.py
+++ b/solution.py
@@ -110,7 +110,7 @@
     return centred * lax.rsqrt(spread + EPS) * gain
 
 
-def product_kernel(place_ref, normed_ref, *refs):
+def product_kernel(place_ref, gains_ref, normed_ref, *refs):
     first, second, own, last = refs[:7], refs[7:14], refs[14], refs[15]
     mine_ref, theirs_ref, weights, sem = refs[16:]
     core = place_ref[4]
@@ -140,41 +140,47 @@
     for m in range(3):
         one, two = raw[:, m * 256 : m * 256 + HD], raw[:, m * 256 + HD : (m + 1) * 256]
         mine_ref[:, m * HD : (m + 1) * HD] = jnp.where(core == 0, one, two)
-        theirs_ref[:, m * HD : (m + 1) * HD] = jnp.where(core == 0, two, one)
-
-
-def multiply(place, normed, shards):
+        theirs_ref[:128, m * HD : (m + 1) * HD] = jnp.where(core == 0, two, one)
+    theirs_ref[128:, :] = gains_ref[...]
+
+
+def multiply(place, gains, normed, shards):
     rows = 128
     return pl.pallas_call(
         product_kernel,
         grid=(512 // rows,),
-        out_shape=[jax.ShapeDtypeStruct((512, 3 * HD), F32)] * 2,
-        in_specs=[pl.BlockSpec(memory_space=pltpu.SMEM), pl.BlockSpec((rows, WINDOW), lambda r: (r, 0))]
+        out_shape=[jax.ShapeDtypeStruct((512, 3 * HD), F32), jax.ShapeDtypeStruct((544, 3 * HD), F32)],
+        in_specs=[pl.BlockSpec(memory_space=pltpu.SMEM), pl.BlockSpec((8, 3 * HD), lambda r: (0, 0)), pl.BlockSpec((rows, WINDOW), lambda r: (r, 0))]
         + [pl.BlockSpec(memory_space=pl.ANY)] * 16,
-        out_specs=[pl.BlockSpec((rows, 3 * HD), lambda r: (r, 0))] * 2,
+        out_specs=[pl.BlockSpec((n, 3 * HD), lambda r: (r, 0)) for n in (rows, rows + 8)],
         scratch_shapes=[pltpu.VMEM((WINDOW, 768), BF), pltpu.SemaphoreType.DMA((48,))],
         compiler_params=pltpu.CompilerParams(vmem_limit_bytes=32 << 20),
         cost_estimate=pl.CostEstimate(flops=2 * 512 * WINDOW * 768, bytes_accessed=10_000_000, transcendentals=0),
-    )(place, normed, *shards)
-
-
-def heads_kernel(mine_ref, theirs_ref, gains_ref, q_ref, kv_ref):
-    raw = mine_ref[...] + theirs_ref[...]
-    query = head_norm(raw[:, :HD], gains_ref[0:1, :]) * HD ** (-0.5)
-    q_ref[...] = query.astype(BF)
-    kv_ref[0] = head_norm(raw[:, HD : 2 * HD], gains_ref[1:2, :]).astype(BF)
-    kv_ref[1] = raw[:, 2 * HD :].astype(BF)
-
-
-def split_heads(mine, theirs, gains):
+    )(place, gains, normed, *shards)
+
+
+def heads_kernel(place_ref, mine_ref, theirs_ref, gains_ref, q_ref, kv_ref):
+    ylo, core = place_ref[0], place_ref[4]
+    pair = jnp.where(core == ylo, gains_ref[0:2, :256], theirs_ref[0, 128:130, :256])
+    gains = jnp.where(core == 0, pair[:, :HD], pair[:, HD:])
+    for r in range(4):
+        rows = slice(r * 128, (r + 1) * 128)
+        raw = mine_ref[rows, :] + theirs_ref[r, :128, :]
+        query = head_norm(raw[:, :HD], gains[0:1, :]) * HD ** (-0.5)
+        q_ref[rows, :] = query.astype(BF)
+        kv_ref[0, rows, :] = head_norm(raw[:, HD : 2 * HD], gains[1:2, :]).astype(BF)
+        kv_ref[1, rows, :] = raw[:, 2 * HD :].astype(BF)
+
+
+def split_heads(place, mine, theirs, gains):
     return pl.pallas_call(
         heads_kernel,
         out_shape=(jax.ShapeDtypeStruct((512, HD), BF), jax.ShapeDtypeStruct((2, 512, HD), BF)),
-        in_specs=[pl.BlockSpec(memory_space=pltpu.VMEM)] * 3,
+        in_specs=[pl.BlockSpec(memory_space=pltpu.SMEM)] + [pl.BlockSpec(memory_space=pltpu.VMEM)] * 3,
         out_specs=(pl.BlockSpec(memory_space=pltpu.VMEM), pl.BlockSpec(memory_space=pltpu.VMEM)),
         compiler_params=pltpu.CompilerParams(vmem_limit_bytes=32 << 20),
         cost_estimate=pl.CostEstimate(flops=4_000_000, bytes_accessed=2_000_000, transcendentals=0),
-    )(mine, theirs, gains)
+    )(place, mine, theirs.reshape(4, 136, 3 * HD), gains)
 
 
 def attend_kernel(place_ref, q_ref, *refs):
@@ -205,14 +211,14 @@
             value = ref[1, pl.ds(start, 256), :]
             mixed += jnp.dot(expd.astype(BF), value, preferred_element_type=F32)
         result = (mixed / total).astype(BF)
-        for copy in range(8):
+        for copy in range(4):
             out_ref[copy, slot * 256 : (slot + 1) * 256, :] = result
 
 
 def attend(place, query, kvs):
     return pl.pallas_call(
         attend_kernel,
-        out_shape=jax.ShapeDtypeStruct((8, 512, HD), BF),
+        out_shape=jax.ShapeDtypeStruct((4, 512, HD), BF),
         in_specs=[pl.BlockSpec(memory_space=pltpu.SMEM)] + [pl.BlockSpec(memory_space=pltpu.VMEM)] * 6,
         out_specs=pl.BlockSpec(memory_space=pltpu.VMEM),
         compiler_params=pltpu.CompilerParams(vmem_limit_bytes=32 << 20),
@@ -220,28 +226,30 @@
     )(place, query, *kvs)
 
 
-def out_kernel(place_ref, heads_ref, weights_ref, out_ref):
+def out_kernel(place_ref, heads_ref, others_ref, weights_ref, out_ref):
+    first = place_ref[4] == 0
     corner = 12 + 8 * lax.rem(place_ref[2], 2)
     for slot in range(2):
         part = jnp.zeros((256, 768), F32)
         for x in range(4):
             rows = slice(slot * 256, (slot + 1) * 256)
-            pair = jnp.concatenate([heads_ref[2 * x, rows, :], heads_ref[2 * x + 1, rows, :]], axis=1)
+            held, far = heads_ref[x, rows, :], others_ref[x, rows, :]
+            pair = jnp.concatenate([jnp.where(first, held, far), jnp.where(first, far, held)], axis=1)
             block = jnp.concatenate([weights_ref[lax.rem(corner + 4 * r + x, 16)] for r in range(4)], axis=0)
             part += lax.dot_general(pair, block, (((1,), (1,)), ((), ())), preferred_element_type=F32)
         out_ref[slot] = part[:, :384].astype(BF)
         out_ref[2 + slot] = part[:, 384:].astype(BF)
 
 
-def project_out(place, heads, weights):
+def project_out(place, heads, others, weights):
     return pl.pallas_call(
         out_kernel,
         out_shape=jax.ShapeDtypeStruct((4, 256, 384), BF),
-        in_specs=[pl.BlockSpec(memory_space=pltpu.SMEM)] + [pl.BlockSpec(memory_space=pltpu.VMEM)] * 2,
+        in_specs=[pl.BlockSpec(memory_space=pltpu.SMEM)] + [pl.BlockSpec(memory_space=pltpu.VMEM)] * 3,
         out_specs=pl.BlockSpec(memory_space=pltpu.VMEM),
         compiler_params=pltpu.CompilerParams(vmem_limit_bytes=32 << 20),
         cost_estimate=pl.CostEstimate(flops=2 * 512 * 768 * 1024, bytes_accessed=3_500_000, transcendentals=0),
-    )(place, heads, weights)
+    )(place, heads, others, weights)
 
 
 def per_device(patches, ln_gain, w_query, w_key, w_value, query_gain, key_gain, w_out):
@@ -267,16 +275,14 @@
     out_weights = lax.all_gather(turned, "z", axis=0, tiled=False)
 
     normed = normalise(place, acts, ln_gain)
-    mine, theirs = multiply(place, normed, shards[0] + shards[1] + [own, last])
-    gains = jnp.stack([query_gain, key_gain])
-    gains = jnp.where(home, gains, send(gains, other_core)).reshape(2, 2, HD)
-    gains = jnp.where(core == 0, gains[:, 0], gains[:, 1])
-    query, kv = split_heads(mine, send(theirs, other_core), gains)
+    gains = jnp.pad(jnp.stack([query_gain, key_gain]), ((0, 6), (0, 128)))
+    mine, theirs = multiply(place, gains, normed, shards[0] + shards[1] + [own, last])
+    query, kv = split_heads(place, mine, send(theirs, other_core), gains)
     near = {offset: send(kv, along_z(-offset)) for offset in (-2, 2, -1, 1)}
     near[0] = kv
     attended = attend(place, query, [near[o] for o in (-2, -1, 0, 1, 2)])
-    heads = lax.all_to_all(attended, ("x", "core"), 0, 0, tiled=True)
-    parts = project_out(place, heads, out_weights)
+    heads = lax.all_to_all(attended, "x", 0, 0, tiled=True)
+    parts = project_out(place, heads, send(heads, other_core), out_weights)
     parts = lax.all_to_all(parts, ("yh", "ylo"), 0, 0, tiled=True)
     return jnp.sum(parts.astype(F32), axis=0).astype(BF)
 

time: 216 us -> 212 us (0.981)
  waiting for transfers between devices: 58.2 us -> 44.9 us
  blocking collectives: 15.5 us -> 28.7 us
  starting transfers between devices: 100 us -> 96.1 us
    all_to_all x0 -> x1, blocking collectives: none -> 13.5 us  [per_device(): heads = lax.all_to_all(attended, 'x', 0, 0, tiled=True)]
    all_to_all x1 -> x0, waiting for transfers between devices: 10.8 us -> none  [per_device(): heads = lax.all_to_all(attended, ('x', 'core'), 0, 0, tiled=True)]
    all_to_all x1 -> x0, starting transfers between devices: 6.54 us -> none  [per_device(): heads = lax.all_to_all(attended, ('x', 'core'), 0, 0, tiled=True)]
    all_gather x1, waiting for transfers between devices: 4.34 us -> 0.02 us  [per_device(): out_weights = lax.all_gather(turned, 'z', axis=0, tiled=False)]
    ppermute x24, starting transfers between devices: 93.5 us -> 96 us  [send(): return lax.ppermute(value, AXES, pairs)]
  transfers between devices with their start and end apart: 27 -> 26, of which waited for: 14 -> 13; matrix products, arithmetic and copies ran while one was open for 1% -> 1% of each run, Pallas kernels for 7% -> 7%
where the time goes in v3:
time: 212 us; the launch traced here: 211 us
  starting transfers between devices  96.1 us (45%)
  waiting for transfers between devices  44.9 us (21%)
  blocking collectives  28.7 us (14%)
  Pallas kernels  17.2 us (8%)
  between operations  13.8 us (7%)
  local copies, waits for them, and re-layouts  6.38 us (3%)
  other arithmetic  3.65 us (2%)
    ppermute x24, starting transfers between devices, send(): return lax.ppermute(value, AXES, pairs)  96 us
    ppermute x24, waiting for transfers between devices, send(): return lax.ppermute(value, AXES, pairs)  44.1 us
    all_to_all x1, blocking collectives, per_device(): parts = lax.all_to_all(parts, ('yh', 'ylo'), 0, 0, tiled=True)  15.3 us
    all_to_all x1, blocking collectives, per_device(): heads = lax.all_to_all(attended, 'x', 0, 0, tiled=True)  13.5 us
    pallas_call x1, Pallas kernels, normalise(): pl.pallas_call(norm_kernel, grid=(2, 256 // rows), out_shape=jax.ShapeDty...  6.4 us
    unnamed x20, local copies, waits for them, and re-layouts  6.29 us
    pallas_call x1, Pallas kernels, multiply(): pl.pallas_call(product_kernel, grid=(512 // rows,), out_shape=[jax.ShapeD...  6.17 us
  transfers between devices with their start and end apart: 26, of which 13 were waited for; matrix products, arithmetic and copies ran while one was open for 1% of the time, Pallas kernels for 7%

profile of v3, /device:TPU:1, one launch (start us, length us, event | category | flops | bytes accessed | tf_op | source)
XLA Modules:
  0.0 210.7 jit_solution(12372801022614111694)
XLA Ops:
  8.3 4.0 %collective-permute-start = (bf16[3,192,256]{2,1,0:T(8,128)(2,1)S(1)}, bf16[3,192,256]{2,1,0:T(8,128)(2,1)S(1)}, u32[]{:S(2)}, u32[]{:S(2)}) collective-permute-start(bf16[3,192,256]{2,1,0:T(8,128)(2,1)S(1)} %pad_maximum_fusion), channel_id=1, source_target_pairs={{0,1},{1,257},{2,3},{3,259},{4,5},{5,261},{6,7},{7,263},{8,9},{9,2... | collective-permute-start | bytes 884744 | tf_op jit(solution)/shard_map/ppermute | solution.py:37
  12.4 5.8 %collective-permute-done = bf16[3,192,256]{2,1,0:T(8,128)(2,1)S(1)} collective-permute-done((bf16[3,192,256]{2,1,0:T(8,128)(2,1)S(1)}, bf16[3,192,256]{2,1,0:T(8,128)(2,1)S(1)}, u32[]{:S(2)}, u32[]{:S(2)}) %collective-permute-start) | collective-permute-done | bytes 294944 | tf_op jit(solution)/shard_map/ppermute | solution.py:37
  19.5 6.7 %collective-permute-done.8 = bf16[3,192,256]{2,1,0:T(8,128)(2,1)S(1)} collective-permute-done((bf16[3,192,256]{2,1,0:T(8,128)(2,1)S(1)}, bf16[3,192,256]{2,1,0:T(8,128)(2,1)S(1)}, u32[]{:S(2)}, u32[]{:S(2)}) %collective-permute-start.8) | collective-permute-done | bytes 294944 | tf_op jit(solution)/shard_map/ppermute | solution.py:37
  27.2 5.7 %collective-permute-start.1 = (bf16[3,192,256]{2,1,0:T(8,128)(2,1)S(1)}, bf16[3,192,256]{2,1,0:T(8,128)(2,1)S(1)}, u32[]{:S(2)}, u32[]{:S(2)}) collective-permute-start(bf16[3,192,256]{2,1,0:T(8,128)(2,1)S(1)} %get-tuple-element.15), channel_id=1, source_target_pairs={{0,16},{1,241},{2,18},{3,243},{4,20},{5,245},{6,22},{7,247},{8,24}... | collective-permute-start | bytes 884744 | tf_op jit(solution)/shard_map/ppermute | solution.py:37
  36.6 5.0 %collective-permute-start.2 = (bf16[3,192,256]{2,1,0:T(8,128)(2,1)S(1)}, bf16[3,192,256]{2,1,0:T(8,128)(2,1)S(1)}, u32[]{:S(2)}, u32[]{:S(2)}) collective-permute-start(bf16[3,192,256]{2,1,0:T(8,128)(2,1)S(1)} %collective-permute-done.1.refs_0_), channel_id=1, source_target_pairs={{0,16},{1,241},{2,18},{3,243},{4,20},{5,245},{6,22},{7,247},{8,24}... | collective-permute-start | bytes 884744 | tf_op jit(solution)/shard_map/ppermute | solution.py:37
  41.7 3.1 %collective-permute-start.10 = (bf16[3,192,256]{2,1,0:T(8,128)(2,1)S(1)}, bf16[3,192,256]{2,1,0:T(8,128)(2,1)S(1)}, u32[]{:S(2)}, u32[]{:S(2)}) collective-permute-start(bf16[3,192,256]{2,1,0:T(8,128)(2,1)S(1)} %collective-permute-done.9.refs_7_), channel_id=1, source_target_pairs={{0,16},{1,241},{2,18},{3,243},{4,20},{5,245},{6,22},{7,247},{8,24}... | collective-permute-start | bytes 884744 | tf_op jit(solution)/shard_map/ppermute | solution.py:37
  45.3 5.0 %collective-permute-start.3 = (bf16[3,192,256]{2,1,0:T(8,128)(2,1)S(1)}, bf16[3,192,256]{2,1,0:T(8,128)(2,1)S(1)}, u32[]{:S(2)}, u32[]{:S(2)}) collective-permute-start(bf16[3,192,256]{2,1,0:T(8,128)(2,1)S(1)} %collective-permute-done.2.refs_1_), channel_id=1, source_target_pairs={{0,16},{1,241},{2,18},{3,243},{4,20},{5,245},{6,22},{7,247},{8,24}... | collective-permute-start | bytes 884744 | tf_op jit(solution)/shard_map/ppermute | solution.py:37
  50.3 3.1 %collective-permute-start.11 = (bf16[3,192,256]{2,1,0:T(8,128)(2,1)S(1)}, bf16[3,192,256]{2,1,0:T(8,128)(2,1)S(1)}, u32[]{:S(2)}, u32[]{:S(2)}) collective-permute-start(bf16[3,192,256]{2,1,0:T(8,128)(2,1)S(1)} %collective-permute-done.10.refs_8_), channel_id=1, source_target_pairs={{0,16},{1,241},{2,18},{3,243},{4,20},{5,245},{6,22},{7,247},{8,24}... | collective-permute-start | bytes 884744 | tf_op jit(solution)/shard_map/ppermute | solution.py:37
  54.0 5.0 %collective-permute-start.4 = (bf16[3,192,256]{2,1,0:T(8,128)(2,1)S(1)}, bf16[3,192,256]{2,1,0:T(8,128)(2,1)S(1)}, u32[]{:S(2)}, u32[]{:S(2)}) collective-permute-start(bf16[3,192,256]{2,1,0:T(8,128)(2,1)S(1)} %collective-permute-done.3.refs_2_), channel_id=1, source_target_pairs={{0,16},{1,241},{2,18},{3,243},{4,20},{5,245},{6,22},{7,247},{8,24}... | collective-permute-start | bytes 884744 | tf_op jit(solution)/shard_map/ppermute | solution.py:37
  62.6 5.0 %collective-permute-start.5 = (bf16[3,192,256]{2,1,0:T(8,128)(2,1)S(1)}, bf16[3,192,256]{2,1,0:T(8,128)(2,1)S(1)}, u32[]{:S(2)}, u32[]{:S(2)}) collective-permute-start(bf16[3,192,256]{2,1,0:T(8,128)(2,1)S(1)} %collective-permute-done.4.refs_3_), channel_id=1, source_target_pairs={{0,16},{1,241},{2,18},{3,243},{4,20},{5,245},{6,22},{7,247},{8,24}... | collective-permute-start | bytes 884744 | tf_op jit(solution)/shard_map/ppermute | solution.py:37
  71.3 5.0 %collective-permute-start.6 = (bf16[3,192,256]{2,1,0:T(8,128)(2,1)S(1)}, bf16[3,192,256]{2,1,0:T(8,128)(2,1)}, u32[]{:S(2)}, u32[]{:S(2)}) collective-permute-start(bf16[3,192,256]{2,1,0:T(8,128)(2,1)S(1)} %collective-permute-done.5.refs_4_), channel_id=1, source_target_pairs={{0,16},{1,241},{2,18},{3,243},{4,20},{5,245},{6,22},{7,247},{8,24}... | collective-permute-start | bytes 884744 | tf_op jit(solution)/shard_map/ppermute | solution.py:37
  80.2 4.9 %collective-permute-start.7 = (bf16[3,192,256]{2,1,0:T(8,128)(2,1)}, bf16[3,192,256]{2,1,0:T(8,128)(2,1)S(1)}, u32[]{:S(2)}, u32[]{:S(2)}) collective-permute-start(bf16[3,192,256]{2,1,0:T(8,128)(2,1)} %collective-permute-done.6.refs_5_), channel_id=1, source_target_pairs={{0,16},{1,241},{2,18},{3,243},{4,20},{5,245},{6,22},{7,247},{8,24}... | collective-permute-start | bytes 884744 | tf_op jit(solution)/shard_map/ppermute | solution.py:37
  88.3 10.1 %collective-permute-start.23 = (bf16[192,256]{1,0:T(8,128)(2,1)}, bf16[192,256]{1,0:T(8,128)(2,1)S(1)}, u32[]{:S(2)}, u32[]{:S(2)}) collective-permute-start(bf16[192,256]{1,0:T(8,128)(2,1)} %bitcast.25), channel_id=1, source_target_pairs={{0,192},{1,448},{2,194},{3,450},{4,208},{5,464},{6,210},{7,466},{8... | collective-permute-start | bytes 294920 | tf_op jit(solution)/shard_map/ppermute | solution.py:37
  108.1 6.4 %shard_map.82.normed_ref = bf16[512,3456]{1,0:T(8,128)(2,1)S(1)} custom-call(s32[5]{0:T(128)S(1)} %stack.44.place_ref, bf16[2,16,256,384]{3,2,1,0:T(8,128)(2,1)S(1)} %bitcast.14, f32[16,384]{1,0:T(8,128)S(1)} %reshape.10.gain_ref), custom_call_target="tpu_custom_call" | custom-call | flops 30000000 | bytes 10000000 | tf_op jit(solution)/shard_map/pallas_call | solution.py:91
  114.5 6.2 %shard_map.83 = (f32[512,384]{1,0:T(8,128)S(1)}, f32[544,384]{1,0:T(8,128)S(1)}) custom-call(s32[5]{0:T(128)S(1)} %stack.44.place_ref, f32[8,384]{1,0:T(8,128)S(1)} %select_maximum_fusion.gains_ref, bf16[512,3456]{1,0:T(8,128)(2,1)S(1)} %shard_map.82.normed_ref, bf16[3,192,256]{2,1,0:T(8,128)(2,1)S(1)} %collective-permute-done.1.refs_0_, ...), custom_call_target="tpu_custom_call" | custom-call | flops 2717908992 | bytes 10000000 | tf_op jit(solution)/shard_map/pallas_call | solution.py:149
  126.9 4.0 %collective-permute-start.18 = (bf16[2,512,128]{2,1,0:T(8,128)(2,1)S(1)}, bf16[2,512,128]{2,1,0:T(8,128)(2,1)S(1)}, u32[]{:S(2)}, u32[]{:S(2)}) collective-permute-start(bf16[2,512,128]{2,1,0:T(8,128)(2,1)S(1)} %get-tuple-element.12.refs_2_), channel_id=1, source_target_pairs={{0,32},{1,33},{2,34},{3,35},{4,36},{5,37},{6,38},{7,39},{8,40},{9,... | collective-permute-start | bytes 786440 | tf_op jit(solution)/shard_map/ppermute | solution.py:37
  132.9 4.6 %collective-permute-start.20 = (bf16[2,512,128]{2,1,0:T(8,128)(2,1)S(1)}, bf16[2,512,128]{2,1,0:T(8,128)(2,1)S(1)}, u32[]{:S(2)}, u32[]{:S(2)}) collective-permute-start(bf16[2,512,128]{2,1,0:T(8,128)(2,1)S(1)} %get-tuple-element.12.refs_2_), channel_id=1, source_target_pairs={{0,240},{1,241},{2,242},{3,243},{4,244},{5,245},{6,246},{7,247},{8... | collective-permute-start | bytes 786440 | tf_op jit(solution)/shard_map/ppermute | solution.py:37
  137.4 3.1 %collective-permute-start.21 = (bf16[2,512,128]{2,1,0:T(8,128)(2,1)S(1)}, bf16[2,512,128]{2,1,0:T(8,128)(2,1)S(1)}, u32[]{:S(2)}, u32[]{:S(2)}) collective-permute-start(bf16[2,512,128]{2,1,0:T(8,128)(2,1)S(1)} %get-tuple-element.12.refs_2_), channel_id=1, source_target_pairs={{0,224},{1,225},{2,226},{3,227},{4,228},{5,229},{6,230},{7,231},{8... | collective-permute-start | bytes 786440 | tf_op jit(solution)/shard_map/ppermute | solution.py:37
  140.6 6.3 %collective-permute-done.18.refs_0_ = bf16[2,512,128]{2,1,0:T(8,128)(2,1)S(1)} collective-permute-done((bf16[2,512,128]{2,1,0:T(8,128)(2,1)S(1)}, bf16[2,512,128]{2,1,0:T(8,128)(2,1)S(1)}, u32[]{:S(2)}, u32[]{:S(2)}) %collective-permute-start.18) | collective-permute-done | bytes 262176 | tf_op jit(solution)/shard_map/ppermute | solution.py:37
  146.9 8.8 %collective-permute-done.19.refs_1_ = bf16[2,512,128]{2,1,0:T(8,128)(2,1)S(1)} collective-permute-done((bf16[2,512,128]{2,1,0:T(8,128)(2,1)S(1)}, bf16[2,512,128]{2,1,0:T(8,128)(2,1)S(1)}, u32[]{:S(2)}, u32[]{:S(2)}) %collective-permute-start.19) | collective-permute-done | bytes 262176 | tf_op jit(solution)/shard_map/ppermute | solution.py:37
  155.7 7.7 %collective-permute-done.21.refs_4_ = bf16[2,512,128]{2,1,0:T(8,128)(2,1)S(1)} collective-permute-done((bf16[2,512,128]{2,1,0:T(8,128)(2,1)S(1)}, bf16[2,512,128]{2,1,0:T(8,128)(2,1)S(1)}, u32[]{:S(2)}, u32[]{:S(2)}) %collective-permute-start.21) | collective-permute-done | bytes 262176 | tf_op jit(solution)/shard_map/ppermute | solution.py:37
  165.3 13.5 %all_to_all.10.heads_ref = bf16[4,512,128]{2,1,0:T(8,128)(2,1)S(1)} all-to-all(bf16[4,512,128]{2,1,0:T(8,128)(2,1)S(1)} %shard_map.85), channel_id=1, replica_groups=mesh['ylo'=2,'z'=16,'x'=4,'yh'=2,'core'=2] {'x'}, dimensions={0} | all-to-all | bytes 1048576 | tf_op jit(solution)/shard_map/all_to_all | solution.py:284
  178.8 4.4 %collective-permute-start.22 = (bf16[4,512,128]{2,1,0:T(8,128)(2,1)S(1)}, bf16[4,512,128]{2,1,0:T(8,128)(2,1)S(1)}, u32[]{:S(2)}, u32[]{:S(2)}) collective-permute-start(bf16[4,512,128]{2,1,0:T(8,128)(2,1)S(1)} %all_to_all.10.heads_ref), channel_id=1, source_target_pairs={{0,1},{1,0},{2,3},{3,2},{4,5},{5,4},{6,7},{7,6},{8,9},{9,8},{10,11... | collective-permute-start | bytes 1572872 | tf_op jit(solution)/shard_map/ppermute | solution.py:37
  187.8 15.3 %all_to_all.11 = bf16[4,256,384]{2,1,0:T(8,128)(2,1)S(1)} all-to-all(bf16[4,256,384]{2,1,0:T(8,128)(2,1)S(1)} %shard_map.86), channel_id=1, replica_groups=mesh['ylo'=2,'z'=16,'x'=4,'yh'=2,'core'=2] {'yh','ylo'}, dimensions={0} | all-to-all | bytes 1572864 | tf_op jit(solution)/shard_map/all_to_all | solution.py:286
  (64 shorter events, 47.9 us)
Async XLA Ops:
  6.5 98.7 %all-gather.5.cloned.1.call-start = ((), (), s32[]{:S(2)}) async-start(), calls=%async_computation.2 | async-start | bytes 6488064 | tf_op jit(solution)/shard_map/all_gather | solution.py:259
  7.3 176.0 %all-gather.7.cloned.1.call-start = ((), (), s32[]{:S(2)}) async-start(), calls=%async_computation.3 | async-start | bytes 1671168 | tf_op jit(solution)/shard_map/all_gather | solution.py:275
  8.3 9.9 %collective-permute-start = (bf16[3,192,256]{2,1,0:T(8,128)(2,1)S(1)}, bf16[3,192,256]{2,1,0:T(8,128)(2,1)S(1)}, u32[]{:S(2)}, u32[]{:S(2)}) collective-permute-start(bf16[3,192,256]{2,1,0:T(8,128)(2,1)S(1)} %pad_maximum_fusion), channel_id=1, source_target_pairs={{0,1},{1,257},{2,3},{3,259},{4,5},{5,261},{6,7},{7,263},{8,9},{9,2... | collective-permute-start | bytes 884744 | tf_op jit(solution)/shard_map/ppermute | solution.py:37
  18.2 8.0 %collective-permute-start.8 = (bf16[3,192,256]{2,1,0:T(8,128)(2,1)S(1)}, bf16[3,192,256]{2,1,0:T(8,128)(2,1)S(1)}, u32[]{:S(2)}, u32[]{:S(2)}) collective-permute-start(bf16[3,192,256]{2,1,0:T(8,128)(2,1)S(1)} %collective-permute-done), channel_id=1, source_target_pairs={{0,1},{2,3},{4,5},{6,7},{8,9},{10,11},{12,13},{14,15},{16,17},{18,... | collective-permute-start | bytes 884744 | tf_op jit(solution)/shard_map/ppermute | solution.py:37
  27.2 9.4 %collective-permute-start.1 = (bf16[3,192,256]{2,1,0:T(8,128)(2,1)S(1)}, bf16[3,192,256]{2,1,0:T(8,128)(2,1)S(1)}, u32[]{:S(2)}, u32[]{:S(2)}) collective-permute-start(bf16[3,192,256]{2,1,0:T(8,128)(2,1)S(1)} %get-tuple-element.15), channel_id=1, source_target_pairs={{0,16},{1,241},{2,18},{3,243},{4,20},{5,245},{6,22},{7,247},{8,24}... | collective-permute-start | bytes 884744 | tf_op jit(solution)/shard_map/ppermute | solution.py:37
  33.0 8.7 %collective-permute-start.9 = (bf16[3,192,256]{2,1,0:T(8,128)(2,1)S(1)}, bf16[3,192,256]{2,1,0:T(8,128)(2,1)S(1)}, u32[]{:S(2)}, u32[]{:S(2)}) collective-permute-start(bf16[3,192,256]{2,1,0:T(8,128)(2,1)S(1)} %get-tuple-element.14), channel_id=1, source_target_pairs={{0,16},{1,241},{2,18},{3,243},{4,20},{5,245},{6,22},{7,247},{8,24}... | collective-permute-start | bytes 884744 | tf_op jit(solution)/shard_map/ppermute | solution.py:37
  36.6 8.7 %collective-permute-start.2 = (bf16[3,192,256]{2,1,0:T(8,128)(2,1)S(1)}, bf16[3,192,256]{2,1,0:T(8,128)(2,1)S(1)}, u32[]{:S(2)}, u32[]{:S(2)}) collective-permute-start(bf16[3,192,256]{2,1,0:T(8,128)(2,1)S(1)} %collective-permute-done.1.refs_0_), channel_id=1, source_target_pairs={{0,16},{1,241},{2,18},{3,243},{4,20},{5,245},{6,22},{7,247},{8,24}... | collective-permute-start | bytes 884744 | tf_op jit(solution)/shard_map/ppermute | solution.py:37
  41.7 8.7 %collective-permute-start.10 = (bf16[3,192,256]{2,1,0:T(8,128)(2,1)S(1)}, bf16[3,192,256]{2,1,0:T(8,128)(2,1)S(1)}, u32[]{:S(2)}, u32[]{:S(2)}) collective-permute-start(bf16[3,192,256]{2,1,0:T(8,128)(2,1)S(1)} %collective-permute-done.9.refs_7_), channel_id=1, source_target_pairs={{0,16},{1,241},{2,18},{3,243},{4,20},{5,245},{6,22},{7,247},{8,24}... | collective-permute-start | bytes 884744 | tf_op jit(solution)/shard_map/ppermute | solution.py:37
  45.3 8.7 %collective-permute-start.3 = (bf16[3,192,256]{2,1,0:T(8,128)(2,1)S(1)}, bf16[3,192,256]{2,1,0:T(8,128)(2,1)S(1)}, u32[]{:S(2)}, u32[]{:S(2)}) collective-permute-start(bf16[3,192,256]{2,1,0:T(8,128)(2,1)S(1)} %collective-permute-done.2.refs_1_), channel_id=1, source_target_pairs={{0,16},{1,241},{2,18},{3,243},{4,20},{5,245},{6,22},{7,247},{8,24}... | collective-permute-start | bytes 884744 | tf_op jit(solution)/shard_map/ppermute | solution.py:37
  50.3 8.7 %collective-permute-start.11 = (bf16[3,192,256]{2,1,0:T(8,128)(2,1)S(1)}, bf16[3,192,256]{2,1,0:T(8,128)(2,1)S(1)}, u32[]{:S(2)}, u32[]{:S(2)}) collective-permute-start(bf16[3,192,256]{2,1,0:T(8,128)(2,1)S(1)} %collective-permute-done.10.refs_8_), channel_id=1, source_target_pairs={{0,16},{1,241},{2,18},{3,243},{4,20},{5,245},{6,22},{7,247},{8,24}... | collective-permute-start | bytes 884744 | tf_op jit(solution)/shard_map/ppermute | solution.py:37
  54.0 8.7 %collective-permute-start.4 = (bf16[3,192,256]{2,1,0:T(8,128)(2,1)S(1)}, bf16[3,192,256]{2,1,0:T(8,128)(2,1)S(1)}, u32[]{:S(2)}, u32[]{:S(2)}) collective-permute-start(bf16[3,192,256]{2,1,0:T(8,128)(2,1)S(1)} %collective-permute-done.3.refs_2_), channel_id=1, source_target_pairs={{0,16},{1,241},{2,18},{3,243},{4,20},{5,245},{6,22},{7,247},{8,24}... | collective-permute-start | bytes 884744 | tf_op jit(solution)/shard_map/ppermute | solution.py:37
  59.0 8.7 %collective-permute-start.12 = (bf16[3,192,256]{2,1,0:T(8,128)(2,1)S(1)}, bf16[3,192,256]{2,1,0:T(8,128)(2,1)S(1)}, u32[]{:S(2)}, u32[]{:S(2)}) collective-permute-start(bf16[3,192,256]{2,1,0:T(8,128)(2,1)S(1)} %collective-permute-done.11.refs_9_), channel_id=1, source_target_pairs={{0,16},{1,241},{2,18},{3,243},{4,20},{5,245},{6,22},{7,247},{8,24}... | collective-permute-start | bytes 884744 | tf_op jit(solution)/shard_map/ppermute | solution.py:37
  62.6 8.7 %collective-permute-start.5 = (bf16[3,192,256]{2,1,0:T(8,128)(2,1)S(1)}, bf16[3,192,256]{2,1,0:T(8,128)(2,1)S(1)}, u32[]{:S(2)}, u32[]{:S(2)}) collective-permute-start(bf16[3,192,256]{2,1,0:T(8,128)(2,1)S(1)} %collective-permute-done.4.refs_3_), channel_id=1, source_target_pairs={{0,16},{1,241},{2,18},{3,243},{4,20},{5,245},{6,22},{7,247},{8,24}... | collective-permute-start | bytes 884744 | tf_op jit(solution)/shard_map/ppermute | solution.py:37
  67.7 9.4 %collective-permute-start.13 = (bf16[3,192,256]{2,1,0:T(8,128)(2,1)S(1)}, bf16[3,192,256]{2,1,0:T(8,128)(2,1)S(1)}, u32[]{:S(2)}, u32[]{:S(2)}) collective-permute-start(bf16[3,192,256]{2,1,0:T(8,128)(2,1)S(1)} %collective-permute-done.12.refs_10_), channel_id=1, source_target_pairs={{0,16},{1,241},{2,18},{3,243},{4,20},{5,245},{6,22},{7,247},{8,24}... | collective-permute-start | bytes 884744 | tf_op jit(solution)/shard_map/ppermute | solution.py:37
  71.3 8.9 %collective-permute-start.6 = (bf16[3,192,256]{2,1,0:T(8,128)(2,1)S(1)}, bf16[3,192,256]{2,1,0:T(8,128)(2,1)}, u32[]{:S(2)}, u32[]{:S(2)}) collective-permute-start(bf16[3,192,256]{2,1,0:T(8,128)(2,1)S(1)} %collective-permute-done.5.refs_4_), channel_id=1, source_target_pairs={{0,16},{1,241},{2,18},{3,243},{4,20},{5,245},{6,22},{7,247},{8,24}... | collective-permute-start | bytes 884744 | tf_op jit(solution)/shard_map/ppermute | solution.py:37
  77.1 8.0 %collective-permute-start.14 = (bf16[3,192,256]{2,1,0:T(8,128)(2,1)S(1)}, bf16[3,192,256]{2,1,0:T(8,128)(2,1)}, u32[]{:S(2)}, u32[]{:S(2)}) collective-permute-start(bf16[3,192,256]{2,1,0:T(8,128)(2,1)S(1)} %collective-permute-done.13.refs_11_), channel_id=1, source_target_pairs={{0,16},{1,241},{2,18},{3,243},{4,20},{5,245},{6,22},{7,247},{8,24}... | collective-permute-start | bytes 884744 | tf_op jit(solution)/shard_map/ppermute | solution.py:37
  80.2 21.2 %collective-permute-start.7 = (bf16[3,192,256]{2,1,0:T(8,128)(2,1)}, bf16[3,192,256]{2,1,0:T(8,128)(2,1)S(1)}, u32[]{:S(2)}, u32[]{:S(2)}) collective-permute-start(bf16[3,192,256]{2,1,0:T(8,128)(2,1)} %collective-permute-done.6.refs_5_), channel_id=1, source_target_pairs={{0,16},{1,241},{2,18},{3,243},{4,20},{5,245},{6,22},{7,247},{8,24}... | collective-permute-start | bytes 884744 | tf_op jit(solution)/shard_map/ppermute | solution.py:37
  85.1 16.3 %collective-permute-start.15 = (bf16[3,192,256]{2,1,0:T(8,128)(2,1)}, bf16[3,192,256]{2,1,0:T(8,128)(2,1)S(1)}, u32[]{:S(2)}, u32[]{:S(2)}) collective-permute-start(bf16[3,192,256]{2,1,0:T(8,128)(2,1)} %collective-permute-done.14.refs_12_), channel_id=1, source_target_pairs={{0,16},{1,241},{2,18},{3,243},{4,20},{5,245},{6,22},{7,247},{8,24}... | collective-permute-start | bytes 884744 | tf_op jit(solution)/shard_map/ppermute | solution.py:37
  88.3 12.5 %collective-permute-start.23 = (bf16[192,256]{1,0:T(8,128)(2,1)}, bf16[192,256]{1,0:T(8,128)(2,1)S(1)}, u32[]{:S(2)}, u32[]{:S(2)}) collective-permute-start(bf16[192,256]{1,0:T(8,128)(2,1)} %bitcast.25), channel_id=1, source_target_pairs={{0,192},{1,448},{2,194},{3,450},{4,208},{5,464},{6,210},{7,466},{8... | collective-permute-start | bytes 294920 | tf_op jit(solution)/shard_map/ppermute | solution.py:37
  102.2 12.3 %collective-permute-start.16 = (bf16[3,192,256]{2,1,0:T(8,128)(2,1)}, bf16[3,192,256]{2,1,0:T(8,128)(2,1)}, u32[]{:S(2)}, u32[]{:S(2)}) collective-permute-start(bf16[3,192,256]{2,1,0:T(8,128)(2,1)} %broadcast_select_fusion), channel_id=1, source_target_pairs={{0,16},{1,241},{2,18},{3,243},{4,20},{5,245},{6,22},{7,247},{8,24}... | collective-permute-start | bytes 884744 | tf_op jit(solution)/shard_map/ppermute | solution.py:37
  126.9 20.0 %collective-permute-start.18 = (bf16[2,512,128]{2,1,0:T(8,128)(2,1)S(1)}, bf16[2,512,128]{2,1,0:T(8,128)(2,1)S(1)}, u32[]{:S(2)}, u32[]{:S(2)}) collective-permute-start(bf16[2,512,128]{2,1,0:T(8,128)(2,1)S(1)} %get-tuple-element.12.refs_2_), channel_id=1, source_target_pairs={{0,32},{1,33},{2,34},{3,35},{4,36},{5,37},{6,38},{7,39},{8,40},{9,... | collective-permute-start | bytes 786440 | tf_op jit(solution)/shard_map/ppermute | solution.py:37
  130.9 24.8 %collective-permute-start.19 = (bf16[2,512,128]{2,1,0:T(8,128)(2,1)S(1)}, bf16[2,512,128]{2,1,0:T(8,128)(2,1)S(1)}, u32[]{:S(2)}, u32[]{:S(2)}) collective-permute-start(bf16[2,512,128]{2,1,0:T(8,128)(2,1)S(1)} %get-tuple-element.12.refs_2_), channel_id=1, source_target_pairs={{0,16},{1,17},{2,18},{3,19},{4,20},{5,21},{6,22},{7,23},{8,24},{9,... | collective-permute-start | bytes 786440 | tf_op jit(solution)/shard_map/ppermute | solution.py:37
  132.9 22.9 %collective-permute-start.20 = (bf16[2,512,128]{2,1,0:T(8,128)(2,1)S(1)}, bf16[2,512,128]{2,1,0:T(8,128)(2,1)S(1)}, u32[]{:S(2)}, u32[]{:S(2)}) collective-permute-start(bf16[2,512,128]{2,1,0:T(8,128)(2,1)S(1)} %get-tuple-element.12.refs_2_), channel_id=1, source_target_pairs={{0,240},{1,241},{2,242},{3,243},{4,244},{5,245},{6,246},{7,247},{8... | collective-permute-start | bytes 786440 | tf_op jit(solution)/shard_map/ppermute | solution.py:37
  137.4 26.0 %collective-permute-start.21 = (bf16[2,512,128]{2,1,0:T(8,128)(2,1)S(1)}, bf16[2,512,128]{2,1,0:T(8,128)(2,1)S(1)}, u32[]{:S(2)}, u32[]{:S(2)}) collective-permute-start(bf16[2,512,128]{2,1,0:T(8,128)(2,1)S(1)} %get-tuple-element.12.refs_2_), channel_id=1, source_target_pairs={{0,224},{1,225},{2,226},{3,227},{4,228},{5,229},{6,230},{7,231},{8... | collective-permute-start | bytes 786440 | tf_op jit(solution)/shard_map/ppermute | solution.py:37
  (12 other events, 326.1 us)
Sparse Core Ops, SparseCore 0:
  9.5 76.7 all-gather.4
  101.5 75.7 all-gather.6

commit v4 on v3

--- a/solution.py
+++ b/solution.py
@@ -98,7 +98,7 @@
             pl.BlockSpec((16, 384), lambda s, r: (0, 0)),
         ],
         out_specs=pl.BlockSpec((rows, WINDOW), lambda s, r: (s * (256 // rows) + r, 0)),
-        compiler_params=pltpu.CompilerParams(vmem_limit_bytes=32 << 20),
+        compiler_params=pltpu.CompilerParams(vmem_limit_bytes=60 << 20),
         cost_estimate=pl.CostEstimate(flops=30_000_000, bytes_accessed=10_000_000, transcendentals=0),
     )(place, acts.reshape(2, 16, 256, 384), gain.reshape(16, 384))
 

time: 212 us -> 217 us (1.024)
  Pallas kernels: 17.2 us -> 20.3 us
  blocking collectives: 28.7 us -> 31.1 us
    pallas_call x1, Pallas kernels: 6.4 us -> 9.34 us  [normalise(): pl.pallas_call(norm_kernel, grid=(2, 256 // rows), out_shape=jax.ShapeDty...]
    all_to_all x1, blocking collectives: 13.5 us -> 15.7 us  [per_device(): heads = lax.all_to_all(attended, 'x', 0, 0, tiled=True)]
    unnamed x20 -> x22, local copies, waits for them, and re-layouts: 6.29 us -> 6.46 us
  transfers between devices with their start and end apart: 26 -> 26, of which waited for: 13 -> 13; matrix products, arithmetic and copies ran while one was open for 1% -> 2% of each run, Pallas kernels for 7% -> 9%
where the time goes in v4:
time: 217 us; the launch traced here: 216 us
  starting transfers between devices  96 us (44%)
  waiting for transfers between devices  43.1 us (20%)
  blocking collectives  31.1 us (14%)
  Pallas kernels  20.3 us (9%)
  between operations  13.8 us (6%)
  local copies, waits for them, and re-layouts  7.67 us (4%)
  other arithmetic  3.65 us (2%)
    ppermute x24, starting transfers between devices, send(): return lax.ppermute(value, AXES, pairs)  95.9 us
    ppermute x24, waiting for transfers between devices, send(): return lax.ppermute(value, AXES, pairs)  42.3 us
    all_to_all x1, blocking collectives, per_device(): heads = lax.all_to_all(attended, 'x', 0, 0, tiled=True)  15.7 us
    all_to_all x1, blocking collectives, per_device(): parts = lax.all_to_all(parts, ('yh', 'ylo'), 0, 0, tiled=True)  15.4 us
    pallas_call x1, Pallas kernels, normalise(): pl.pallas_call(norm_kernel, grid=(2, 256 // rows), out_shape=jax.ShapeDty...  9.34 us
    unnamed x22, local copies, waits for them, and re-layouts  6.46 us
    pallas_call x1, Pallas kernels, multiply(): pl.pallas_call(product_kernel, grid=(512 // rows,), out_shape=[jax.ShapeD...  6.32 us
  transfers between devices with their start and end apart: 26, of which 13 were waited for; matrix products, arithmetic and copies ran while one was open for 2% of the time, Pallas kernels for 9%

profile of v4, /device:TPU:1, one launch (start us, length us, event | category | flops | bytes accessed | tf_op | source)
XLA Modules:
  0.0 215.6 jit_solution(1511064925492412883)
XLA Ops:
  8.3 4.0 %collective-permute-start = (bf16[3,192,256]{2,1,0:T(8,128)(2,1)S(1)}, bf16[3,192,256]{2,1,0:T(8,128)(2,1)S(1)}, u32[]{:S(2)}, u32[]{:S(2)}) collective-permute-start(bf16[3,192,256]{2,1,0:T(8,128)(2,1)S(1)} %pad_maximum_fusion), channel_id=1, source_target_pairs={{0,1},{1,257},{2,3},{3,259},{4,5},{5,261},{6,7},{7,263},{8,9},{9,2... | collective-permute-start | bytes 884744 | tf_op jit(solution)/shard_map/ppermute | solution.py:37
  12.4 5.8 %collective-permute-done = bf16[3,192,256]{2,1,0:T(8,128)(2,1)S(1)} collective-permute-done((bf16[3,192,256]{2,1,0:T(8,128)(2,1)S(1)}, bf16[3,192,256]{2,1,0:T(8,128)(2,1)S(1)}, u32[]{:S(2)}, u32[]{:S(2)}) %collective-permute-start) | collective-permute-done | bytes 294944 | tf_op jit(solution)/shard_map/ppermute | solution.py:37
  19.5 6.7 %collective-permute-done.8 = bf16[3,192,256]{2,1,0:T(8,128)(2,1)S(1)} collective-permute-done((bf16[3,192,256]{2,1,0:T(8,128)(2,1)S(1)}, bf16[3,192,256]{2,1,0:T(8,128)(2,1)S(1)}, u32[]{:S(2)}, u32[]{:S(2)}) %collective-permute-start.8) | collective-permute-done | bytes 294944 | tf_op jit(solution)/shard_map/ppermute | solution.py:37
  27.2 5.7 %collective-permute-start.1 = (bf16[3,192,256]{2,1,0:T(8,128)(2,1)S(1)}, bf16[3,192,256]{2,1,0:T(8,128)(2,1)S(1)}, u32[]{:S(2)}, u32[]{:S(2)}) collective-permute-start(bf16[3,192,256]{2,1,0:T(8,128)(2,1)S(1)} %get-tuple-element.15), channel_id=1, source_target_pairs={{0,16},{1,241},{2,18},{3,243},{4,20},{5,245},{6,22},{7,247},{8,24}... | collective-permute-start | bytes 884744 | tf_op jit(solution)/shard_map/ppermute | solution.py:37
  36.6 5.0 %collective-permute-start.2 = (bf16[3,192,256]{2,1,0:T(8,128)(2,1)S(1)}, bf16[3,192,256]{2,1,0:T(8,128)(2,1)S(1)}, u32[]{:S(2)}, u32[]{:S(2)}) collective-permute-start(bf16[3,192,256]{2,1,0:T(8,128)(2,1)S(1)} %collective-permute-done.1.refs_0_), channel_id=1, source_target_pairs={{0,16},{1,241},{2,18},{3,243},{4,20},{5,245},{6,22},{7,247},{8,24}... | collective-permute-start | bytes 884744 | tf_op jit(solution)/shard_map/ppermute | solution.py:37
  41.7 3.1 %collective-permute-start.10 = (bf16[3,192,256]{2,1,0:T(8,128)(2,1)S(1)}, bf16[3,192,256]{2,1,0:T(8,128)(2,1)S(1)}, u32[]{:S(2)}, u32[]{:S(2)}) collective-permute-start(bf16[3,192,256]{2,1,0:T(8,128)(2,1)S(1)} %collective-permute-done.9.refs_7_), channel_id=1, source_target_pairs={{0,16},{1,241},{2,18},{3,243},{4,20},{5,245},{6,22},{7,247},{8,24}... | collective-permute-start | bytes 884744 | tf_op jit(solution)/shard_map/ppermute | solution.py:37
  45.3 5.0 %collective-permute-start.3 = (bf16[3,192,256]{2,1,0:T(8,128)(2,1)S(1)}, bf16[3,192,256]{2,1,0:T(8,128)(2,1)S(1)}, u32[]{:S(2)}, u32[]{:S(2)}) collective-permute-start(bf16[3,192,256]{2,1,0:T(8,128)(2,1)S(1)} %collective-permute-done.2.refs_1_), channel_id=1, source_target_pairs={{0,16},{1,241},{2,18},{3,243},{4,20},{5,245},{6,22},{7,247},{8,24}... | collective-permute-start | bytes 884744 | tf_op jit(solution)/shard_map/ppermute | solution.py:37
  50.3 3.1 %collective-permute-start.11 = (bf16[3,192,256]{2,1,0:T(8,128)(2,1)S(1)}, bf16[3,192,256]{2,1,0:T(8,128)(2,1)S(1)}, u32[]{:S(2)}, u32[]{:S(2)}) collective-permute-start(bf16[3,192,256]{2,1,0:T(8,128)(2,1)S(1)} %collective-permute-done.10.refs_8_), channel_id=1, source_target_pairs={{0,16},{1,241},{2,18},{3,243},{4,20},{5,245},{6,22},{7,247},{8,24}... | collective-permute-start | bytes 884744 | tf_op jit(solution)/shard_map/ppermute | solution.py:37
  54.0 5.0 %collective-permute-start.4 = (bf16[3,192,256]{2,1,0:T(8,128)(2,1)S(1)}, bf16[3,192,256]{2,1,0:T(8,128)(2,1)S(1)}, u32[]{:S(2)}, u32[]{:S(2)}) collective-permute-start(bf16[3,192,256]{2,1,0:T(8,128)(2,1)S(1)} %collective-permute-done.3.refs_2_), channel_id=1, source_target_pairs={{0,16},{1,241},{2,18},{3,243},{4,20},{5,245},{6,22},{7,247},{8,24}... | collective-permute-start | bytes 884744 | tf_op jit(solution)/shard_map/ppermute | solution.py:37
  59.0 3.1 %collective-permute-start.12 = (bf16[3,192,256]{2,1,0:T(8,128)(2,1)S(1)}, bf16[3,192,256]{2,1,0:T(8,128)(2,1)S(1)}, u32[]{:S(2)}, u32[]{:S(2)}) collective-permute-start(bf16[3,192,256]{2,1,0:T(8,128)(2,1)S(1)} %collective-permute-done.11.refs_9_), channel_id=1, source_target_pairs={{0,16},{1,241},{2,18},{3,243},{4,20},{5,245},{6,22},{7,247},{8,24}... | collective-permute-start | bytes 884744 | tf_op jit(solution)/shard_map/ppermute | solution.py:37
  62.6 5.0 %collective-permute-start.5 = (bf16[3,192,256]{2,1,0:T(8,128)(2,1)S(1)}, bf16[3,192,256]{2,1,0:T(8,128)(2,1)S(1)}, u32[]{:S(2)}, u32[]{:S(2)}) collective-permute-start(bf16[3,192,256]{2,1,0:T(8,128)(2,1)S(1)} %collective-permute-done.4.refs_3_), channel_id=1, source_target_pairs={{0,16},{1,241},{2,18},{3,243},{4,20},{5,245},{6,22},{7,247},{8,24}... | collective-permute-start | bytes 884744 | tf_op jit(solution)/shard_map/ppermute | solution.py:37
  71.3 5.0 %collective-permute-start.6 = (bf16[3,192,256]{2,1,0:T(8,128)(2,1)S(1)}, bf16[3,192,256]{2,1,0:T(8,128)(2,1)}, u32[]{:S(2)}, u32[]{:S(2)}) collective-permute-start(bf16[3,192,256]{2,1,0:T(8,128)(2,1)S(1)} %collective-permute-done.5.refs_4_), channel_id=1, source_target_pairs={{0,16},{1,241},{2,18},{3,243},{4,20},{5,245},{6,22},{7,247},{8,24}... | collective-permute-start | bytes 884744 | tf_op jit(solution)/shard_map/ppermute | solution.py:37
  80.2 4.9 %collective-permute-start.7 = (bf16[3,192,256]{2,1,0:T(8,128)(2,1)}, bf16[3,192,256]{2,1,0:T(8,128)(2,1)S(1)}, u32[]{:S(2)}, u32[]{:S(2)}) collective-permute-start(bf16[3,192,256]{2,1,0:T(8,128)(2,1)} %collective-permute-done.6.refs_5_), channel_id=1, source_target_pairs={{0,16},{1,241},{2,18},{3,243},{4,20},{5,245},{6,22},{7,247},{8,24}... | collective-permute-start | bytes 884744 | tf_op jit(solution)/shard_map/ppermute | solution.py:37
  88.3 10.1 %collective-permute-start.23 = (bf16[192,256]{1,0:T(8,128)(2,1)}, bf16[192,256]{1,0:T(8,128)(2,1)S(1)}, u32[]{:S(2)}, u32[]{:S(2)}) collective-permute-start(bf16[192,256]{1,0:T(8,128)(2,1)} %bitcast.25), channel_id=1, source_target_pairs={{0,192},{1,448},{2,194},{3,450},{4,208},{5,464},{6,210},{7,466},{8... | collective-permute-start | bytes 294920 | tf_op jit(solution)/shard_map/ppermute | solution.py:37
  106.4 9.3 %shard_map.82.normed_ref = bf16[512,3456]{1,0:T(8,128)(2,1)} custom-call(s32[5]{0:T(128)} %stack.44.place_ref, bf16[2,16,256,384]{3,2,1,0:T(8,128)(2,1)} %bitcast.16, f32[16,384]{1,0:T(8,128)} %reshape.10.gain_ref), custom_call_target="tpu_custom_call" | custom-call | flops 30000000 | bytes 10000000 | tf_op jit(solution)/shard_map/pallas_call | solution.py:91
  118.7 6.3 %shard_map.83 = (f32[512,384]{1,0:T(8,128)S(1)}, f32[544,384]{1,0:T(8,128)S(1)}) custom-call(s32[5]{0:T(128)S(1)} %copy-done.2, f32[8,384]{1,0:T(8,128)S(1)} %select_maximum_fusion.gains_ref, bf16[512,3456]{1,0:T(8,128)(2,1)S(1)} %copy-done, bf16[3,192,256]{2,1,0:T(8,128)(2,1)S(1)} %collective-permute-done.1.refs_0_, ...), custom_call_target="tpu_custom_call" | custom-call | flops 2717908992 | bytes 10000000 | tf_op jit(solution)/shard_map/pallas_call | solution.py:149
  131.3 4.0 %collective-permute-start.18 = (bf16[2,512,128]{2,1,0:T(8,128)(2,1)S(1)}, bf16[2,512,128]{2,1,0:T(8,128)(2,1)S(1)}, u32[]{:S(2)}, u32[]{:S(2)}) collective-permute-start(bf16[2,512,128]{2,1,0:T(8,128)(2,1)S(1)} %get-tuple-element.12.refs_2_), channel_id=1, source_target_pairs={{0,32},{1,33},{2,34},{3,35},{4,36},{5,37},{6,38},{7,39},{8,40},{9,... | collective-permute-start | bytes 786440 | tf_op jit(solution)/shard_map/ppermute | solution.py:37
  137.2 4.6 %collective-permute-start.20 = (bf16[2,512,128]{2,1,0:T(8,128)(2,1)S(1)}, bf16[2,512,128]{2,1,0:T(8,128)(2,1)S(1)}, u32[]{:S(2)}, u32[]{:S(2)}) collective-permute-start(bf16[2,512,128]{2,1,0:T(8,128)(2,1)S(1)} %get-tuple-element.12.refs_2_), channel_id=1, source_target_pairs={{0,240},{1,241},{2,242},{3,243},{4,244},{5,245},{6,246},{7,247},{8... | collective-permute-start | bytes 786440 | tf_op jit(solution)/shard_map/ppermute | solution.py:37
  144.9 7.3 %collective-permute-done.18.refs_0_ = bf16[2,512,128]{2,1,0:T(8,128)(2,1)S(1)} collective-permute-done((bf16[2,512,128]{2,1,0:T(8,128)(2,1)S(1)}, bf16[2,512,128]{2,1,0:T(8,128)(2,1)S(1)}, u32[]{:S(2)}, u32[]{:S(2)}) %collective-permute-start.18) | collective-permute-done | bytes 262176 | tf_op jit(solution)/shard_map/ppermute | solution.py:37
  152.3 7.3 %collective-permute-done.19.refs_1_ = bf16[2,512,128]{2,1,0:T(8,128)(2,1)S(1)} collective-permute-done((bf16[2,512,128]{2,1,0:T(8,128)(2,1)S(1)}, bf16[2,512,128]{2,1,0:T(8,128)(2,1)S(1)}, u32[]{:S(2)}, u32[]{:S(2)}) %collective-permute-start.19) | collective-permute-done | bytes 262176 | tf_op jit(solution)/shard_map/ppermute | solution.py:37
  159.6 6.5 %collective-permute-done.21.refs_4_ = bf16[2,512,128]{2,1,0:T(8,128)(2,1)S(1)} collective-permute-done((bf16[2,512,128]{2,1,0:T(8,128)(2,1)S(1)}, bf16[2,512,128]{2,1,0:T(8,128)(2,1)S(1)}, u32[]{:S(2)}, u32[]{:S(2)}) %collective-permute-start.21) | collective-permute-done | bytes 262176 | tf_op jit(solution)/shard_map/ppermute | solution.py:37
  167.9 15.7 %all_to_all.10.heads_ref = bf16[4,512,128]{2,1,0:T(8,128)(2,1)S(1)} all-to-all(bf16[4,512,128]{2,1,0:T(8,128)(2,1)S(1)} %shard_map.85), channel_id=1, replica_groups=mesh['ylo'=2,'z'=16,'x'=4,'yh'=2,'core'=2] {'x'}, dimensions={0} | all-to-all | bytes 1048576 | tf_op jit(solution)/shard_map/all_to_all | solution.py:284
  183.6 4.4 %collective-permute-start.22 = (bf16[4,512,128]{2,1,0:T(8,128)(2,1)S(1)}, bf16[4,512,128]{2,1,0:T(8,128)(2,1)S(1)}, u32[]{:S(2)}, u32[]{:S(2)}) collective-permute-start(bf16[4,512,128]{2,1,0:T(8,128)(2,1)S(1)} %all_to_all.10.heads_ref), channel_id=1, source_target_pairs={{0,1},{1,0},{2,3},{3,2},{4,5},{5,4},{6,7},{7,6},{8,9},{9,8},{10,11... | collective-permute-start | bytes 1572872 | tf_op jit(solution)/shard_map/ppermute | solution.py:37
  192.5 15.4 %all_to_all.11 = bf16[4,256,384]{2,1,0:T(8,128)(2,1)S(1)} all-to-all(bf16[4,256,384]{2,1,0:T(8,128)(2,1)S(1)} %shard_map.86), channel_id=1, replica_groups=mesh['ylo'=2,'z'=16,'x'=4,'yh'=2,'core'=2] {'yh','ylo'}, dimensions={0} | all-to-all | bytes 1572864 | tf_op jit(solution)/shard_map/all_to_all | solution.py:286
  (66 shorter events, 49.2 us)
Async XLA Ops:
  6.5 99.8 %all-gather.5.cloned.1.call-start = ((), (), s32[]{:S(2)}) async-start(), calls=%async_computation.2 | async-start | bytes 6488064 | tf_op jit(solution)/shard_map/all_gather | solution.py:259
  7.3 180.8 %all-gather.7.cloned.1.call-start = ((), (), s32[]{:S(2)}) async-start(), calls=%async_computation.3 | async-start | bytes 1671168 | tf_op jit(solution)/shard_map/all_gather | solution.py:275
  8.3 9.9 %collective-permute-start = (bf16[3,192,256]{2,1,0:T(8,128)(2,1)S(1)}, bf16[3,192,256]{2,1,0:T(8,128)(2,1)S(1)}, u32[]{:S(2)}, u32[]{:S(2)}) collective-permute-start(bf16[3,192,256]{2,1,0:T(8,128)(2,1)S(1)} %pad_maximum_fusion), channel_id=1, source_target_pairs={{0,1},{1,257},{2,3},{3,259},{4,5},{5,261},{6,7},{7,263},{8,9},{9,2... | collective-permute-start | bytes 884744 | tf_op jit(solution)/shard_map/ppermute | solution.py:37
  18.2 8.0 %collective-permute-start.8 = (bf16[3,192,256]{2,1,0:T(8,128)(2,1)S(1)}, bf16[3,192,256]{2,1,0:T(8,128)(2,1)S(1)}, u32[]{:S(2)}, u32[]{:S(2)}) collective-permute-start(bf16[3,192,256]{2,1,0:T(8,128)(2,1)S(1)} %collective-permute-done), channel_id=1, source_target_pairs={{0,1},{2,3},{4,5},{6,7},{8,9},{10,11},{12,13},{14,15},{16,17},{18,... | collective-permute-start | bytes 884744 | tf_op jit(solution)/shard_map/ppermute | solution.py:37
  27.2 9.4 %collective-permute-start.1 = (bf16[3,192,256]{2,1,0:T(8,128)(2,1)S(1)}, bf16[3,192,256]{2,1,0:T(8,128)(2,1)S(1)}, u32[]{:S(2)}, u32[]{:S(2)}) collective-permute-start(bf16[3,192,256]{2,1,0:T(8,128)(2,1)S(1)} %get-tuple-element.15), channel_id=1, source_target_pairs={{0,16},{1,241},{2,18},{3,243},{4,20},{5,245},{6,22},{7,247},{8,24}... | collective-permute-start | bytes 884744 | tf_op jit(solution)/shard_map/ppermute | solution.py:37
  33.0 8.7 %collective-permute-start.9 = (bf16[3,192,256]{2,1,0:T(8,128)(2,1)S(1)}, bf16[3,192,256]{2,1,0:T(8,128)(2,1)S(1)}, u32[]{:S(2)}, u32[]{:S(2)}) collective-permute-start(bf16[3,192,256]{2,1,0:T(8,128)(2,1)S(1)} %get-tuple-element.14), channel_id=1, source_target_pairs={{0,16},{1,241},{2,18},{3,243},{4,20},{5,245},{6,22},{7,247},{8,24}... | collective-permute-start | bytes 884744 | tf_op jit(solution)/shard_map/ppermute | solution.py:37
  36.6 8.7 %collective-permute-start.2 = (bf16[3,192,256]{2,1,0:T(8,128)(2,1)S(1)}, bf16[3,192,256]{2,1,0:T(8,128)(2,1)S(1)}, u32[]{:S(2)}, u32[]{:S(2)}) collective-permute-start(bf16[3,192,256]{2,1,0:T(8,128)(2,1)S(1)} %collective-permute-done.1.refs_0_), channel_id=1, source_target_pairs={{0,16},{1,241},{2,18},{3,243},{4,20},{5,245},{6,22},{7,247},{8,24}... | collective-permute-start | bytes 884744 | tf_op jit(solution)/shard_map/ppermute | solution.py:37
  41.7 8.7 %collective-permute-start.10 = (bf16[3,192,256]{2,1,0:T(8,128)(2,1)S(1)}, bf16[3,192,256]{2,1,0:T(8,128)(2,1)S(1)}, u32[]{:S(2)}, u32[]{:S(2)}) collective-permute-start(bf16[3,192,256]{2,1,0:T(8,128)(2,1)S(1)} %collective-permute-done.9.refs_7_), channel_id=1, source_target_pairs={{0,16},{1,241},{2,18},{3,243},{4,20},{5,245},{6,22},{7,247},{8,24}... | collective-permute-start | bytes 884744 | tf_op jit(solution)/shard_map/ppermute | solution.py:37
  45.3 8.7 %collective-permute-start.3 = (bf16[3,192,256]{2,1,0:T(8,128)(2,1)S(1)}, bf16[3,192,256]{2,1,0:T(8,128)(2,1)S(1)}, u32[]{:S(2)}, u32[]{:S(2)}) collective-permute-start(bf16[3,192,256]{2,1,0:T(8,128)(2,1)S(1)} %collective-permute-done.2.refs_1_), channel_id=1, source_target_pairs={{0,16},{1,241},{2,18},{3,243},{4,20},{5,245},{6,22},{7,247},{8,24}... | collective-permute-start | bytes 884744 | tf_op jit(solution)/shard_map/ppermute | solution.py:37
  50.3 8.7 %collective-permute-start.11 = (bf16[3,192,256]{2,1,0:T(8,128)(2,1)S(1)}, bf16[3,192,256]{2,1,0:T(8,128)(2,1)S(1)}, u32[]{:S(2)}, u32[]{:S(2)}) collective-permute-start(bf16[3,192,256]{2,1,0:T(8,128)(2,1)S(1)} %collective-permute-done.10.refs_8_), channel_id=1, source_target_pairs={{0,16},{1,241},{2,18},{3,243},{4,20},{5,245},{6,22},{7,247},{8,24}... | collective-permute-start | bytes 884744 | tf_op jit(solution)/shard_map/ppermute | solution.py:37
  54.0 8.7 %collective-permute-start.4 = (bf16[3,192,256]{2,1,0:T(8,128)(2,1)S(1)}, bf16[3,192,256]{2,1,0:T(8,128)(2,1)S(1)}, u32[]{:S(2)}, u32[]{:S(2)}) collective-permute-start(bf16[3,192,256]{2,1,0:T(8,128)(2,1)S(1)} %collective-permute-done.3.refs_2_), channel_id=1, source_target_pairs={{0,16},{1,241},{2,18},{3,243},{4,20},{5,245},{6,22},{7,247},{8,24}... | collective-permute-start | bytes 884744 | tf_op jit(solution)/shard_map/ppermute | solution.py:37
  59.0 8.7 %collective-permute-start.12 = (bf16[3,192,256]{2,1,0:T(8,128)(2,1)S(1)}, bf16[3,192,256]{2,1,0:T(8,128)(2,1)S(1)}, u32[]{:S(2)}, u32[]{:S(2)}) collective-permute-start(bf16[3,192,256]{2,1,0:T(8,128)(2,1)S(1)} %collective-permute-done.11.refs_9_), channel_id=1, source_target_pairs={{0,16},{1,241},{2,18},{3,243},{4,20},{5,245},{6,22},{7,247},{8,24}... | collective-permute-start | bytes 884744 | tf_op jit(solution)/shard_map/ppermute | solution.py:37
  62.6 8.7 %collective-permute-start.5 = (bf16[3,192,256]{2,1,0:T(8,128)(2,1)S(1)}, bf16[3,192,256]{2,1,0:T(8,128)(2,1)S(1)}, u32[]{:S(2)}, u32[]{:S(2)}) collective-permute-start(bf16[3,192,256]{2,1,0:T(8,128)(2,1)S(1)} %collective-permute-done.4.refs_3_), channel_id=1, source_target_pairs={{0,16},{1,241},{2,18},{3,243},{4,20},{5,245},{6,22},{7,247},{8,24}... | collective-permute-start | bytes 884744 | tf_op jit(solution)/shard_map/ppermute | solution.py:37
  67.7 9.4 %collective-permute-start.13 = (bf16[3,192,256]{2,1,0:T(8,128)(2,1)S(1)}, bf16[3,192,256]{2,1,0:T(8,128)(2,1)S(1)}, u32[]{:S(2)}, u32[]{:S(2)}) collective-permute-start(bf16[3,192,256]{2,1,0:T(8,128)(2,1)S(1)} %collective-permute-done.12.refs_10_), channel_id=1, source_target_pairs={{0,16},{1,241},{2,18},{3,243},{4,20},{5,245},{6,22},{7,247},{8,24}... | collective-permute-start | bytes 884744 | tf_op jit(solution)/shard_map/ppermute | solution.py:37
  71.3 8.9 %collective-permute-start.6 = (bf16[3,192,256]{2,1,0:T(8,128)(2,1)S(1)}, bf16[3,192,256]{2,1,0:T(8,128)(2,1)}, u32[]{:S(2)}, u32[]{:S(2)}) collective-permute-start(bf16[3,192,256]{2,1,0:T(8,128)(2,1)S(1)} %collective-permute-done.5.refs_4_), channel_id=1, source_target_pairs={{0,16},{1,241},{2,18},{3,243},{4,20},{5,245},{6,22},{7,247},{8,24}... | collective-permute-start | bytes 884744 | tf_op jit(solution)/shard_map/ppermute | solution.py:37
  77.1 8.0 %collective-permute-start.14 = (bf16[3,192,256]{2,1,0:T(8,128)(2,1)S(1)}, bf16[3,192,256]{2,1,0:T(8,128)(2,1)}, u32[]{:S(2)}, u32[]{:S(2)}) collective-permute-start(bf16[3,192,256]{2,1,0:T(8,128)(2,1)S(1)} %collective-permute-done.13.refs_11_), channel_id=1, source_target_pairs={{0,16},{1,241},{2,18},{3,243},{4,20},{5,245},{6,22},{7,247},{8,24}... | collective-permute-start | bytes 884744 | tf_op jit(solution)/shard_map/ppermute | solution.py:37
  80.2 21.2 %collective-permute-start.7 = (bf16[3,192,256]{2,1,0:T(8,128)(2,1)}, bf16[3,192,256]{2,1,0:T(8,128)(2,1)S(1)}, u32[]{:S(2)}, u32[]{:S(2)}) collective-permute-start(bf16[3,192,256]{2,1,0:T(8,128)(2,1)} %collective-permute-done.6.refs_5_), channel_id=1, source_target_pairs={{0,16},{1,241},{2,18},{3,243},{4,20},{5,245},{6,22},{7,247},{8,24}... | collective-permute-start | bytes 884744 | tf_op jit(solution)/shard_map/ppermute | solution.py:37
  85.1 16.3 %collective-permute-start.15 = (bf16[3,192,256]{2,1,0:T(8,128)(2,1)}, bf16[3,192,256]{2,1,0:T(8,128)(2,1)S(1)}, u32[]{:S(2)}, u32[]{:S(2)}) collective-permute-start(bf16[3,192,256]{2,1,0:T(8,128)(2,1)} %collective-permute-done.14.refs_12_), channel_id=1, source_target_pairs={{0,16},{1,241},{2,18},{3,243},{4,20},{5,245},{6,22},{7,247},{8,24}... | collective-permute-start | bytes 884744 | tf_op jit(solution)/shard_map/ppermute | solution.py:37
  88.3 12.5 %collective-permute-start.23 = (bf16[192,256]{1,0:T(8,128)(2,1)}, bf16[192,256]{1,0:T(8,128)(2,1)S(1)}, u32[]{:S(2)}, u32[]{:S(2)}) collective-permute-start(bf16[192,256]{1,0:T(8,128)(2,1)} %bitcast.25), channel_id=1, source_target_pairs={{0,192},{1,448},{2,194},{3,450},{4,208},{5,464},{6,210},{7,466},{8... | collective-permute-start | bytes 294920 | tf_op jit(solution)/shard_map/ppermute | solution.py:37
  102.2 13.5 %collective-permute-start.16 = (bf16[3,192,256]{2,1,0:T(8,128)(2,1)}, bf16[3,192,256]{2,1,0:T(8,128)(2,1)}, u32[]{:S(2)}, u32[]{:S(2)}) collective-permute-start(bf16[3,192,256]{2,1,0:T(8,128)(2,1)} %broadcast_select_fusion), channel_id=1, source_target_pairs={{0,16},{1,241},{2,18},{3,243},{4,20},{5,245},{6,22},{7,247},{8,24}... | collective-permute-start | bytes 884744 | tf_op jit(solution)/shard_map/ppermute | solution.py:37
  131.3 21.0 %collective-permute-start.18 = (bf16[2,512,128]{2,1,0:T(8,128)(2,1)S(1)}, bf16[2,512,128]{2,1,0:T(8,128)(2,1)S(1)}, u32[]{:S(2)}, u32[]{:S(2)}) collective-permute-start(bf16[2,512,128]{2,1,0:T(8,128)(2,1)S(1)} %get-tuple-element.12.refs_2_), channel_id=1, source_target_pairs={{0,32},{1,33},{2,34},{3,35},{4,36},{5,37},{6,38},{7,39},{8,40},{9,... | collective-permute-start | bytes 786440 | tf_op jit(solution)/shard_map/ppermute | solution.py:37
  135.3 24.3 %collective-permute-start.19 = (bf16[2,512,128]{2,1,0:T(8,128)(2,1)S(1)}, bf16[2,512,128]{2,1,0:T(8,128)(2,1)S(1)}, u32[]{:S(2)}, u32[]{:S(2)}) collective-permute-start(bf16[2,512,128]{2,1,0:T(8,128)(2,1)S(1)} %get-tuple-element.12.refs_2_), channel_id=1, source_target_pairs={{0,16},{1,17},{2,18},{3,19},{4,20},{5,21},{6,22},{7,23},{8,24},{9,... | collective-permute-start | bytes 786440 | tf_op jit(solution)/shard_map/ppermute | solution.py:37
  137.2 22.3 %collective-permute-start.20 = (bf16[2,512,128]{2,1,0:T(8,128)(2,1)S(1)}, bf16[2,512,128]{2,1,0:T(8,128)(2,1)S(1)}, u32[]{:S(2)}, u32[]{:S(2)}) collective-permute-start(bf16[2,512,128]{2,1,0:T(8,128)(2,1)S(1)} %get-tuple-element.12.refs_2_), channel_id=1, source_target_pairs={{0,240},{1,241},{2,242},{3,243},{4,244},{5,245},{6,246},{7,247},{8... | collective-permute-start | bytes 786440 | tf_op jit(solution)/shard_map/ppermute | solution.py:37
  141.8 24.2 %collective-permute-start.21 = (bf16[2,512,128]{2,1,0:T(8,128)(2,1)S(1)}, bf16[2,512,128]{2,1,0:T(8,128)(2,1)S(1)}, u32[]{:S(2)}, u32[]{:S(2)}) collective-permute-start(bf16[2,512,128]{2,1,0:T(8,128)(2,1)S(1)} %get-tuple-element.12.refs_2_), channel_id=1, source_target_pairs={{0,224},{1,225},{2,226},{3,227},{4,228},{5,229},{6,230},{7,231},{8... | collective-permute-start | bytes 786440 | tf_op jit(solution)/shard_map/ppermute | solution.py:37
  (13 other events, 334.3 us)
Sparse Core Ops, SparseCore 0:
  9.5 76.7 all-gather.4
  101.5 75.9 all-gather.6

commit v5 on v4

--- a/solution.py
+++ b/solution.py
@@ -98,7 +98,7 @@
             pl.BlockSpec((16, 384), lambda s, r: (0, 0)),
         ],
         out_specs=pl.BlockSpec((rows, WINDOW), lambda s, r: (s * (256 // rows) + r, 0)),
-        compiler_params=pltpu.CompilerParams(vmem_limit_bytes=60 << 20),
+        compiler_params=pltpu.CompilerParams(vmem_limit_bytes=16 << 20),
         cost_estimate=pl.CostEstimate(flops=30_000_000, bytes_accessed=10_000_000, transcendentals=0),
     )(place, acts.reshape(2, 16, 256, 384), gain.reshape(16, 384))
 
@@ -154,7 +154,7 @@
         + [pl.BlockSpec(memory_space=pl.ANY)] * 16,
         out_specs=[pl.BlockSpec((n, 3 * HD), lambda r: (r, 0)) for n in (rows, rows + 8)],
         scratch_shapes=[pltpu.VMEM((WINDOW, 768), BF), pltpu.SemaphoreType.DMA((48,))],
-        compiler_params=pltpu.CompilerParams(vmem_limit_bytes=32 << 20),
+        compiler_params=pltpu.CompilerParams(vmem_limit_bytes=16 << 20),
         cost_estimate=pl.CostEstimate(flops=2 * 512 * WINDOW * 768, bytes_accessed=10_000_000, transcendentals=0),
     )(place, gains, normed, *shards)
 
@@ -178,7 +178,7 @@
         out_shape=(jax.ShapeDtypeStruct((512, HD), BF), jax.ShapeDtypeStruct((2, 512, HD), BF)),
         in_specs=[pl.BlockSpec(memory_space=pltpu.SMEM)] + [pl.BlockSpec(memory_space=pltpu.VMEM)] * 3,
         out_specs=(pl.BlockSpec(memory_space=pltpu.VMEM), pl.BlockSpec(memory_space=pltpu.VMEM)),
-        compiler_params=pltpu.CompilerParams(vmem_limit_bytes=32 << 20),
+        compiler_params=pltpu.CompilerParams(vmem_limit_bytes=16 << 20),
         cost_estimate=pl.CostEstimate(flops=4_000_000, bytes_accessed=2_000_000, transcendentals=0),
     )(place, mine, theirs.reshape(4, 136, 3 * HD), gains)
 
@@ -221,7 +221,7 @@
         out_shape=jax.ShapeDtypeStruct((4, 512, HD), BF),
         in_specs=[pl.BlockSpec(memory_space=pltpu.SMEM)] + [pl.BlockSpec(memory_space=pltpu.VMEM)] * 6,
         out_specs=pl.BlockSpec(memory_space=pltpu.VMEM),
-        compiler_params=pltpu.CompilerParams(vmem_limit_bytes=32 << 20),
+        compiler_params=pltpu.CompilerParams(vmem_limit_bytes=16 << 20),
         cost_estimate=pl.CostEstimate(flops=4 * 512 * 1280 * HD, bytes_accessed=1_600_000, transcendentals=512 * 1280),
     )(place, query, *kvs)
 
@@ -247,7 +247,7 @@
         out_shape=jax.ShapeDtypeStruct((4, 256, 384), BF),
         in_specs=[pl.BlockSpec(memory_space=pltpu.SMEM)] + [pl.BlockSpec(memory_space=pltpu.VMEM)] * 3,
         out_specs=pl.BlockSpec(memory_space=pltpu.VMEM),
-        compiler_params=pltpu.CompilerParams(vmem_limit_bytes=32 << 20),
+        compiler_params=pltpu.CompilerParams(vmem_limit_bytes=16 << 20),
         cost_estimate=pl.CostEstimate(flops=2 * 512 * 768 * 1024, bytes_accessed=3_500_000, transcendentals=0),
     )(place, heads, others, weights)
 

time: 217 us -> 212 us (0.977)
  Pallas kernels: 20.3 us -> 17.2 us
  blocking collectives: 31.1 us -> 28.7 us
    pallas_call x1, Pallas kernels: 9.34 us -> 6.4 us  [normalise(): pl.pallas_call(norm_kernel, grid=(2, 256 // rows), out_shape=jax.ShapeDty...]
    all_to_all x1, blocking collectives: 15.7 us -> 13.5 us  [per_device(): heads = lax.all_to_all(attended, 'x', 0, 0, tiled=True)]
    unnamed x22 -> x20, local copies, waits for them, and re-layouts: 6.46 us -> 6.29 us
  transfers between devices with their start and end apart: 26 -> 26, of which waited for: 13 -> 13; matrix products, arithmetic and copies ran while one was open for 2% -> 1% of each run, Pallas kernels for 9% -> 7%
where the time goes in v5:
time: 212 us; the launch traced here: 211 us
  starting transfers between devices  96.1 us (45%)
  waiting for transfers between devices  44.9 us (21%)
  blocking collectives  28.7 us (14%)
  Pallas kernels  17.2 us (8%)
  between operations  13.8 us (7%)
  local copies, waits for them, and re-layouts  6.38 us (3%)
  other arithmetic  3.65 us (2%)
    ppermute x24, starting transfers between devices, send(): return lax.ppermute(value, AXES, pairs)  96 us
    ppermute x24, waiting for transfers between devices, send(): return lax.ppermute(value, AXES, pairs)  44.1 us
    all_to_all x1, blocking collectives, per_device(): parts = lax.all_to_all(parts, ('yh', 'ylo'), 0, 0, tiled=True)  15.3 us
    all_to_all x1, blocking collectives, per_device(): heads = lax.all_to_all(attended, 'x', 0, 0, tiled=True)  13.5 us
    pallas_call x1, Pallas kernels, normalise(): pl.pallas_call(norm_kernel, grid=(2, 256 // rows), out_shape=jax.ShapeDty...  6.4 us
    unnamed x20, local copies, waits for them, and re-layouts  6.29 us
    pallas_call x1, Pallas kernels, multiply(): pl.pallas_call(product_kernel, grid=(512 // rows,), out_shape=[jax.ShapeD...  6.17 us
  transfers between devices with their start and end apart: 26, of which 13 were waited for; matrix products, arithmetic and copies ran while one was open for 1% of the time, Pallas kernels for 7%

profile of v5, /device:TPU:1, one launch (start us, length us, event | category | flops | bytes accessed | tf_op | source)
XLA Modules:
  0.0 210.7 jit_solution(17784508195150649668)
XLA Ops:
  8.3 4.0 %collective-permute-start = (bf16[3,192,256]{2,1,0:T(8,128)(2,1)S(1)}, bf16[3,192,256]{2,1,0:T(8,128)(2,1)S(1)}, u32[]{:S(2)}, u32[]{:S(2)}) collective-permute-start(bf16[3,192,256]{2,1,0:T(8,128)(2,1)S(1)} %pad_maximum_fusion), channel_id=1, source_target_pairs={{0,1},{1,257},{2,3},{3,259},{4,5},{5,261},{6,7},{7,263},{8,9},{9,2... | collective-permute-start | bytes 884744 | tf_op jit(solution)/shard_map/ppermute | solution.py:37
  12.4 5.8 %collective-permute-done = bf16[3,192,256]{2,1,0:T(8,128)(2,1)S(1)} collective-permute-done((bf16[3,192,256]{2,1,0:T(8,128)(2,1)S(1)}, bf16[3,192,256]{2,1,0:T(8,128)(2,1)S(1)}, u32[]{:S(2)}, u32[]{:S(2)}) %collective-permute-start) | collective-permute-done | bytes 294944 | tf_op jit(solution)/shard_map/ppermute | solution.py:37
  19.5 6.7 %collective-permute-done.8 = bf16[3,192,256]{2,1,0:T(8,128)(2,1)S(1)} collective-permute-done((bf16[3,192,256]{2,1,0:T(8,128)(2,1)S(1)}, bf16[3,192,256]{2,1,0:T(8,128)(2,1)S(1)}, u32[]{:S(2)}, u32[]{:S(2)}) %collective-permute-start.8) | collective-permute-done | bytes 294944 | tf_op jit(solution)/shard_map/ppermute | solution.py:37
  27.2 5.7 %collective-permute-start.1 = (bf16[3,192,256]{2,1,0:T(8,128)(2,1)S(1)}, bf16[3,192,256]{2,1,0:T(8,128)(2,1)S(1)}, u32[]{:S(2)}, u32[]{:S(2)}) collective-permute-start(bf16[3,192,256]{2,1,0:T(8,128)(2,1)S(1)} %get-tuple-element.15), channel_id=1, source_target_pairs={{0,16},{1,241},{2,18},{3,243},{4,20},{5,245},{6,22},{7,247},{8,24}... | collective-permute-start | bytes 884744 | tf_op jit(solution)/shard_map/ppermute | solution.py:37
  36.6 5.0 %collective-permute-start.2 = (bf16[3,192,256]{2,1,0:T(8,128)(2,1)S(1)}, bf16[3,192,256]{2,1,0:T(8,128)(2,1)S(1)}, u32[]{:S(2)}, u32[]{:S(2)}) collective-permute-start(bf16[3,192,256]{2,1,0:T(8,128)(2,1)S(1)} %collective-permute-done.1.refs_0_), channel_id=1, source_target_pairs={{0,16},{1,241},{2,18},{3,243},{4,20},{5,245},{6,22},{7,247},{8,24}... | collective-permute-start | bytes 884744 | tf_op jit(solution)/shard_map/ppermute | solution.py:37
  41.7 3.1 %collective-permute-start.10 = (bf16[3,192,256]{2,1,0:T(8,128)(2,1)S(1)}, bf16[3,192,256]{2,1,0:T(8,128)(2,1)S(1)}, u32[]{:S(2)}, u32[]{:S(2)}) collective-permute-start(bf16[3,192,256]{2,1,0:T(8,128)(2,1)S(1)} %collective-permute-done.9.refs_7_), channel_id=1, source_target_pairs={{0,16},{1,241},{2,18},{3,243},{4,20},{5,245},{6,22},{7,247},{8,24}... | collective-permute-start | bytes 884744 | tf_op jit(solution)/shard_map/ppermute | solution.py:37
  45.3 5.0 %collective-permute-start.3 = (bf16[3,192,256]{2,1,0:T(8,128)(2,1)S(1)}, bf16[3,192,256]{2,1,0:T(8,128)(2,1)S(1)}, u32[]{:S(2)}, u32[]{:S(2)}) collective-permute-start(bf16[3,192,256]{2,1,0:T(8,128)(2,1)S(1)} %collective-permute-done.2.refs_1_), channel_id=1, source_target_pairs={{0,16},{1,241},{2,18},{3,243},{4,20},{5,245},{6,22},{7,247},{8,24}... | collective-permute-start | bytes 884744 | tf_op jit(solution)/shard_map/ppermute | solution.py:37
  50.3 3.1 %collective-permute-start.11 = (bf16[3,192,256]{2,1,0:T(8,128)(2,1)S(1)}, bf16[3,192,256]{2,1,0:T(8,128)(2,1)S(1)}, u32[]{:S(2)}, u32[]{:S(2)}) collective-permute-start(bf16[3,192,256]{2,1,0:T(8,128)(2,1)S(1)} %collective-permute-done.10.refs_8_), channel_id=1, source_target_pairs={{0,16},{1,241},{2,18},{3,243},{4,20},{5,245},{6,22},{7,247},{8,24}... | collective-permute-start | bytes 884744 | tf_op jit(solution)/shard_map/ppermute | solution.py:37
  54.0 5.0 %collective-permute-start.4 = (bf16[3,192,256]{2,1,0:T(8,128)(2,1)S(1)}, bf16[3,192,256]{2,1,0:T(8,128)(2,1)S(1)}, u32[]{:S(2)}, u32[]{:S(2)}) collective-permute-start(bf16[3,192,256]{2,1,0:T(8,128)(2,1)S(1)} %collective-permute-done.3.refs_2_), channel_id=1, source_target_pairs={{0,16},{1,241},{2,18},{3,243},{4,20},{5,245},{6,22},{7,247},{8,24}... | collective-permute-start | bytes 884744 | tf_op jit(solution)/shard_map/ppermute | solution.py:37
  62.6 5.0 %collective-permute-start.5 = (bf16[3,192,256]{2,1,0:T(8,128)(2,1)S(1)}, bf16[3,192,256]{2,1,0:T(8,128)(2,1)S(1)}, u32[]{:S(2)}, u32[]{:S(2)}) collective-permute-start(bf16[3,192,256]{2,1,0:T(8,128)(2,1)S(1)} %collective-permute-done.4.refs_3_), channel_id=1, source_target_pairs={{0,16},{1,241},{2,18},{3,243},{4,20},{5,245},{6,22},{7,247},{8,24}... | collective-permute-start | bytes 884744 | tf_op jit(solution)/shard_map/ppermute | solution.py:37
  71.3 5.0 %collective-permute-start.6 = (bf16[3,192,256]{2,1,0:T(8,128)(2,1)S(1)}, bf16[3,192,256]{2,1,0:T(8,128)(2,1)}, u32[]{:S(2)}, u32[]{:S(2)}) collective-permute-start(bf16[3,192,256]{2,1,0:T(8,128)(2,1)S(1)} %collective-permute-done.5.refs_4_), channel_id=1, source_target_pairs={{0,16},{1,241},{2,18},{3,243},{4,20},{5,245},{6,22},{7,247},{8,24}... | collective-permute-start | bytes 884744 | tf_op jit(solution)/shard_map/ppermute | solution.py:37
  80.2 4.9 %collective-permute-start.7 = (bf16[3,192,256]{2,1,0:T(8,128)(2,1)}, bf16[3,192,256]{2,1,0:T(8,128)(2,1)S(1)}, u32[]{:S(2)}, u32[]{:S(2)}) collective-permute-start(bf16[3,192,256]{2,1,0:T(8,128)(2,1)} %collective-permute-done.6.refs_5_), channel_id=1, source_target_pairs={{0,16},{1,241},{2,18},{3,243},{4,20},{5,245},{6,22},{7,247},{8,24}... | collective-permute-start | bytes 884744 | tf_op jit(solution)/shard_map/ppermute | solution.py:37
  88.3 10.1 %collective-permute-start.23 = (bf16[192,256]{1,0:T(8,128)(2,1)}, bf16[192,256]{1,0:T(8,128)(2,1)S(1)}, u32[]{:S(2)}, u32[]{:S(2)}) collective-permute-start(bf16[192,256]{1,0:T(8,128)(2,1)} %bitcast.25), channel_id=1, source_target_pairs={{0,192},{1,448},{2,194},{3,450},{4,208},{5,464},{6,210},{7,466},{8... | collective-permute-start | bytes 294920 | tf_op jit(solution)/shard_map/ppermute | solution.py:37
  108.1 6.4 %shard_map.82.normed_ref = bf16[512,3456]{1,0:T(8,128)(2,1)S(1)} custom-call(s32[5]{0:T(128)S(1)} %stack.44.place_ref, bf16[2,16,256,384]{3,2,1,0:T(8,128)(2,1)S(1)} %bitcast.14, f32[16,384]{1,0:T(8,128)S(1)} %reshape.10.gain_ref), custom_call_target="tpu_custom_call" | custom-call | flops 30000000 | bytes 10000000 | tf_op jit(solution)/shard_map/pallas_call | solution.py:91
  114.5 6.2 %shard_map.83 = (f32[512,384]{1,0:T(8,128)S(1)}, f32[544,384]{1,0:T(8,128)S(1)}) custom-call(s32[5]{0:T(128)S(1)} %stack.44.place_ref, f32[8,384]{1,0:T(8,128)S(1)} %select_maximum_fusion.gains_ref, bf16[512,3456]{1,0:T(8,128)(2,1)S(1)} %shard_map.82.normed_ref, bf16[3,192,256]{2,1,0:T(8,128)(2,1)S(1)} %collective-permute-done.1.refs_0_, ...), custom_call_target="tpu_custom_call" | custom-call | flops 2717908992 | bytes 10000000 | tf_op jit(solution)/shard_map/pallas_call | solution.py:149
  126.9 4.0 %collective-permute-start.18 = (bf16[2,512,128]{2,1,0:T(8,128)(2,1)S(1)}, bf16[2,512,128]{2,1,0:T(8,128)(2,1)S(1)}, u32[]{:S(2)}, u32[]{:S(2)}) collective-permute-start(bf16[2,512,128]{2,1,0:T(8,128)(2,1)S(1)} %get-tuple-element.12.refs_2_), channel_id=1, source_target_pairs={{0,32},{1,33},{2,34},{3,35},{4,36},{5,37},{6,38},{7,39},{8,40},{9,... | collective-permute-start | bytes 786440 | tf_op jit(solution)/shard_map/ppermute | solution.py:37
  132.9 4.6 %collective-permute-start.20 = (bf16[2,512,128]{2,1,0:T(8,128)(2,1)S(1)}, bf16[2,512,128]{2,1,0:T(8,128)(2,1)S(1)}, u32[]{:S(2)}, u32[]{:S(2)}) collective-permute-start(bf16[2,512,128]{2,1,0:T(8,128)(2,1)S(1)} %get-tuple-element.12.refs_2_), channel_id=1, source_target_pairs={{0,240},{1,241},{2,242},{3,243},{4,244},{5,245},{6,246},{7,247},{8... | collective-permute-start | bytes 786440 | tf_op jit(solution)/shard_map/ppermute | solution.py:37
  137.4 3.1 %collective-permute-start.21 = (bf16[2,512,128]{2,1,0:T(8,128)(2,1)S(1)}, bf16[2,512,128]{2,1,0:T(8,128)(2,1)S(1)}, u32[]{:S(2)}, u32[]{:S(2)}) collective-permute-start(bf16[2,512,128]{2,1,0:T(8,128)(2,1)S(1)} %get-tuple-element.12.refs_2_), channel_id=1, source_target_pairs={{0,224},{1,225},{2,226},{3,227},{4,228},{5,229},{6,230},{7,231},{8... | collective-permute-start | bytes 786440 | tf_op jit(solution)/shard_map/ppermute | solution.py:37
  140.6 6.3 %collective-permute-done.18.refs_0_ = bf16[2,512,128]{2,1,0:T(8,128)(2,1)S(1)} collective-permute-done((bf16[2,512,128]{2,1,0:T(8,128)(2,1)S(1)}, bf16[2,512,128]{2,1,0:T(8,128)(2,1)S(1)}, u32[]{:S(2)}, u32[]{:S(2)}) %collective-permute-start.18) | collective-permute-done | bytes 262176 | tf_op jit(solution)/shard_map/ppermute | solution.py:37
  146.9 8.8 %collective-permute-done.19.refs_1_ = bf16[2,512,128]{2,1,0:T(8,128)(2,1)S(1)} collective-permute-done((bf16[2,512,128]{2,1,0:T(8,128)(2,1)S(1)}, bf16[2,512,128]{2,1,0:T(8,128)(2,1)S(1)}, u32[]{:S(2)}, u32[]{:S(2)}) %collective-permute-start.19) | collective-permute-done | bytes 262176 | tf_op jit(solution)/shard_map/ppermute | solution.py:37
  155.7 7.7 %collective-permute-done.21.refs_4_ = bf16[2,512,128]{2,1,0:T(8,128)(2,1)S(1)} collective-permute-done((bf16[2,512,128]{2,1,0:T(8,128)(2,1)S(1)}, bf16[2,512,128]{2,1,0:T(8,128)(2,1)S(1)}, u32[]{:S(2)}, u32[]{:S(2)}) %collective-permute-start.21) | collective-permute-done | bytes 262176 | tf_op jit(solution)/shard_map/ppermute | solution.py:37
  165.3 13.5 %all_to_all.10.heads_ref = bf16[4,512,128]{2,1,0:T(8,128)(2,1)S(1)} all-to-all(bf16[4,512,128]{2,1,0:T(8,128)(2,1)S(1)} %shard_map.85), channel_id=1, replica_groups=mesh['ylo'=2,'z'=16,'x'=4,'yh'=2,'core'=2] {'x'}, dimensions={0} | all-to-all | bytes 1048576 | tf_op jit(solution)/shard_map/all_to_all | solution.py:284
  178.8 4.4 %collective-permute-start.22 = (bf16[4,512,128]{2,1,0:T(8,128)(2,1)S(1)}, bf16[4,512,128]{2,1,0:T(8,128)(2,1)S(1)}, u32[]{:S(2)}, u32[]{:S(2)}) collective-permute-start(bf16[4,512,128]{2,1,0:T(8,128)(2,1)S(1)} %all_to_all.10.heads_ref), channel_id=1, source_target_pairs={{0,1},{1,0},{2,3},{3,2},{4,5},{5,4},{6,7},{7,6},{8,9},{9,8},{10,11... | collective-permute-start | bytes 1572872 | tf_op jit(solution)/shard_map/ppermute | solution.py:37
  187.8 15.3 %all_to_all.11 = bf16[4,256,384]{2,1,0:T(8,128)(2,1)S(1)} all-to-all(bf16[4,256,384]{2,1,0:T(8,128)(2,1)S(1)} %shard_map.86), channel_id=1, replica_groups=mesh['ylo'=2,'z'=16,'x'=4,'yh'=2,'core'=2] {'yh','ylo'}, dimensions={0} | all-to-all | bytes 1572864 | tf_op jit(solution)/shard_map/all_to_all | solution.py:286
  (64 shorter events, 47.9 us)
Async XLA Ops:
  6.5 98.7 %all-gather.5.cloned.1.call-start = ((), (), s32[]{:S(2)}) async-start(), calls=%async_computation.2 | async-start | bytes 6488064 | tf_op jit(solution)/shard_map/all_gather | solution.py:259
  7.3 176.0 %all-gather.7.cloned.1.call-start = ((), (), s32[]{:S(2)}) async-start(), calls=%async_computation.3 | async-start | bytes 1671168 | tf_op jit(solution)/shard_map/all_gather | solution.py:275
  8.3 9.9 %collective-permute-start = (bf16[3,192,256]{2,1,0:T(8,128)(2,1)S(1)}, bf16[3,192,256]{2,1,0:T(8,128)(2,1)S(1)}, u32[]{:S(2)}, u32[]{:S(2)}) collective-permute-start(bf16[3,192,256]{2,1,0:T(8,128)(2,1)S(1)} %pad_maximum_fusion), channel_id=1, source_target_pairs={{0,1},{1,257},{2,3},{3,259},{4,5},{5,261},{6,7},{7,263},{8,9},{9,2... | collective-permute-start | bytes 884744 | tf_op jit(solution)/shard_map/ppermute | solution.py:37
  18.2 8.0 %collective-permute-start.8 = (bf16[3,192,256]{2,1,0:T(8,128)(2,1)S(1)}, bf16[3,192,256]{2,1,0:T(8,128)(2,1)S(1)}, u32[]{:S(2)}, u32[]{:S(2)}) collective-permute-start(bf16[3,192,256]{2,1,0:T(8,128)(2,1)S(1)} %collective-permute-done), channel_id=1, source_target_pairs={{0,1},{2,3},{4,5},{6,7},{8,9},{10,11},{12,13},{14,15},{16,17},{18,... | collective-permute-start | bytes 884744 | tf_op jit(solution)/shard_map/ppermute | solution.py:37
  27.2 9.4 %collective-permute-start.1 = (bf16[3,192,256]{2,1,0:T(8,128)(2,1)S(1)}, bf16[3,192,256]{2,1,0:T(8,128)(2,1)S(1)}, u32[]{:S(2)}, u32[]{:S(2)}) collective-permute-start(bf16[3,192,256]{2,1,0:T(8,128)(2,1)S(1)} %get-tuple-element.15), channel_id=1, source_target_pairs={{0,16},{1,241},{2,18},{3,243},{4,20},{5,245},{6,22},{7,247},{8,24}... | collective-permute-start | bytes 884744 | tf_op jit(solution)/shard_map/ppermute | solution.py:37
  33.0 8.7 %collective-permute-start.9 = (bf16[3,192,256]{2,1,0:T(8,128)(2,1)S(1)}, bf16[3,192,256]{2,1,0:T(8,128)(2,1)S(1)}, u32[]{:S(2)}, u32[]{:S(2)}) collective-permute-start(bf16[3,192,256]{2,1,0:T(8,128)(2,1)S(1)} %get-tuple-element.14), channel_id=1, source_target_pairs={{0,16},{1,241},{2,18},{3,243},{4,20},{5,245},{6,22},{7,247},{8,24}... | collective-permute-start | bytes 884744 | tf_op jit(solution)/shard_map/ppermute | solution.py:37
  36.6 8.7 %collective-permute-start.2 = (bf16[3,192,256]{2,1,0:T(8,128)(2,1)S(1)}, bf16[3,192,256]{2,1,0:T(8,128)(2,1)S(1)}, u32[]{:S(2)}, u32[]{:S(2)}) collective-permute-start(bf16[3,192,256]{2,1,0:T(8,128)(2,1)S(1)} %collective-permute-done.1.refs_0_), channel_id=1, source_target_pairs={{0,16},{1,241},{2,18},{3,243},{4,20},{5,245},{6,22},{7,247},{8,24}... | collective-permute-start | bytes 884744 | tf_op jit(solution)/shard_map/ppermute | solution.py:37
  41.7 8.7 %collective-permute-start.10 = (bf16[3,192,256]{2,1,0:T(8,128)(2,1)S(1)}, bf16[3,192,256]{2,1,0:T(8,128)(2,1)S(1)}, u32[]{:S(2)}, u32[]{:S(2)}) collective-permute-start(bf16[3,192,256]{2,1,0:T(8,128)(2,1)S(1)} %collective-permute-done.9.refs_7_), channel_id=1, source_target_pairs={{0,16},{1,241},{2,18},{3,243},{4,20},{5,245},{6,22},{7,247},{8,24}... | collective-permute-start | bytes 884744 | tf_op jit(solution)/shard_map/ppermute | solution.py:37
  45.3 8.7 %collective-permute-start.3 = (bf16[3,192,256]{2,1,0:T(8,128)(2,1)S(1)}, bf16[3,192,256]{2,1,0:T(8,128)(2,1)S(1)}, u32[]{:S(2)}, u32[]{:S(2)}) collective-permute-start(bf16[3,192,256]{2,1,0:T(8,128)(2,1)S(1)} %collective-permute-done.2.refs_1_), channel_id=1, source_target_pairs={{0,16},{1,241},{2,18},{3,243},{4,20},{5,245},{6,22},{7,247},{8,24}... | collective-permute-start | bytes 884744 | tf_op jit(solution)/shard_map/ppermute | solution.py:37
  50.3 8.7 %collective-permute-start.11 = (bf16[3,192,256]{2,1,0:T(8,128)(2,1)S(1)}, bf16[3,192,256]{2,1,0:T(8,128)(2,1)S(1)}, u32[]{:S(2)}, u32[]{:S(2)}) collective-permute-start(bf16[3,192,256]{2,1,0:T(8,128)(2,1)S(1)} %collective-permute-done.10.refs_8_), channel_id=1, source_target_pairs={{0,16},{1,241},{2,18},{3,243},{4,20},{5,245},{6,22},{7,247},{8,24}... | collective-permute-start | bytes 884744 | tf_op jit(solution)/shard_map/ppermute | solution.py:37
  54.0 8.7 %collective-permute-start.4 = (bf16[3,192,256]{2,1,0:T(8,128)(2,1)S(1)}, bf16[3,192,256]{2,1,0:T(8,128)(2,1)S(1)}, u32[]{:S(2)}, u32[]{:S(2)}) collective-permute-start(bf16[3,192,256]{2,1,0:T(8,128)(2,1)S(1)} %collective-permute-done.3.refs_2_), channel_id=1, source_target_pairs={{0,16},{1,241},{2,18},{3,243},{4,20},{5,245},{6,22},{7,247},{8,24}... | collective-permute-start | bytes 884744 | tf_op jit(solution)/shard_map/ppermute | solution.py:37
  59.0 8.7 %collective-permute-start.12 = (bf16[3,192,256]{2,1,0:T(8,128)(2,1)S(1)}, bf16[3,192,256]{2,1,0:T(8,128)(2,1)S(1)}, u32[]{:S(2)}, u32[]{:S(2)}) collective-permute-start(bf16[3,192,256]{2,1,0:T(8,128)(2,1)S(1)} %collective-permute-done.11.refs_9_), channel_id=1, source_target_pairs={{0,16},{1,241},{2,18},{3,243},{4,20},{5,245},{6,22},{7,247},{8,24}... | collective-permute-start | bytes 884744 | tf_op jit(solution)/shard_map/ppermute | solution.py:37
  62.6 8.7 %collective-permute-start.5 = (bf16[3,192,256]{2,1,0:T(8,128)(2,1)S(1)}, bf16[3,192,256]{2,1,0:T(8,128)(2,1)S(1)}, u32[]{:S(2)}, u32[]{:S(2)}) collective-permute-start(bf16[3,192,256]{2,1,0:T(8,128)(2,1)S(1)} %collective-permute-done.4.refs_3_), channel_id=1, source_target_pairs={{0,16},{1,241},{2,18},{3,243},{4,20},{5,245},{6,22},{7,247},{8,24}... | collective-permute-start | bytes 884744 | tf_op jit(solution)/shard_map/ppermute | solution.py:37
  67.7 9.4 %collective-permute-start.13 = (bf16[3,192,256]{2,1,0:T(8,128)(2,1)S(1)}, bf16[3,192,256]{2,1,0:T(8,128)(2,1)S(1)}, u32[]{:S(2)}, u32[]{:S(2)}) collective-permute-start(bf16[3,192,256]{2,1,0:T(8,128)(2,1)S(1)} %collective-permute-done.12.refs_10_), channel_id=1, source_target_pairs={{0,16},{1,241},{2,18},{3,243},{4,20},{5,245},{6,22},{7,247},{8,24}... | collective-permute-start | bytes 884744 | tf_op jit(solution)/shard_map/ppermute | solution.py:37
  71.3 8.9 %collective-permute-start.6 = (bf16[3,192,256]{2,1,0:T(8,128)(2,1)S(1)}, bf16[3,192,256]{2,1,0:T(8,128)(2,1)}, u32[]{:S(2)}, u32[]{:S(2)}) collective-permute-start(bf16[3,192,256]{2,1,0:T(8,128)(2,1)S(1)} %collective-permute-done.5.refs_4_), channel_id=1, source_target_pairs={{0,16},{1,241},{2,18},{3,243},{4,20},{5,245},{6,22},{7,247},{8,24}... | collective-permute-start | bytes 884744 | tf_op jit(solution)/shard_map/ppermute | solution.py:37
  77.1 8.0 %collective-permute-start.14 = (bf16[3,192,256]{2,1,0:T(8,128)(2,1)S(1)}, bf16[3,192,256]{2,1,0:T(8,128)(2,1)}, u32[]{:S(2)}, u32[]{:S(2)}) collective-permute-start(bf16[3,192,256]{2,1,0:T(8,128)(2,1)S(1)} %collective-permute-done.13.refs_11_), channel_id=1, source_target_pairs={{0,16},{1,241},{2,18},{3,243},{4,20},{5,245},{6,22},{7,247},{8,24}... | collective-permute-start | bytes 884744 | tf_op jit(solution)/shard_map/ppermute | solution.py:37
  80.2 21.2 %collective-permute-start.7 = (bf16[3,192,256]{2,1,0:T(8,128)(2,1)}, bf16[3,192,256]{2,1,0:T(8,128)(2,1)S(1)}, u32[]{:S(2)}, u32[]{:S(2)}) collective-permute-start(bf16[3,192,256]{2,1,0:T(8,128)(2,1)} %collective-permute-done.6.refs_5_), channel_id=1, source_target_pairs={{0,16},{1,241},{2,18},{3,243},{4,20},{5,245},{6,22},{7,247},{8,24}... | collective-permute-start | bytes 884744 | tf_op jit(solution)/shard_map/ppermute | solution.py:37
  85.1 16.3 %collective-permute-start.15 = (bf16[3,192,256]{2,1,0:T(8,128)(2,1)}, bf16[3,192,256]{2,1,0:T(8,128)(2,1)S(1)}, u32[]{:S(2)}, u32[]{:S(2)}) collective-permute-start(bf16[3,192,256]{2,1,0:T(8,128)(2,1)} %collective-permute-done.14.refs_12_), channel_id=1, source_target_pairs={{0,16},{1,241},{2,18},{3,243},{4,20},{5,245},{6,22},{7,247},{8,24}... | collective-permute-start | bytes 884744 | tf_op jit(solution)/shard_map/ppermute | solution.py:37
  88.3 12.5 %collective-permute-start.23 = (bf16[192,256]{1,0:T(8,128)(2,1)}, bf16[192,256]{1,0:T(8,128)(2,1)S(1)}, u32[]{:S(2)}, u32[]{:S(2)}) collective-permute-start(bf16[192,256]{1,0:T(8,128)(2,1)} %bitcast.25), channel_id=1, source_target_pairs={{0,192},{1,448},{2,194},{3,450},{4,208},{5,464},{6,210},{7,466},{8... | collective-permute-start | bytes 294920 | tf_op jit(solution)/shard_map/ppermute | solution.py:37
  102.2 12.3 %collective-permute-start.16 = (bf16[3,192,256]{2,1,0:T(8,128)(2,1)}, bf16[3,192,256]{2,1,0:T(8,128)(2,1)}, u32[]{:S(2)}, u32[]{:S(2)}) collective-permute-start(bf16[3,192,256]{2,1,0:T(8,128)(2,1)} %broadcast_select_fusion), channel_id=1, source_target_pairs={{0,16},{1,241},{2,18},{3,243},{4,20},{5,245},{6,22},{7,247},{8,24}... | collective-permute-start | bytes 884744 | tf_op jit(solution)/shard_map/ppermute | solution.py:37
  126.9 20.0 %collective-permute-start.18 = (bf16[2,512,128]{2,1,0:T(8,128)(2,1)S(1)}, bf16[2,512,128]{2,1,0:T(8,128)(2,1)S(1)}, u32[]{:S(2)}, u32[]{:S(2)}) collective-permute-start(bf16[2,512,128]{2,1,0:T(8,128)(2,1)S(1)} %get-tuple-element.12.refs_2_), channel_id=1, source_target_pairs={{0,32},{1,33},{2,34},{3,35},{4,36},{5,37},{6,38},{7,39},{8,40},{9,... | collective-permute-start | bytes 786440 | tf_op jit(solution)/shard_map/ppermute | solution.py:37
  130.9 24.8 %collective-permute-start.19 = (bf16[2,512,128]{2,1,0:T(8,128)(2,1)S(1)}, bf16[2,512,128]{2,1,0:T(8,128)(2,1)S(1)}, u32[]{:S(2)}, u32[]{:S(2)}) collective-permute-start(bf16[2,512,128]{2,1,0:T(8,128)(2,1)S(1)} %get-tuple-element.12.refs_2_), channel_id=1, source_target_pairs={{0,16},{1,17},{2,18},{3,19},{4,20},{5,21},{6,22},{7,23},{8,24},{9,... | collective-permute-start | bytes 786440 | tf_op jit(solution)/shard_map/ppermute | solution.py:37
  132.9 22.9 %collective-permute-start.20 = (bf16[2,512,128]{2,1,0:T(8,128)(2,1)S(1)}, bf16[2,512,128]{2,1,0:T(8,128)(2,1)S(1)}, u32[]{:S(2)}, u32[]{:S(2)}) collective-permute-start(bf16[2,512,128]{2,1,0:T(8,128)(2,1)S(1)} %get-tuple-element.12.refs_2_), channel_id=1, source_target_pairs={{0,240},{1,241},{2,242},{3,243},{4,244},{5,245},{6,246},{7,247},{8... | collective-permute-start | bytes 786440 | tf_op jit(solution)/shard_map/ppermute | solution.py:37
  137.4 26.0 %collective-permute-start.21 = (bf16[2,512,128]{2,1,0:T(8,128)(2,1)S(1)}, bf16[2,512,128]{2,1,0:T(8,128)(2,1)S(1)}, u32[]{:S(2)}, u32[]{:S(2)}) collective-permute-start(bf16[2,512,128]{2,1,0:T(8,128)(2,1)S(1)} %get-tuple-element.12.refs_2_), channel_id=1, source_target_pairs={{0,224},{1,225},{2,226},{3,227},{4,228},{5,229},{6,230},{7,231},{8... | collective-permute-start | bytes 786440 | tf_op jit(solution)/shard_map/ppermute | solution.py:37
  (12 other events, 326.1 us)
Sparse Core Ops, SparseCore 0:
  9.5 76.7 all-gather.4
  101.5 75.7 all-gather.6
